TPU v7x, 32 devices: a whole 2x2x4 slice. The times are simulated.
32 devices in a mesh: dp: 8 (over y, x, core), tensor: 4 (over z).
Axes of the slice: x: 2, y: 2, z: 4, core: 2. Of those that a mesh axis runs over, the one named last changes fastest.
Arguments:
- frames: bfloat16 [16, 1024, 1024], P('dp', 'tensor'), may hold values from -6 to 6
- cotangent: bfloat16 [16, 1024, 1024], P('dp', 'tensor'), may hold values from -6 to 6
- clip_valid: int32 [16], P('dp'), may hold values 0 or 1
- frame_counts: int32 [16], P('dp'), may hold values from 256 to 1024, as said below
- rel_rows: int32 [73], replicated, may hold values from 0 to 72, each once
- first_up: bfloat16 [1024, 4096], P('dp', 'tensor'), may hold values from -0.1875 to 0.1875
- first_down: bfloat16 [4096, 1024], P('tensor', 'dp'), may hold values from -0.1875 to 0.1875
- attend_in: bfloat16 [3, 1024, 1024], P(None, 'dp', 'tensor'), may hold values from -0.1875 to 0.1875
- attend_out: bfloat16 [1024, 1024], P('tensor', 'dp'), may hold values from -1.5 to 1.5
- pointwise_in: bfloat16 [2, 1024, 1024], P(None, 'dp', 'tensor'), may hold values from -0.1875 to 0.1875
- pointwise_out: bfloat16 [1024, 1024], P('tensor', 'dp'), may hold values from -0.25 to 0.25
- second_up: bfloat16 [1024, 4096], P('dp', 'tensor'), may hold values from -0.1875 to 0.1875
- second_down: bfloat16 [4096, 1024], P('tensor', 'dp'), may hold values from -0.1875 to 0.1875
- vectors: bfloat16 [56, 1024], P(None, 'dp')
- distance: bfloat16 [73, 64], replicated, may hold values from -6 to 6
Outputs:
- frames_out: bfloat16 [16, 1024, 1024], P('dp', 'tensor')
- frames_grad: bfloat16 [16, 1024, 1024], P('dp', 'tensor')
- grad_first_up: float32 [1024, 4096], P('dp', 'tensor')
- grad_first_down: float32 [4096, 1024], P('tensor', 'dp')
- grad_attend_in: float32 [3, 1024, 1024], P(None, 'dp', 'tensor')
- grad_attend_out: float32 [1024, 1024], P('tensor', 'dp')
- grad_pointwise_in: float32 [2, 1024, 1024], P(None, 'dp', 'tensor')
- grad_pointwise_out: float32 [1024, 1024], P('tensor', 'dp')
- grad_second_up: float32 [1024, 4096], P('dp', 'tensor')
- grad_second_down: float32 [4096, 1024], P('tensor', 'dp')
- grad_vectors: float32 [56, 1024], P(None, ('dp', 'tensor'))
- grad_distance: float32 [73, 64], replicated
Inputs may be any that keep to these rules, and one draw needn't show every extreme that they name: `frame_counts`: in each aligned run of 2 slots (those of one index of dp) at least one has all 1024 frames. `rel_rows`: names each row of distance once.
All inputs are finite; a program needn't handle non-finite values. No bound on the sum of `clip_valid` on one device may be relied on, other than what follows from the above.
Results may differ from a plain program's by a relative error of at most 0.035.
Values may be sent and summed in bfloat16 or wider, within the bound.
No kernel may reach another device: no remote copies, remote signals or barrier semaphores. Data moves between devices by JAX's collectives and lax.ppermute only.
A program may use at most 256 MiB of HBM per device.

v0:
```python
import jax
import jax.numpy as jnp
from jax import lax
from jax.sharding import PartitionSpec as P

HEADS = 16
HEAD_DIM = 64
FF = 4096
KERNEL = 31
LEFT = 64
OFFSETS = 73


EPSILON = 1e-05


def apply_swish(values):
    return values * jax.nn.sigmoid(values)


def swish_slope(values):
    logistic = jax.nn.sigmoid(values)
    return logistic + values * logistic * (1.0 - logistic)


def matmul(left_side, right_side):
    return jnp.dot(left_side, right_side, preferred_element_type=jnp.float32)


def norm_rows(values, gain_row, shift_row):
    centred = values - jnp.mean(values, axis=-1, keepdims=True)
    variance = jnp.mean(centred * centred, axis=-1, keepdims=True)
    inverse = lax.rsqrt(variance + EPSILON)
    normal = centred * inverse
    return (normal * gain_row + shift_row, normal, inverse)


def norm_back(grad_out, normal, inverse, gain_row):
    grad_normal = grad_out * gain_row
    grad_in = inverse * (
        grad_normal
        - jnp.mean(grad_normal, axis=-1, keepdims=True)
        - normal * jnp.mean(grad_normal * normal, axis=-1, keepdims=True)
    )
    return (grad_in, jnp.sum(grad_out * normal, axis=0), jnp.sum(grad_out, axis=0))


def spread(row_block):
    return lax.all_gather(row_block, "tensor", axis=0, tiled=True)


def spread_back(row_block):
    return lax.all_gather(row_block, "tensor", axis=0, tiled=True)


def row_term(left_side, right_side, pattern):

    def term(start, count):
        return jnp.einsum(pattern, left_side, right_side, preferred_element_type=jnp.float32)

    return term


def collect_term(term, total_rows):
    return lax.psum_scatter(
        term(0, total_rows).astype(jnp.bfloat16), "tensor", scatter_dimension=0, tiled=True
    ).astype(jnp.float32)


def collect_back_term(term, total_rows):
    return lax.psum_scatter(
        term(0, total_rows).astype(jnp.bfloat16), "tensor", scatter_dimension=0, tiled=True
    ).astype(jnp.float32)


def shift_table(block_start, block_rows, slot_len):
    span = slot_len + block_rows + 1
    positions = jnp.arange(span)[None, :] - block_rows - block_start + LEFT
    clipped = jnp.clip(positions, 0, OFFSETS - 1)
    return (clipped == jnp.arange(OFFSETS)[:, None]).astype(jnp.bfloat16)


def expand(query_table, table_shift, block_rows):
    head_count = query_table.shape[0]
    span = table_shift.shape[1]
    wide_rows = jnp.einsum(
        "hbr,rp->hbp", query_table, table_shift, preferred_element_type=jnp.float32
    )
    skewed = wide_rows.reshape(head_count, block_rows * span)[:, : block_rows * (span - 1)]
    skewed = skewed.reshape(head_count, block_rows, span - 1)
    return skewed[:, :, block_rows:]


def collapse(grad_scores, table_shift, block_rows):
    head_count = grad_scores.shape[0]
    span = table_shift.shape[1]
    padded = jnp.pad(grad_scores, ((0, 0), (0, 0), (block_rows, 0)))
    flat = jnp.pad(padded.reshape(head_count, block_rows * (span - 1)), ((0, 0), (0, block_rows)))
    flat = flat.reshape(head_count, block_rows, span)
    return jnp.einsum("hbp,rp->hbr", flat, table_shift, preferred_element_type=jnp.float32)


def feed_forward(inputs, up_weight, down_weight, up_bias, down_bias, gain_row, shift_row):
    normed, normal, inverse = norm_rows(inputs, gain_row, shift_row)
    spread_rows = spread(normed.astype(jnp.bfloat16))
    upper_rows = matmul(spread_rows, up_weight) + up_bias
    hidden = apply_swish(upper_rows).astype(jnp.bfloat16)
    result = collect_term(row_term(hidden, down_weight, "tf,fd->td"), hidden.shape[0]) + down_bias
    return (result, (normal, inverse, spread_rows, upper_rows, hidden))


def feed_back(grad_result, stored, up_weight, down_weight, gain_row):
    normal, inverse, spread_rows, upper_rows, hidden = stored
    grad_low = grad_result.astype(jnp.bfloat16)
    grad_rows = spread_back(grad_low)
    grad_down = jnp.einsum("tf,td->fd", hidden, grad_rows, preferred_element_type=jnp.float32)
    grad_hidden = jnp.einsum(
        "td,fd->tf", grad_rows, down_weight, preferred_element_type=jnp.float32
    )
    grad_upper = (grad_hidden * swish_slope(upper_rows)).astype(jnp.bfloat16)
    grad_up = jnp.einsum("tc,tf->cf", spread_rows, grad_upper, preferred_element_type=jnp.float32)
    grad_normed = collect_back_term(
        row_term(grad_upper, up_weight, "tf,cf->tc"), grad_upper.shape[0]
    )
    grad_in, grad_gain, grad_shift = norm_back(grad_normed, normal, inverse, gain_row)
    up_bias_grad = jnp.sum(grad_upper.astype(jnp.float32), axis=0)
    down_bias_grad = jnp.sum(grad_low.astype(jnp.float32), axis=0)
    return (grad_in, (grad_up, grad_down), (grad_gain, grad_shift, up_bias_grad, down_bias_grad))


def block_scores(
    head_rows, table_low, table_shift, live_mask, block_start, block_rows, score_scale
):
    query_block = head_rows[0][:, block_start : block_start + block_rows]
    query_table = jnp.einsum(
        "hbd,rd->hbr", query_block, table_low, preferred_element_type=jnp.float32
    ).astype(jnp.bfloat16)
    direct = jnp.einsum(
        "hbd,hjd->hbj", query_block, head_rows[1], preferred_element_type=jnp.float32
    )
    scores = (direct + expand(query_table, table_shift, block_rows)) * score_scale
    return (jnp.where(live_mask[None, None, :] > 0, scores, -1e30), query_block)


def attention(
    inputs,
    mix_weight,
    back_weight,
    query_bias,
    value_bias,
    out_bias,
    gain_row,
    shift_row,
    table_low,
    live_mask,
    tables,
    block_rows,
    heads_here,
    score_scale,
):
    normed, normal, inverse = norm_rows(inputs, gain_row, shift_row)
    spread_rows = spread(normed.astype(jnp.bfloat16))
    slot_len = spread_rows.shape[0]
    projected = jnp.einsum(
        "tc,kcf->ktf", spread_rows, mix_weight, preferred_element_type=jnp.float32
    )
    biases = jnp.stack([query_bias, jnp.zeros_like(query_bias), value_bias])
    projected = (projected + biases[:, None, :]).astype(jnp.bfloat16)
    head_rows = projected.reshape(3, slot_len, heads_here, HEAD_DIM).transpose(0, 2, 1, 3)
    contexts = []
    log_totals = []
    for number, block_start in enumerate(range(0, slot_len, block_rows)):
        masked, query_block = block_scores(
            head_rows, table_low, tables[number], live_mask, block_start, block_rows, score_scale
        )
        row_peak = jnp.max(masked, axis=-1, keepdims=True)
        exp_rows = jnp.exp(masked - row_peak)
        row_total = jnp.sum(exp_rows, axis=-1, keepdims=True)
        shares = exp_rows / row_total
        log_totals.append(row_peak + jnp.log(row_total))
        contexts.append(
            jnp.einsum(
                "hbj,hjd->hbd",
                shares.astype(jnp.bfloat16),
                head_rows[2],
                preferred_element_type=jnp.float32,
            )
        )
    context = (
        jnp.concatenate(contexts, axis=1)
        .transpose(1, 0, 2)
        .reshape(slot_len, heads_here * HEAD_DIM)
        .astype(jnp.bfloat16)
    )
    result = collect_term(row_term(context, back_weight, "tf,fd->td"), slot_len) + out_bias
    return (
        result,
        (normal, inverse, spread_rows, head_rows, jnp.concatenate(log_totals, axis=1), context),
    )


def attention_back(
    grad_result,
    stored,
    mix_weight,
    back_weight,
    gain_row,
    table_low,
    live_mask,
    tables,
    block_rows,
    heads_here,
    score_scale,
):
    normal, inverse, spread_rows, head_rows, log_totals, context = stored
    slot_len = spread_rows.shape[0]
    grad_low = grad_result.astype(jnp.bfloat16)
    grad_rows = spread_back(grad_low)
    grad_back = jnp.einsum("tf,td->fd", context, grad_rows, preferred_element_type=jnp.float32)
    grad_context = jnp.einsum(
        "td,fd->tf", grad_rows, back_weight, preferred_element_type=jnp.float32
    ).astype(jnp.bfloat16)
    grad_heads = grad_context.reshape(slot_len, heads_here, HEAD_DIM).transpose(1, 0, 2)
    grad_keys = jnp.zeros(head_rows.shape[1:], jnp.float32)
    grad_values = jnp.zeros(head_rows.shape[1:], jnp.float32)
    grad_table = jnp.zeros(table_low.shape, jnp.float32)
    query_parts = []
    for number, block_start in enumerate(range(0, slot_len, block_rows)):
        masked, query_block = block_scores(
            head_rows, table_low, tables[number], live_mask, block_start, block_rows, score_scale
        )
        shares = jnp.exp(masked - log_totals[:, block_start : block_start + block_rows])
        grad_block = grad_heads[:, block_start : block_start + block_rows]
        grad_shares = jnp.einsum(
            "hbd,hjd->hbj", grad_block, head_rows[2], preferred_element_type=jnp.float32
        )
        inner = jnp.sum(shares * grad_shares, axis=-1, keepdims=True)
        grad_scores = (shares * (grad_shares - inner)).astype(jnp.bfloat16)
        grad_values = grad_values + jnp.einsum(
            "hbj,hbd->hjd",
            shares.astype(jnp.bfloat16),
            grad_block,
            preferred_element_type=jnp.float32,
        )
        grad_keys = (
            grad_keys
            + jnp.einsum(
                "hbj,hbd->hjd", grad_scores, query_block, preferred_element_type=jnp.float32
            )
            * score_scale
        )
        grad_query_table = (collapse(grad_scores, tables[number], block_rows) * score_scale).astype(
            jnp.bfloat16
        )
        query_direct = (
            jnp.einsum(
                "hbj,hjd->hbd", grad_scores, head_rows[1], preferred_element_type=jnp.float32
            )
            * score_scale
        )
        query_parts.append(
            query_direct
            + jnp.einsum(
                "hbr,rd->hbd", grad_query_table, table_low, preferred_element_type=jnp.float32
            )
        )
        grad_table = grad_table + jnp.einsum(
            "hbr,hbd->rd", grad_query_table, query_block, preferred_element_type=jnp.float32
        )
    grad_queries = jnp.concatenate(query_parts, axis=1)
    grad_stack = jnp.stack([grad_queries, grad_keys, grad_values]).astype(jnp.bfloat16)
    grad_stack = grad_stack.transpose(0, 2, 1, 3).reshape(3, slot_len, heads_here * HEAD_DIM)
    grad_mix = jnp.einsum(
        "tc,ktf->kcf", spread_rows, grad_stack, preferred_element_type=jnp.float32
    )
    grad_normed = collect_back_term(row_term(grad_stack, mix_weight, "ktf,kcf->tc"), slot_len)
    grad_in, grad_gain, grad_shift = norm_back(grad_normed, normal, inverse, gain_row)
    bias_sums = jnp.sum(grad_stack.astype(jnp.float32), axis=1)
    out_bias_grad = jnp.sum(grad_low.astype(jnp.float32), axis=0)
    return (
        grad_in,
        (grad_mix, grad_back, grad_table),
        (grad_gain, grad_shift, bias_sums[0], bias_sums[2], out_bias_grad),
    )


def convolve(
    inputs,
    mix_weight,
    back_weight,
    gain_row,
    shift_row,
    deep_gain,
    deep_shift,
    taps_here,
    live_mask,
    model_width,
):
    normed, normal, inverse = norm_rows(inputs, gain_row, shift_row)
    spread_rows = spread(normed.astype(jnp.bfloat16))
    slot_len = spread_rows.shape[0]
    pair_rows = jnp.einsum(
        "tc,kcf->ktf", spread_rows, mix_weight, preferred_element_type=jnp.float32
    )
    logistic = jax.nn.sigmoid(pair_rows[1])
    gated_rows = pair_rows[0] * logistic * live_mask[:, None]
    padded = jnp.pad(gated_rows, ((KERNEL - 1, 0), (0, 0)))
    depth_out = jnp.zeros_like(gated_rows)
    for offset in range(KERNEL):
        depth_out = depth_out + taps_here[offset] * padded[offset : offset + slot_len]
    moments = lax.psum(
        (jnp.sum(depth_out, axis=1), jnp.sum(depth_out * depth_out, axis=1)), "tensor"
    )
    mean_row = moments[0][:, None] / model_width
    inverse_deep = lax.rsqrt(moments[1][:, None] / model_width - mean_row * mean_row + EPSILON)
    normal_deep = (depth_out - mean_row) * inverse_deep
    deep_norm = normal_deep * deep_gain + deep_shift
    activated = apply_swish(deep_norm).astype(jnp.bfloat16)
    result = collect_term(row_term(activated, back_weight, "tf,fd->td"), slot_len)
    return (
        result,
        (
            normal,
            inverse,
            spread_rows,
            pair_rows,
            logistic,
            padded,
            normal_deep,
            inverse_deep,
            deep_norm,
            activated,
        ),
    )


def convolve_back(
    grad_result,
    stored,
    mix_weight,
    back_weight,
    gain_row,
    deep_gain,
    taps_here,
    live_mask,
    model_width,
):
    (
        normal,
        inverse,
        spread_rows,
        pair_rows,
        logistic,
        padded,
        normal_deep,
        inverse_deep,
        deep_norm,
        activated,
    ) = stored
    slot_len = spread_rows.shape[0]
    grad_low = grad_result.astype(jnp.bfloat16)
    grad_rows = spread_back(grad_low)
    grad_back = jnp.einsum("tf,td->fd", activated, grad_rows, preferred_element_type=jnp.float32)
    grad_activated = jnp.einsum(
        "td,fd->tf", grad_rows, back_weight, preferred_element_type=jnp.float32
    )
    grad_deep = grad_activated * swish_slope(deep_norm)
    deep_gain_grad = jnp.sum(grad_deep * normal_deep, axis=0)
    deep_shift_grad = jnp.sum(grad_deep, axis=0)
    grad_normal = grad_deep * deep_gain
    moments = lax.psum(
        (jnp.sum(grad_normal, axis=1), jnp.sum(grad_normal * normal_deep, axis=1)), "tensor"
    )
    grad_depth = inverse_deep * (
        grad_normal
        - moments[0][:, None] / model_width
        - normal_deep * moments[1][:, None] / model_width
    )
    extended = jnp.pad(grad_depth, ((0, KERNEL - 1), (0, 0)))
    grad_gated = jnp.zeros_like(grad_depth)
    tap_grads = []
    for offset in range(KERNEL):
        tap_grads.append(jnp.sum(padded[offset : offset + slot_len] * grad_depth, axis=0))
        grad_gated = (
            grad_gated
            + taps_here[offset] * extended[KERNEL - 1 - offset : KERNEL - 1 - offset + slot_len]
        )
    grad_gated = grad_gated * live_mask[:, None]
    grad_pair = jnp.stack(
        [grad_gated * logistic, grad_gated * pair_rows[0] * logistic * (1.0 - logistic)]
    ).astype(jnp.bfloat16)
    grad_mix = jnp.einsum("tc,ktf->kcf", spread_rows, grad_pair, preferred_element_type=jnp.float32)
    grad_normed = collect_back_term(row_term(grad_pair, mix_weight, "ktf,kcf->tc"), slot_len)
    grad_in, grad_gain, grad_shift = norm_back(grad_normed, normal, inverse, gain_row)
    return (
        grad_in,
        (grad_mix, grad_back),
        (grad_gain, grad_shift, deep_gain_grad, deep_shift_grad, jnp.stack(tap_grads)),
    )


def widen_piece(piece, total_len, start_at):
    return lax.dynamic_update_slice(jnp.zeros((total_len,), jnp.float32), piece, (start_at,))


def assemble_rows(
    one_parts,
    attend_parts,
    conv_parts,
    two_parts,
    final_parts,
    model_width,
    col_start,
    hidden_start,
):
    ratio_rows = FF // model_width

    def hidden_rows(piece):
        return widen_piece(piece, FF, hidden_start).reshape(ratio_rows, model_width)

    def column_row(piece):
        return widen_piece(piece, model_width, col_start)

    zero_index = jnp.zeros((), jnp.int32)
    tap_rows = lax.dynamic_update_slice(
        jnp.zeros((KERNEL, model_width), jnp.float32), conv_parts[4], (zero_index, col_start)
    )
    return jnp.concatenate(
        [
            jnp.stack([one_parts[0], one_parts[1]]),
            hidden_rows(one_parts[2]),
            one_parts[3][None],
            jnp.stack(
                [
                    attend_parts[0],
                    attend_parts[1],
                    column_row(attend_parts[2]),
                    column_row(attend_parts[3]),
                    attend_parts[4],
                ]
            ),
            jnp.stack(
                [conv_parts[0], conv_parts[1], column_row(conv_parts[2]), column_row(conv_parts[3])]
            ),
            jnp.stack([two_parts[0], two_parts[1]]),
            hidden_rows(two_parts[2]),
            two_parts[3][None],
            jnp.stack([final_parts[0], final_parts[1]]),
            tap_rows,
        ],
        axis=0,
    )


def reduce_weights(grads):
    return (
        lax.psum_scatter(
            grads[0].astype(jnp.bfloat16), "dp", scatter_dimension=0, tiled=True
        ).astype(jnp.float32),
        lax.psum_scatter(
            grads[1].astype(jnp.bfloat16), "dp", scatter_dimension=1, tiled=True
        ).astype(jnp.float32),
        lax.psum_scatter(
            grads[2].astype(jnp.bfloat16), "dp", scatter_dimension=1, tiled=True
        ).astype(jnp.float32),
        lax.psum_scatter(
            grads[3].astype(jnp.bfloat16), "dp", scatter_dimension=1, tiled=True
        ).astype(jnp.float32),
        lax.psum_scatter(
            grads[4].astype(jnp.bfloat16), "dp", scatter_dimension=1, tiled=True
        ).astype(jnp.float32),
        lax.psum_scatter(
            grads[5].astype(jnp.bfloat16), "dp", scatter_dimension=1, tiled=True
        ).astype(jnp.float32),
        lax.psum_scatter(
            grads[6].astype(jnp.bfloat16), "dp", scatter_dimension=0, tiled=True
        ).astype(jnp.float32),
        lax.psum_scatter(
            grads[7].astype(jnp.bfloat16), "dp", scatter_dimension=1, tiled=True
        ).astype(jnp.float32),
    )


def body(
    frames,
    cotangent,
    clip_valid,
    frame_counts,
    rel_rows,
    first_up,
    first_down,
    attend_in,
    attend_out,
    pointwise_in,
    pointwise_out,
    second_up,
    second_down,
    vectors,
    distance,
):
    micro_count = frames.shape[0]
    local_rows = frames.shape[1]
    model_width = frames.shape[2]
    tensor_count = lax.axis_size("tensor")
    tensor_pos = lax.axis_index("tensor")
    slot_len = local_rows * tensor_count
    cols_here = model_width // tensor_count
    hidden_here = FF // tensor_count
    heads_here = HEADS // tensor_count
    ratio_rows = FF // model_width
    attend_base = 3 + ratio_rows
    conv_base = attend_base + 5
    second_base = conv_base + 4
    final_base = second_base + 3 + ratio_rows
    taps_base = final_base + 2
    block_rows = min(512, slot_len)
    score_scale = HEAD_DIM ** (-0.5)
    col_start = tensor_pos * cols_here
    hidden_start = tensor_pos * hidden_here
    tables = [
        shift_table(block_start, block_rows, slot_len)
        for block_start in range(0, slot_len, block_rows)
    ]
    pick_rows = (rel_rows[:, None] == jnp.arange(OFFSETS)[None, :]).astype(jnp.bfloat16)
    table_low = matmul(pick_rows, distance).astype(jnp.bfloat16)

    def fetch_weights():
        return (
            lax.all_gather(first_up, "dp", axis=0, tiled=True),
            lax.all_gather(first_down, "dp", axis=1, tiled=True),
            lax.all_gather(attend_in, "dp", axis=1, tiled=True),
            lax.all_gather(attend_out, "dp", axis=1, tiled=True),
            lax.all_gather(pointwise_in, "dp", axis=1, tiled=True),
            lax.all_gather(pointwise_out, "dp", axis=1, tiled=True),
            lax.all_gather(second_up, "dp", axis=0, tiled=True),
            lax.all_gather(second_down, "dp", axis=1, tiled=True),
            lax.all_gather(vectors, "dp", axis=1, tiled=True),
        )

    local_shapes = (
        (model_width, hidden_here),
        (hidden_here, model_width),
        (3, model_width, cols_here),
        (cols_here, model_width),
        (2, model_width, cols_here),
        (cols_here, model_width),
        (model_width, hidden_here),
        (hidden_here, model_width),
    )
    start_grads = tuple((jnp.zeros(shape_one, jnp.float32) for shape_one in local_shapes))

    def micro_step(micro_index, carry):
        weight_acc, vector_acc, table_acc, out_acc, grad_acc = carry
        forward_set = fetch_weights()
        rows_in = lax.dynamic_index_in_dim(frames, micro_index, 0, keepdims=False).astype(
            jnp.float32
        )
        rows_cot = lax.dynamic_index_in_dim(cotangent, micro_index, 0, keepdims=False).astype(
            jnp.float32
        )
        valid_flag = (
            lax.dynamic_index_in_dim(clip_valid, micro_index, 0, keepdims=False) > 0
        ).astype(jnp.float32)
        frame_total = lax.dynamic_index_in_dim(frame_counts, micro_index, 0, keepdims=False)
        live_mask = (jnp.arange(slot_len) < frame_total).astype(jnp.float32)
        (
            up_one,
            down_one,
            attend_mix,
            attend_back,
            point_mix,
            point_back,
            up_two,
            down_two,
            vector_all,
        ) = forward_set
        vector_wide = vector_all.astype(jnp.float32)

        def column_piece(row_number):
            return lax.dynamic_slice_in_dim(vector_wide[row_number], col_start, cols_here)

        def hidden_piece(base_row):
            return lax.dynamic_slice_in_dim(
                vector_wide[base_row + 2 : base_row + 2 + ratio_rows].reshape(FF),
                hidden_start,
                hidden_here,
            )

        taps_here = lax.dynamic_slice_in_dim(
            vector_wide[taps_base : taps_base + KERNEL], col_start, cols_here, axis=1
        )
        deep_gain = column_piece(conv_base + 2)
        one_out, one_kept = feed_forward(
            rows_in,
            up_one,
            down_one,
            hidden_piece(0),
            vector_wide[2 + ratio_rows],
            vector_wide[0],
            vector_wide[1],
        )
        after_one = rows_in + 0.5 * one_out
        attend_result, attend_kept = attention(
            after_one,
            attend_mix,
            attend_back,
            column_piece(attend_base + 2),
            column_piece(attend_base + 3),
            vector_wide[attend_base + 4],
            vector_wide[attend_base],
            vector_wide[attend_base + 1],
            table_low,
            live_mask,
            tables,
            block_rows,
            heads_here,
            score_scale,
        )
        after_two = after_one + attend_result
        conv_result, conv_kept = convolve(
            after_two,
            point_mix,
            point_back,
            vector_wide[conv_base],
            vector_wide[conv_base + 1],
            deep_gain,
            column_piece(conv_base + 3),
            taps_here,
            live_mask,
            model_width,
        )
        after_three = after_two + conv_result
        two_out, two_kept = feed_forward(
            after_three,
            up_two,
            down_two,
            hidden_piece(second_base),
            vector_wide[second_base + 2 + ratio_rows],
            vector_wide[second_base],
            vector_wide[second_base + 1],
        )
        after_four = after_three + 0.5 * two_out
        final_rows, final_normal, final_inverse = norm_rows(
            after_four, vector_wide[final_base], vector_wide[final_base + 1]
        )
        row_out = jnp.where(valid_flag > 0, final_rows, rows_in)
        backward_set = fetch_weights()
        (
            up_one_b,
            down_one_b,
            attend_mix_b,
            attend_back_b,
            point_mix_b,
            point_back_b,
            up_two_b,
            down_two_b,
            vector_back,
        ) = backward_set
        gains_back = vector_back.astype(jnp.float32)
        grad_final = rows_cot * valid_flag
        grad_four, final_gain_grad, final_shift_grad = norm_back(
            grad_final, final_normal, final_inverse, gains_back[final_base]
        )
        grad_two_in, two_weights, two_parts = feed_back(
            0.5 * grad_four, two_kept, up_two_b, down_two_b, gains_back[second_base]
        )
        grad_three = grad_four + grad_two_in
        grad_conv_in, conv_weights, conv_parts = convolve_back(
            grad_three,
            conv_kept,
            point_mix_b,
            point_back_b,
            gains_back[conv_base],
            deep_gain,
            taps_here,
            live_mask,
            model_width,
        )
        grad_two = grad_three + grad_conv_in
        grad_attend_in, attend_weights, attend_parts = attention_back(
            grad_two,
            attend_kept,
            attend_mix_b,
            attend_back_b,
            gains_back[attend_base],
            table_low,
            live_mask,
            tables,
            block_rows,
            heads_here,
            score_scale,
        )
        grad_one = grad_two + grad_attend_in
        grad_one_in, one_weights, one_parts = feed_back(
            0.5 * grad_one, one_kept, up_one_b, down_one_b, gains_back[0]
        )
        grad_rows = grad_one + grad_one_in + (1.0 - valid_flag) * rows_cot
        micro_grads = (
            one_weights[0],
            one_weights[1],
            attend_weights[0],
            attend_weights[1],
            conv_weights[0],
            conv_weights[1],
            two_weights[0],
            two_weights[1],
        )
        weight_acc = jax.tree.map(jnp.add, weight_acc, micro_grads)
        vector_acc = vector_acc + assemble_rows(
            one_parts,
            attend_parts,
            conv_parts,
            two_parts,
            (final_gain_grad, final_shift_grad),
            model_width,
            col_start,
            hidden_start,
        )
        table_acc = table_acc + attend_weights[2]
        out_acc = lax.dynamic_update_index_in_dim(
            out_acc, row_out.astype(jnp.bfloat16), micro_index, 0
        )
        grad_acc = lax.dynamic_update_index_in_dim(
            grad_acc, grad_rows.astype(jnp.bfloat16), micro_index, 0
        )
        return (weight_acc, vector_acc, table_acc, out_acc, grad_acc)

    initial_carry = (
        start_grads,
        jnp.zeros((vectors.shape[0], model_width), jnp.float32),
        jnp.zeros((OFFSETS, HEAD_DIM), jnp.float32),
        jnp.zeros_like(frames),
        jnp.zeros_like(frames),
    )
    weight_acc, vector_acc, table_acc, frames_out, frames_grad = lax.fori_loop(
        0, micro_count, micro_step, initial_carry
    )
    weight_final = reduce_weights(weight_acc)
    grad_vectors = lax.psum_scatter(vector_acc, ("dp", "tensor"), scatter_dimension=1, tiled=True)
    local_distance = jnp.dot(
        pick_rows.astype(jnp.float32).T, table_acc, precision=lax.Precision.HIGHEST
    )
    grad_distance = lax.psum(local_distance, ("dp", "tensor"))
    return (
        frames_out,
        frames_grad,
        weight_final[0],
        weight_final[1],
        weight_final[2],
        weight_final[3],
        weight_final[4],
        weight_final[5],
        weight_final[6],
        weight_final[7],
        grad_vectors,
        grad_distance,
    )


def solution(mesh):
    return jax.shard_map(
        body,
        mesh=mesh,
        in_specs=(
            P("dp", "tensor", None),
            P("dp", "tensor", None),
            P("dp"),
            P("dp"),
            P(),
            P("dp", "tensor"),
            P("tensor", "dp"),
            P(None, "dp", "tensor"),
            P("tensor", "dp"),
            P(None, "dp", "tensor"),
            P("tensor", "dp"),
            P("dp", "tensor"),
            P("tensor", "dp"),
            P(None, "dp"),
            P(),
        ),
        out_specs=(
            P("dp", "tensor", None),
            P("dp", "tensor", None),
            P("dp", "tensor"),
            P("tensor", "dp"),
            P(None, "dp", "tensor"),
            P("tensor", "dp"),
            P(None, "dp", "tensor"),
            P("tensor", "dp"),
            P("dp", "tensor"),
            P("tensor", "dp"),
            P(None, ("dp", "tensor")),
            P(),
        ),
        check_vma=False,
    )
```

profile of v0, /device:TPU:0, one launch (start us, length us, event | category | flops | bytes accessed | tf_op | source)
XLA Modules:
  0.0 3131.5 jit_solution(5749010367228401538)
XLA Ops:
  11.9 2640.5 %while.39 = (s32[]{:T(128)}, f32[1024,1024]{1,0:T(8,128)}, f32[1024,1024]{1,0:T(8,128)}, f32[3,1024,256]{1,2,0:T(8,128)}, f32[256,1024]{1,0:T(8,128)}, /*index=5...) while((s32[]{:T(128)}, f32[1024,1024]{1,0:T(8,128)}, ...), condition=%wide.region_92.93_spmd.clone.clone, body=%wide.region_0.92_spmd.clone.clone.sunk | while | flops 42498797568 | bytes 1487596928 | solution.py:735
  29.6 44.8 %all-gather.15.cloned.1.call-done = bf16[1024,1024]{1,0:T(8,128)(2,1)} async-done(((bf16[256,1024]{1,0:T(8,128)(2,1)}), bf16[1024,1024]{1,0:T(8,128)(2,1)}) %all-gather.15.cloned.1.call-update) | async-done | bytes 2097168 | tf_op jit(solution)/shard_map/while/body/eval_jaxpr/all_gather | solution.py:49
  140.5 43.4 %reduce-scatter.44.cloned.1.call-done = bf16[256,1024]{1,0:T(8,128)(2,1)} async-done(((bf16[1024,1024]{1,0:T(8,128)(2,1)}), bf16[256,1024]{1,0:T(8,128)(2,1)}) %reduce-scatter.44.cloned.1.call-update) | async-done | bytes 524304 | tf_op jit(solution)/shard_map/while/body/eval_jaxpr/reduce_scatter | solution.py:65
  212.0 48.0 %all-gather.23.cloned.1.call-done = bf16[1024,1024]{1,0:T(8,128)(2,1)} async-done(((bf16[256,1024]{1,0:T(8,128)(2,1)}), bf16[1024,1024]{1,0:T(8,128)(2,1)}) %all-gather.23.cloned.1.call-update) | async-done | bytes 2097168 | tf_op jit(solution)/shard_map/while/body/eval_jaxpr/all_gather | solution.py:49
  489.6 48.2 %all-gather.27.cloned.1.call-done = bf16[1024,1024]{1,0:T(8,128)(2,1)} async-done(((bf16[256,1024]{1,0:T(8,128)(2,1)}), bf16[1024,1024]{1,0:T(8,128)(2,1)}) %all-gather.27.cloned.1.call-update) | async-done | bytes 2097168 | tf_op jit(solution)/shard_map/while/body/eval_jaxpr/all_gather | solution.py:49
  630.8 48.0 %all-gather.29.cloned.1.call-done = bf16[1024,1024]{1,0:T(8,128)(2,1)} async-done(((bf16[256,1024]{1,0:T(8,128)(2,1)}), bf16[1024,1024]{1,0:T(8,128)(2,1)}) %all-gather.29.cloned.1.call-update) | async-done | bytes 2097168 | tf_op jit(solution)/shard_map/while/body/eval_jaxpr/all_gather | solution.py:49
  715.5 42.7 %reduce-scatter.50.cloned.1.call-done = bf16[256,1024]{1,0:T(8,128)(2,1)} async-done(((bf16[1024,1024]{1,0:T(8,128)(2,1)}), bf16[256,1024]{1,0:T(8,128)(2,1)}) %reduce-scatter.50.cloned.1.call-update) | async-done | bytes 524304 | tf_op jit(solution)/shard_map/while/body/eval_jaxpr/reduce_scatter | solution.py:65
  765.2 45.1 %all-gather.35.cloned.1.call-done = bf16[1024,1024]{1,0:T(8,128)(2,1)} async-done(((bf16[256,1024]{1,0:T(8,128)(2,1)}), bf16[1024,1024]{1,0:T(8,128)(2,1)}) %all-gather.35.cloned.1.call-update) | async-done | bytes 2097168 | tf_op jit(solution)/shard_map/while/body/eval_jaxpr/all_gather | solution.py:53
  822.3 42.7 %reduce-scatter.52.cloned.1.call-done = bf16[256,1024]{1,0:T(8,128)(2,1)} async-done(((bf16[1024,1024]{1,0:T(8,128)(2,1)}), bf16[256,1024]{1,0:T(8,128)(2,1)}) %reduce-scatter.52.cloned.1.call-update) | async-done | bytes 524304 | tf_op jit(solution)/shard_map/while/body/eval_jaxpr/reduce_scatter | solution.py:71
  870.4 45.3 %all-gather.37.cloned.1.call-done = bf16[1024,1024]{1,0:T(8,128)(2,1)} async-done(((bf16[256,1024]{1,0:T(8,128)(2,1)}), bf16[1024,1024]{1,0:T(8,128)(2,1)}) %all-gather.37.cloned.1.call-update) | async-done | bytes 2097168 | tf_op jit(solution)/shard_map/while/body/eval_jaxpr/all_gather | solution.py:53
  991.8 45.3 %all-gather.39.cloned.1.call-done = bf16[1024,1024]{1,0:T(8,128)(2,1)} async-done(((bf16[256,1024]{1,0:T(8,128)(2,1)}), bf16[1024,1024]{1,0:T(8,128)(2,1)}) %all-gather.39.cloned.1.call-update) | async-done | bytes 2097168 | tf_op jit(solution)/shard_map/while/body/eval_jaxpr/all_gather | solution.py:53
  1347.4 43.0 %all-gather.15.cloned.1.call-done = bf16[1024,1024]{1,0:T(8,128)(2,1)} async-done(((bf16[256,1024]{1,0:T(8,128)(2,1)}), bf16[1024,1024]{1,0:T(8,128)(2,1)}) %all-gather.15.cloned.1.call-update) | async-done | bytes 2097168 | tf_op jit(solution)/shard_map/while/body/eval_jaxpr/all_gather | solution.py:49
  1456.4 43.4 %reduce-scatter.44.cloned.1.call-done = bf16[256,1024]{1,0:T(8,128)(2,1)} async-done(((bf16[1024,1024]{1,0:T(8,128)(2,1)}), bf16[256,1024]{1,0:T(8,128)(2,1)}) %reduce-scatter.44.cloned.1.call-update) | async-done | bytes 524304 | tf_op jit(solution)/shard_map/while/body/eval_jaxpr/reduce_scatter | solution.py:65
  1528.0 48.1 %all-gather.23.cloned.1.call-done = bf16[1024,1024]{1,0:T(8,128)(2,1)} async-done(((bf16[256,1024]{1,0:T(8,128)(2,1)}), bf16[1024,1024]{1,0:T(8,128)(2,1)}) %all-gather.23.cloned.1.call-update) | async-done | bytes 2097168 | tf_op jit(solution)/shard_map/while/body/eval_jaxpr/all_gather | solution.py:49
  1805.6 48.2 %all-gather.27.cloned.1.call-done = bf16[1024,1024]{1,0:T(8,128)(2,1)} async-done(((bf16[256,1024]{1,0:T(8,128)(2,1)}), bf16[1024,1024]{1,0:T(8,128)(2,1)}) %all-gather.27.cloned.1.call-update) | async-done | bytes 2097168 | tf_op jit(solution)/shard_map/while/body/eval_jaxpr/all_gather | solution.py:49
  1946.6 48.1 %all-gather.29.cloned.1.call-done = bf16[1024,1024]{1,0:T(8,128)(2,1)} async-done(((bf16[256,1024]{1,0:T(8,128)(2,1)}), bf16[1024,1024]{1,0:T(8,128)(2,1)}) %all-gather.29.cloned.1.call-update) | async-done | bytes 2097168 | tf_op jit(solution)/shard_map/while/body/eval_jaxpr/all_gather | solution.py:49
  2031.5 42.7 %reduce-scatter.50.cloned.1.call-done = bf16[256,1024]{1,0:T(8,128)(2,1)} async-done(((bf16[1024,1024]{1,0:T(8,128)(2,1)}), bf16[256,1024]{1,0:T(8,128)(2,1)}) %reduce-scatter.50.cloned.1.call-update) | async-done | bytes 524304 | tf_op jit(solution)/shard_map/while/body/eval_jaxpr/reduce_scatter | solution.py:65
  2081.2 45.2 %all-gather.35.cloned.1.call-done = bf16[1024,1024]{1,0:T(8,128)(2,1)} async-done(((bf16[256,1024]{1,0:T(8,128)(2,1)}), bf16[1024,1024]{1,0:T(8,128)(2,1)}) %all-gather.35.cloned.1.call-update) | async-done | bytes 2097168 | tf_op jit(solution)/shard_map/while/body/eval_jaxpr/all_gather | solution.py:53
  2186.4 45.3 %all-gather.37.cloned.1.call-done = bf16[1024,1024]{1,0:T(8,128)(2,1)} async-done(((bf16[256,1024]{1,0:T(8,128)(2,1)}), bf16[1024,1024]{1,0:T(8,128)(2,1)}) %all-gather.37.cloned.1.call-update) | async-done | bytes 2097168 | tf_op jit(solution)/shard_map/while/body/eval_jaxpr/all_gather | solution.py:53
  2307.8 45.3 %all-gather.39.cloned.1.call-done = bf16[1024,1024]{1,0:T(8,128)(2,1)} async-done(((bf16[256,1024]{1,0:T(8,128)(2,1)}), bf16[1024,1024]{1,0:T(8,128)(2,1)}) %all-gather.39.cloned.1.call-update) | async-done | bytes 2097168 | tf_op jit(solution)/shard_map/while/body/eval_jaxpr/all_gather | solution.py:53
  2810.8 42.7 %reduce-scatter.36.cloned.1.call-done = bf16[128,1024]{1,0:T(8,128)(2,1)} async-done(((bf16[1024,1024]{1,0:T(8,128)(2,1)}), bf16[128,1024]{1,0:T(8,128)(2,1)}) %reduce-scatter.36.cloned.1.call-update) | async-done | bytes 262160
  2855.4 42.8 %reduce-scatter.42.cloned.1.call-done = bf16[128,1024]{1,0:T(8,128)(2,1)} async-done(((bf16[1024,1024]{1,0:T(8,128)(2,1)}), bf16[128,1024]{1,0:T(8,128)(2,1)}) %reduce-scatter.42.cloned.1.call-update) | async-done | bytes 262160
  2944.3 42.8 %reduce-scatter.32.cloned.1.call-done = bf16[128,1024]{1,0:T(8,128)(2,1)} async-done(((bf16[1024,1024]{1,0:T(8,128)(2,1)}), bf16[128,1024]{1,0:T(8,128)(2,1)}) %reduce-scatter.32.cloned.1.call-update) | async-done | bytes 262160 | tf_op jit(solution)/shard_map/reduce_scatter | solution.py:475
  2988.9 134.9 %reduce-scatter.34.cloned.1.call-done = f32[56,32]{0,1:T(8,128)} async-done(((f32[56,1024]{0,1:T(8,128)}), f32[56,32]{0,1:T(8,128)}) %reduce-scatter.34.cloned.1.call-update) | async-done | bytes 7184 | tf_op jit(solution)/shard_map/reduce_scatter | solution.py:739
  (1032 shorter events, 1979.1 us)
Async XLA Ops:
  29.4 154.4 %reduce-scatter.44.cloned.1.call-start = ((), (), s32[]{:S(2)}) async-start(), calls=%async_computation.30 | async-start | bytes 2621440 | tf_op jit(solution)/shard_map/while/body/eval_jaxpr/reduce_scatter | solution.py:65
  140.4 119.6 %all-gather.23.cloned.1.call-start = ((), (), s32[]{:S(2)}) async-start(), calls=%async_computation.31 | async-start | bytes 2621440 | tf_op jit(solution)/shard_map/while/body/eval_jaxpr/all_gather | solution.py:49
  188.8 275.9 %reduce-scatter.46.cloned.1.call-start = ((), (), s32[]{:S(2)}) async-start(), calls=%async_computation.32 | async-start | bytes 2621440 | tf_op jit(solution)/shard_map/while/body/eval_jaxpr/reduce_scatter | solution.py:65
  422.8 115.1 %all-gather.27.cloned.1.call-start = ((), (), s32[]{:S(2)}) async-start(), calls=%async_computation.34 | async-start | bytes 2621440 | tf_op jit(solution)/shard_map/while/body/eval_jaxpr/all_gather | solution.py:49
  467.5 134.1 %reduce-scatter.48.cloned.1.call-start = ((), (), s32[]{:S(2)}) async-start(), calls=%async_computation.35 | async-start | bytes 2621440 | tf_op jit(solution)/shard_map/while/body/eval_jaxpr/reduce_scatter | solution.py:65
  559.9 118.8 %all-gather.29.cloned.1.call-start = ((), (), s32[]{:S(2)}) async-start(), calls=%async_computation.36 | async-start | bytes 2621440 | tf_op jit(solution)/shard_map/while/body/eval_jaxpr/all_gather | solution.py:49
  605.0 153.3 %reduce-scatter.50.cloned.1.call-start = ((), (), s32[]{:S(2)}) async-start(), calls=%async_computation.39 | async-start | bytes 2621440 | tf_op jit(solution)/shard_map/while/body/eval_jaxpr/reduce_scatter | solution.py:65
  870.3 116.6 %reduce-scatter.54.cloned.1.call-start = ((), (), s32[]{:S(2)}) async-start(), calls=%async_computation.43 | async-start | bytes 2621440 | tf_op jit(solution)/shard_map/while/body/eval_jaxpr/reduce_scatter | solution.py:71
  991.7 225.5 %reduce-scatter.56.cloned.1.call-start = ((), (), s32[]{:S(2)}) async-start(), calls=%async_computation.45 | async-start | bytes 2621440 | tf_op jit(solution)/shard_map/while/body/eval_jaxpr/reduce_scatter | solution.py:71
  1347.3 152.6 %reduce-scatter.44.cloned.1.call-start = ((), (), s32[]{:S(2)}) async-start(), calls=%async_computation.30 | async-start | bytes 2621440 | tf_op jit(solution)/shard_map/while/body/eval_jaxpr/reduce_scatter | solution.py:65
  1456.4 119.8 %all-gather.23.cloned.1.call-start = ((), (), s32[]{:S(2)}) async-start(), calls=%async_computation.31 | async-start | bytes 2621440 | tf_op jit(solution)/shard_map/while/body/eval_jaxpr/all_gather | solution.py:49
  1504.8 276.1 %reduce-scatter.46.cloned.1.call-start = ((), (), s32[]{:S(2)}) async-start(), calls=%async_computation.32 | async-start | bytes 2621440 | tf_op jit(solution)/shard_map/while/body/eval_jaxpr/reduce_scatter | solution.py:65
  1738.7 115.1 %all-gather.27.cloned.1.call-start = ((), (), s32[]{:S(2)}) async-start(), calls=%async_computation.34 | async-start | bytes 2621440 | tf_op jit(solution)/shard_map/while/body/eval_jaxpr/all_gather | solution.py:49
  1783.7 134.0 %reduce-scatter.48.cloned.1.call-start = ((), (), s32[]{:S(2)}) async-start(), calls=%async_computation.35 | async-start | bytes 2621440 | tf_op jit(solution)/shard_map/while/body/eval_jaxpr/reduce_scatter | solution.py:65
  1875.8 119.0 %all-gather.29.cloned.1.call-start = ((), (), s32[]{:S(2)}) async-start(), calls=%async_computation.36 | async-start | bytes 2621440 | tf_op jit(solution)/shard_map/while/body/eval_jaxpr/all_gather | solution.py:49
  1921.0 153.2 %reduce-scatter.50.cloned.1.call-start = ((), (), s32[]{:S(2)}) async-start(), calls=%async_computation.39 | async-start | bytes 2621440 | tf_op jit(solution)/shard_map/while/body/eval_jaxpr/reduce_scatter | solution.py:65
  2186.3 116.6 %reduce-scatter.54.cloned.1.call-start = ((), (), s32[]{:S(2)}) async-start(), calls=%async_computation.43 | async-start | bytes 2621440 | tf_op jit(solution)/shard_map/while/body/eval_jaxpr/reduce_scatter | solution.py:71
  2307.7 225.5 %reduce-scatter.56.cloned.1.call-start = ((), (), s32[]{:S(2)}) async-start(), calls=%async_computation.45 | async-start | bytes 2621440 | tf_op jit(solution)/shard_map/while/body/eval_jaxpr/reduce_scatter | solution.py:71
  2658.8 150.3 %reduce-scatter.28.cloned.1.call-start = ((), (), s32[]{:S(2)}) async-start(), calls=%async_computation.18 | async-start | bytes 1769472 | tf_op jit(solution)/shard_map/reduce_scatter | solution.py:463
  2661.9 191.5 %reduce-scatter.36.cloned.1.call-start = ((), (), s32[]{:S(2)}) async-start(), calls=%async_computation.22 | async-start | bytes 2359296
  2667.2 231.0 %reduce-scatter.42.cloned.1.call-start = ((), (), s32[]{:S(2)}) async-start(), calls=%async_computation.25 | async-start | bytes 2359296
  2672.4 270.1 %reduce-scatter.26.cloned.1.call-start = ((), (), s32[]{:S(2)}) async-start(), calls=%async_computation.17 | async-start | bytes 2359296 | tf_op jit(solution)/shard_map/reduce_scatter | solution.py:457
  2676.3 310.8 %reduce-scatter.32.cloned.1.call-start = ((), (), s32[]{:S(2)}) async-start(), calls=%async_computation.20 | async-start | bytes 2359296 | tf_op jit(solution)/shard_map/reduce_scatter | solution.py:475
  2680.3 443.6 %reduce-scatter.34.cloned.1.call-start = ((), (), s32[]{:S(2)}) async-start(), calls=%async_computation.21 | async-start | bytes 540672 | tf_op jit(solution)/shard_map/reduce_scatter | solution.py:739
  (283 other events, 13919.1 us)
Sparse Core Ops, SparseCore 0:
  28.0 46.2 all-gather.14
  140.0 43.8 reduce-scatter.43
  214.0 45.9 all-gather.22
  491.9 45.9 all-gather.26
  632.8 45.9 all-gather.28
  714.3 43.8 reduce-scatter.49
  765.0 45.2 all-gather.34
  822.3 42.5 reduce-scatter.51
  870.4 45.2 all-gather.36
  991.8 45.2 all-gather.38
  1174.5 42.5 reduce-scatter.55
  1223.3 45.2 all-gather.40
  1281.3 42.5 reduce-scatter.57
  1346.0 44.3 all-gather.14
  1455.9 43.8 reduce-scatter.43
  1530.2 45.9 all-gather.22
  1807.9 45.9 all-gather.26
  1948.8 45.9 all-gather.28
  2030.3 43.8 reduce-scatter.49
  2081.0 45.2 all-gather.34
  2138.4 42.5 reduce-scatter.51
  2186.4 45.2 all-gather.36
  2307.8 45.2 all-gather.38
  2539.3 45.2 all-gather.40
  (20 shorter events, 654.4 us)
Sparse Core Ops, SparseCore 1:
  2656.5 33.7 reduce-scatter.37
  2694.1 34.2 reduce-scatter.39
  2731.4 35.9 reduce-scatter.29
  2770.7 38.3 reduce-scatter.27
  2812.4 41.0 reduce-scatter.35
  2857.1 41.1 reduce-scatter.41
  2901.4 41.1 reduce-scatter.25
  2946.0 41.1 reduce-scatter.31
  2989.8 134.0 reduce-scatter.33
where the time goes:
time: 3140 us; the launch traced here: 3130 us
  waiting for transfers between devices  1950 us (62%)
  local copies, waits for them, and re-layouts  472 us (15%)
  matrix products  363 us (12%)
  other arithmetic  174 us (6%)
  blocking collectives  141 us (4%)
    all_gather x8, waiting for transfers between devices, spread(): return lax.all_gather(row_block, 'tensor', axis=0, tiled=True)  376 us
    reduce_scatter x8, waiting for transfers between devices, collect_term(): lax.psum_scatter(term(0, total_rows).astype(jnp.bfloat16), 'tensor', scat...  340 us
    all_gather x8, waiting for transfers between devices, spread_back(): return lax.all_gather(row_block, 'tensor', axis=0, tiled=True)  314 us
    reduce_scatter x8, waiting for transfers between devices, collect_back_term(): lax.psum_scatter(term(0, total_rows).astype(jnp.bfloat16), 'tensor', scat...  282 us
    while x522, local copies, waits for them, and re-layouts  250 us
    reduce_scatter x1, waiting for transfers between devices, body(): lax.psum_scatter(vector_acc, ('dp', 'tensor'), scatter_dimension=1, tiled...  135 us
    unnamed x13, waiting for transfers between devices  90.2 us
  transfers between devices with their start and end apart: 53, of which 52 were waited for; matrix products, arithmetic and copies ran while one was open for 6% of the time, Pallas kernels for 0%

commit v1 on v0

v1 whole, which is shorter than its diff:
```python
import jax
import jax.numpy as jnp
from jax import lax
from jax.experimental import pallas as pl
from jax.experimental.pallas import tpu as pltpu
from jax.sharding import Mesh
from jax.sharding import PartitionSpec as P

HEADS = 16
HEAD_DIM = 64
FF = 4096
KERNEL = 31
LEFT = 64
OFFSETS = 73
EPSILON = 1e-05

LANES = 128
RIGHT = OFFSETS - 1 - LEFT
NT = (((1,), (1,)), ((), ()))
NN = (((1,), (0,)), ((), ()))
TN = (((0,), (0,)), ((), ()))


def dot_f32(left_side, right_side, dims):
    return lax.dot_general(left_side, right_side, dims, preferred_element_type=jnp.float32)


def band_distance():
    shape = (LANES, 3 * LANES)
    return (
        lax.broadcasted_iota(jnp.int32, shape, 1)
        - LANES
        - lax.broadcasted_iota(jnp.int32, shape, 0)
    )


def add_relative(score_ref, source, live_row, distance, block, number, key_blocks):
    rows = slice(number * LANES, (number + 1) * LANES)
    own = source[rows]
    left_col = own[:, 2 * LANES - LEFT : 2 * LANES - LEFT + 1]
    right_col = own[:, RIGHT : RIGHT + 1]
    rolled = pltpu.roll(own, LANES, 1, stride=1, stride_axis=0)
    rolled = jnp.concatenate([rolled, rolled[:, :LANES]], axis=1)
    band = jnp.where(
        distance <= -LEFT, left_col, jnp.where(distance >= RIGHT, right_col, rolled)
    )
    lanes = lax.broadcasted_iota(jnp.int32, (LANES, 3 * LANES), 1)
    band = band - jnp.where(lanes < LANES, left_col, right_col)
    window = pl.ds(pl.multiple_of(block * LANES, LANES), 3 * LANES)
    score_ref[rows, window] += band
    base = jnp.concatenate(
        [
            jnp.broadcast_to(jnp.where(place < block, left_col, right_col), (LANES, LANES))
            for place in range(key_blocks)
        ],
        axis=1,
    )
    return score_ref[rows, LANES : LANES + key_blocks * LANES] + base + live_row


def live_keys(meta_ref, key_count):
    places = lax.broadcasted_iota(jnp.int32, (1, key_count), 1)
    return jnp.where(places < meta_ref[1], 0.0, -1e30).astype(jnp.float32)


def attend_kernel(meta_ref, q_ref, k_ref, v_ref, e_ref, c_ref, lse_ref, score_ref, share_ref):
    row_count, key_count = q_ref.shape[0], k_ref.shape[0]
    pair = pl.program_id(0)
    lanes = lax.broadcasted_iota(jnp.int32, (row_count, LANES), 1)
    live_row = live_keys(meta_ref, key_count)
    distance = band_distance()
    result = None
    for half in range(2):
        mine = (lanes < HEAD_DIM) if half == 0 else (lanes >= HEAD_DIM)
        q_half = jnp.where(mine, q_ref[...], 0)
        score_ref[:, LANES : LANES + key_count] = dot_f32(q_half, k_ref[...], NT)
        source = dot_f32(q_half, e_ref[...], NT).astype(jnp.bfloat16).astype(jnp.float32)
        for number in range(row_count // LANES):
            rows = slice(number * LANES, (number + 1) * LANES)
            scores = add_relative(
                score_ref, source, live_row, distance, meta_ref[0] + number, number,
                key_count // LANES,
            )
            peak = jnp.max(scores, axis=1, keepdims=True)
            grown = jnp.exp(scores - peak)
            total = jnp.sum(grown, axis=1, keepdims=True)
            share_ref[rows] = (grown * (1.0 / total)).astype(jnp.bfloat16)
            lse_ref[rows] = jnp.where(
                lanes[rows] == 2 * pair + half, peak + jnp.log(total), lse_ref[rows]
            )
        context = dot_f32(share_ref[...], v_ref[...], NN)
        result = context if half == 0 else jnp.where(mine, context, result)
    c_ref[...] = result.astype(jnp.bfloat16)


def attend_back_kernel(
    meta_ref, q_ref, k_ref, v_ref, e_ref, dc_ref, c_ref, lse_ref,
    dq_ref, dk_ref, dv_ref, de_ref,
    score_ref, grad_ref, share_ref, slope_ref, source_ref, wide_ref,
):
    row_count, key_count = q_ref.shape[0], k_ref.shape[0]
    key_blocks = key_count // LANES
    pair = pl.program_id(0)
    lanes = lax.broadcasted_iota(jnp.int32, (row_count, LANES), 1)
    live_row = live_keys(meta_ref, key_count)
    distance = band_distance()
    inside = (distance > -LEFT) & (distance < RIGHT)
    square = (LANES, LANES)
    flip = (
        lax.broadcasted_iota(jnp.int32, square, 0) + lax.broadcasted_iota(jnp.int32, square, 1)
        == LANES - 1
    ).astype(jnp.float32).astype(jnp.bfloat16)
    spots = lax.broadcasted_iota(jnp.int32, (LANES, 2 * LANES), 1)

    @pl.when(pair == 0)
    def _():
        shape = (key_count, LANES)
        before = lax.broadcasted_iota(jnp.int32, shape, 0) < LANES * lax.broadcasted_iota(
            jnp.int32, shape, 1
        )
        wide_ref[:, LANES:] = before.astype(jnp.float32).astype(jnp.bfloat16)
        slope_ref[:, :LANES] = jnp.zeros((row_count, LANES), jnp.bfloat16)
        slope_ref[:, LANES + key_count :] = jnp.zeros((row_count, LANES), jnp.bfloat16)
        de_ref[...] = jnp.zeros(de_ref.shape, jnp.float32)

    wide_ref[:, :LANES] = k_ref[...]
    inner_all = dc_ref[...].astype(jnp.float32) * c_ref[...].astype(jnp.float32)
    grad_q = grad_k = grad_v = None
    for half in range(2):
        mine = (lanes < HEAD_DIM) if half == 0 else (lanes >= HEAD_DIM)
        q_half = jnp.where(mine, q_ref[...], 0)
        dc_half = jnp.where(mine, dc_ref[...], 0)
        score_ref[:, LANES : LANES + key_count] = dot_f32(q_half, k_ref[...], NT)
        grad_ref[...] = dot_f32(dc_half, v_ref[...], NT)
        source = dot_f32(q_half, e_ref[...], NT).astype(jnp.bfloat16).astype(jnp.float32)
        inner = jnp.sum(jnp.where(mine, inner_all, 0.0), axis=1, keepdims=True)
        level = jnp.sum(
            jnp.where(lanes == 2 * pair + half, lse_ref[...], 0.0), axis=1, keepdims=True
        )
        for number in range(row_count // LANES):
            rows = slice(number * LANES, (number + 1) * LANES)
            scores = add_relative(
                score_ref, source, live_row, distance, meta_ref[0] + number, number, key_blocks
            )
            shares = jnp.exp(scores - level[rows])
            share_ref[rows] = shares.astype(jnp.bfloat16)
            slope_ref[rows, LANES : LANES + key_count] = (
                shares * (grad_ref[rows] - inner[rows])
            ).astype(jnp.bfloat16)
        slopes = slope_ref[:, LANES : LANES + key_count]
        wide = dot_f32(slopes, wide_ref[...], NN)
        before = wide[:, LANES:]
        for number in range(row_count // LANES):
            rows = slice(number * LANES, (number + 1) * LANES)
            block = meta_ref[0] + number
            window = pl.ds(pl.multiple_of(block * LANES, LANES), 3 * LANES)
            seen = slope_ref[rows, window].astype(jnp.float32)
            sums, spot = before[rows], lanes[rows]
            far_left = jnp.sum(
                jnp.where(spot == jnp.maximum(block - 1, 0), sums, 0.0), axis=1, keepdims=True
            ) + jnp.sum(jnp.where(distance <= -LEFT, seen, 0.0), axis=1, keepdims=True)
            far_right = jnp.sum(
                jnp.where(spot == key_blocks, sums, 0.0)
                - jnp.where(spot == jnp.minimum(block + 2, key_blocks), sums, 0.0),
                axis=1,
                keepdims=True,
            ) + jnp.sum(jnp.where(distance >= RIGHT, seen, 0.0), axis=1, keepdims=True)
            band = jnp.where(inside, seen, 0.0)
            band = jnp.concatenate(
                [band[:, :LANES] + band[:, 2 * LANES :], band[:, LANES : 2 * LANES]], axis=1
            )
            turned = dot_f32(flip, band.astype(jnp.bfloat16), NN)
            turned = pltpu.roll(turned, 1, 1, stride=1, stride_axis=0)
            turned = dot_f32(flip, turned.astype(jnp.bfloat16), NN)
            turned = jnp.where(
                spots == 2 * LANES - LEFT, far_left, jnp.where(spots == RIGHT, far_right, turned)
            )
            source_ref[rows] = turned.astype(jnp.bfloat16)
        q_part = wide[:, :LANES] + dot_f32(source_ref[...], e_ref[...], NN)
        k_part = dot_f32(q_half, slopes, TN)
        v_part = dot_f32(dc_half, share_ref[...], TN)
        de_ref[...] += dot_f32(q_half, source_ref[...], TN)
        grad_q = q_part if half == 0 else jnp.where(mine, q_part, grad_q)
        grad_k = k_part if half == 0 else grad_k + k_part
        grad_v = v_part if half == 0 else grad_v + v_part
    dq_ref[...] = (grad_q * HEAD_DIM ** (-0.5)).astype(jnp.bfloat16)
    dk_ref[...] = grad_k.T.astype(jnp.bfloat16)
    dv_ref[...] = grad_v.T.astype(jnp.bfloat16)


def pair_spec(row_count):
    return pl.BlockSpec((row_count, LANES), lambda pair, meta: (0, pair))


def fixed_spec(row_count, column_count):
    return pl.BlockSpec((row_count, column_count), lambda pair, meta: (0, 0))


def attend(meta, queries, key_rows, value_rows, table):
    row_count, width = queries.shape
    key_count = key_rows.shape[0]
    return pl.pallas_call(
        attend_kernel,
        grid_spec=pltpu.PrefetchScalarGridSpec(
            num_scalar_prefetch=1,
            grid=(width // LANES,),
            in_specs=[
                pair_spec(row_count),
                pair_spec(key_count),
                pair_spec(key_count),
                fixed_spec(2 * LANES, LANES),
            ],
            out_specs=[pair_spec(row_count), fixed_spec(row_count, LANES)],
            scratch_shapes=[
                pltpu.VMEM((row_count, key_count + 2 * LANES), jnp.float32),
                pltpu.VMEM((row_count, key_count), jnp.bfloat16),
            ],
        ),
        out_shape=[
            jax.ShapeDtypeStruct((row_count, width), jnp.bfloat16),
            jax.ShapeDtypeStruct((row_count, LANES), jnp.float32),
        ],
        compiler_params=pltpu.CompilerParams(vmem_limit_bytes=48 * 2**20),
        name="attend",
    )(meta, queries, key_rows, value_rows, table)


def attend_back(meta, queries, key_rows, value_rows, table, grad_context, context, levels):
    row_count, width = queries.shape
    key_count = key_rows.shape[0]
    return pl.pallas_call(
        attend_back_kernel,
        grid_spec=pltpu.PrefetchScalarGridSpec(
            num_scalar_prefetch=1,
            grid=(width // LANES,),
            in_specs=[
                pair_spec(row_count),
                pair_spec(key_count),
                pair_spec(key_count),
                fixed_spec(2 * LANES, LANES),
                pair_spec(row_count),
                pair_spec(row_count),
                fixed_spec(row_count, LANES),
            ],
            out_specs=[
                pair_spec(row_count),
                pair_spec(key_count),
                pair_spec(key_count),
                fixed_spec(LANES, 2 * LANES),
            ],
            scratch_shapes=[
                pltpu.VMEM((row_count, key_count + 2 * LANES), jnp.float32),
                pltpu.VMEM((row_count, key_count), jnp.float32),
                pltpu.VMEM((row_count, key_count), jnp.bfloat16),
                pltpu.VMEM((row_count, key_count + 2 * LANES), jnp.bfloat16),
                pltpu.VMEM((row_count, 2 * LANES), jnp.bfloat16),
                pltpu.VMEM((key_count, 2 * LANES), jnp.bfloat16),
            ],
        ),
        out_shape=[
            jax.ShapeDtypeStruct((row_count, width), jnp.bfloat16),
            jax.ShapeDtypeStruct((key_count, width), jnp.bfloat16),
            jax.ShapeDtypeStruct((key_count, width), jnp.bfloat16),
            jax.ShapeDtypeStruct((LANES, 2 * LANES), jnp.float32),
        ],
        compiler_params=pltpu.CompilerParams(vmem_limit_bytes=48 * 2**20),
        name="attend_back",
    )(meta, queries, key_rows, value_rows, table, grad_context, context, levels)


def wide_table(table_low):
    places = jnp.arange(2 * LANES)
    offsets = jnp.clip(jnp.where(places < LANES, places, places - 2 * LANES) + LEFT, 0, OFFSETS - 1)
    rows = table_low[offsets]
    return jnp.concatenate([rows, rows], axis=1)


def table_grad(wide_grad):
    folded = (wide_grad[:HEAD_DIM] + wide_grad[HEAD_DIM:]).T
    return jnp.concatenate([folded[2 * LANES - LEFT :], folded[: RIGHT + 1]], axis=0)


def apply_swish(values):
    return values * jax.nn.sigmoid(values)


def swish_slope(values):
    logistic = jax.nn.sigmoid(values)
    return logistic + values * logistic * (1.0 - logistic)


def matmul(left_side, right_side):
    return dot_f32(left_side, right_side, NN)


def norm_rows(values, gain_row, shift_row):
    centred = values - jnp.mean(values, axis=-1, keepdims=True)
    variance = jnp.mean(centred * centred, axis=-1, keepdims=True)
    inverse = lax.rsqrt(variance + EPSILON)
    normal = centred * inverse
    return (normal * gain_row + shift_row, normal, inverse)


def norm_back(grad_out, normal, inverse, gain_row):
    grad_normal = grad_out * gain_row
    grad_in = inverse * (
        grad_normal
        - jnp.mean(grad_normal, axis=-1, keepdims=True)
        - normal * jnp.mean(grad_normal * normal, axis=-1, keepdims=True)
    )
    return (grad_in, jnp.sum(grad_out * normal, axis=0), jnp.sum(grad_out, axis=0))


TENSOR = ("far", "z")


class Place:
    def __init__(self):
        self.count = {axis: lax.axis_size(axis) for axis in ("y", "x", "core", "far", "z")}
        self.index = {axis: lax.axis_index(axis) for axis in ("y", "x", "core", "far", "z")}
        self.count["t"] = self.count["far"] * self.count["z"]
        self.index["t"] = self.index["far"] * self.count["z"] + self.index["z"]
        self.count["seq"] = self.count["far"] * 2
        self.index["seq"] = self.index["far"] * 2 + self.index["core"]
        self.names = {"t": TENSOR, "seq": ("core", "far")}

    def seq_pair(self, start, end):
        far = self.count["far"]
        return ((start % 2) * far + start // 2, (end % 2) * far + end // 2)

    def turn(self, block, axis, step):
        size = self.count[axis]
        pairs = [(start, (start + step) % size) for start in range(size)]
        if axis == "seq":
            pairs = [self.seq_pair(*pair) for pair in pairs]
        return lax.ppermute(block, self.names.get(axis, axis), pairs)

    def after(self, axis, step):
        return lax.rem(self.index[axis] + step, self.count[axis])


def steps(place, axis):
    return range(1, place.count[axis])


def halves_of(shard, by_rows):
    row_dim = 1 if by_rows else 0
    half = shard.shape[row_dim] // 2
    return [lax.slice_in_dim(shard, number * half, (number + 1) * half, axis=row_dim) for number in range(2)]


def gather_half(place, block, order):
    stack = jnp.stack([block] + [place.turn(block, "t", step) for step in steps(place, "t")])
    pieces = {(0, 0, 0): stack}
    for axis in order:
        where = ("y", "x", "core").index(axis)
        for key, piece in list(pieces.items()):
            for step in steps(place, axis):
                new_key = key[:where] + (step,) + key[where + 1 :]
                pieces[new_key] = place.turn(piece, axis, step)
    return pieces


ORDERS = (("x", "y", "core"), ("y", "x", "core"))


def assemble(place, halves, by_rows):
    keys = [(number, key) for number, pieces in enumerate(halves) for key in pieces]
    arrays = [halves[number][key] for number, key in keys]
    counts = place.count
    tensor_count = counts["t"]
    dp_count = counts["y"] * counts["x"] * counts["core"]
    dtype = arrays[0].dtype
    if by_rows:
        _, depth, half_rows, columns = arrays[0].shape
        shard_rows = half_rows * len(halves)
        out_shape = (depth, shard_rows * dp_count, columns * tensor_count)
    else:
        _, half_rows, columns = arrays[0].shape
        shard_rows = half_rows * len(halves)
        aligned = columns % LANES == 0
        if aligned:
            out_shape = (shard_rows * tensor_count, columns * dp_count)
        else:
            out_shape = (dp_count, shard_rows * tensor_count, columns)

    def kernel(meta_ref, *refs):
        piece_refs, out_ref, sem = refs[: len(keys)], refs[len(keys)], refs[len(keys) + 1]
        copies = []
        for (number, key), piece_ref in zip(keys, piece_refs):
            spot = [
                lax.rem(meta_ref[i] - key[i] + counts[axis], counts[axis])
                for i, axis in enumerate(("y", "x", "core"))
            ]
            dp_spot = (spot[0] * counts["x"] + spot[1]) * counts["core"] + spot[2]
            for step in range(tensor_count):
                t_spot = lax.rem(meta_ref[3] - step + tensor_count, tensor_count)
                if by_rows:
                    rows = pl.ds(
                        pl.multiple_of(dp_spot * shard_rows + number * half_rows, half_rows), half_rows
                    )
                    target = out_ref.at[:, rows, pl.ds(pl.multiple_of(t_spot * columns, columns), columns)]
                else:
                    rows = pl.ds(
                        pl.multiple_of(t_spot * shard_rows + number * half_rows, half_rows), half_rows
                    )
                    if aligned:
                        target = out_ref.at[rows, pl.ds(pl.multiple_of(dp_spot * columns, columns), columns)]
                    else:
                        target = out_ref.at[dp_spot, rows, :]
                copy = pltpu.make_async_copy(piece_ref.at[step], target, sem.at[len(copies)])
                copy.start()
                copies.append(copy)
        for copy in copies:
            copy.wait()

    meta = jnp.stack([place.index[axis] for axis in ("y", "x", "core", "t")]).astype(jnp.int32)
    whole = pl.pallas_call(
        kernel,
        grid_spec=pltpu.PrefetchScalarGridSpec(
            num_scalar_prefetch=1,
            grid=(),
            in_specs=[pl.BlockSpec(memory_space=pl.ANY)] * len(keys),
            out_specs=pl.BlockSpec(memory_space=pltpu.VMEM),
            scratch_shapes=[pltpu.SemaphoreType.DMA((len(keys) * tensor_count,))],
        ),
        out_shape=jax.ShapeDtypeStruct(out_shape, dtype),
        compiler_params=pltpu.CompilerParams(vmem_limit_bytes=20 * 2**20),
        name="assemble",
    )(meta, *arrays)
    if not by_rows and not aligned:
        whole = whole.transpose(1, 0, 2).reshape(shard_rows * tensor_count, columns * dp_count)
    return whole


def fetch(place, shard, by_rows):
    halves = [
        gather_half(place, half, order) for half, order in zip(halves_of(shard, by_rows), ORDERS)
    ]
    return assemble(place, halves, by_rows)


class Part:
    def __init__(self, array, by_rows, spans):
        self.array, self.by_rows, self.spans = array, by_rows, spans

    def pick(self, axis, index):
        spans = dict(self.spans)
        count = spans[axis]
        if count == 1:
            return self
        spans[axis] = 1
        array = self.array
        if self.by_rows:
            if axis == "t":
                width = array.shape[-1] // count
                array = lax.dynamic_slice_in_dim(array, index * width, width, axis=4)
            else:
                array = lax.dynamic_slice_in_dim(array, index, 1, axis={"y": 1, "x": 2}[axis])
        elif axis == "t":
            array = lax.dynamic_slice_in_dim(array, index, 1, axis=0)
        else:
            width = array.shape[-1] // (self.spans["y"] * self.spans["x"])
            if axis == "y":
                width = width * self.spans["x"]
                array = lax.dynamic_slice_in_dim(array, index * width, width, axis=2)
            else:
                array = jnp.concatenate(
                    [
                        lax.dynamic_slice_in_dim(array, (row * count + index) * width, width, axis=2)
                        for row in range(self.spans["y"])
                    ],
                    axis=2,
                )
        return Part(array, self.by_rows, spans)


def added(parts):
    total = parts[0].array.astype(jnp.float32)
    for part in parts[1:]:
        total = total + part.array.astype(jnp.float32)
    return total


def reduce_half(place, parts, order):
    for axis in order:
        arrived = []
        for step in steps(place, axis):
            picked = [part.pick(axis, place.after(axis, step)) for part in parts]
            message = place.turn(added(picked).astype(jnp.bfloat16), axis, step)
            arrived.append(Part(message, picked[0].by_rows, picked[0].spans))
        parts = [part.pick(axis, place.index[axis]) for part in parts] + arrived
    return added(parts)


BACK_ORDERS = (("y", "x", "t"), ("x", "y", "t"))


def reduce_weight(place, product, by_rows, depth):
    counts = place.count
    spans = {"y": counts["y"], "x": counts["x"], "t": counts["t"]}
    other = place.turn(product(1 - place.index["core"]), "core", 1)
    mine = product(place.index["core"])
    results = []
    for number, order in enumerate(BACK_ORDERS):
        parts = []
        for array in (mine, other):
            if by_rows:
                block = array.reshape(
                    depth, counts["y"], counts["x"], 2, -1, array.shape[-1]
                )[:, :, :, number]
            else:
                block = array.reshape(counts["t"], 2, -1, array.shape[-1])[:, number]
            parts.append(Part(block, by_rows, spans))
        results.append(reduce_half(place, parts, order))
    if by_rows:
        return jnp.concatenate([one[:, 0, 0] for one in results], axis=1)
    return jnp.concatenate([one[0] for one in results], axis=0)


def core_columns(place, rows_in, core):
    blocks = place.count["y"] * place.count["x"]
    width = rows_in.shape[-1] // (2 * blocks)
    return jnp.concatenate(
        [
            lax.dynamic_slice_in_dim(rows_in, (2 * block + core) * width, width, axis=-1)
            for block in range(blocks)
        ],
        axis=-1,
    )


def grad_by_rows(place, inputs, grads):
    def product(core):
        left_side = core_columns(place, inputs, core)
        return jnp.stack([dot_f32(left_side, grad, TN).astype(jnp.bfloat16) for grad in grads])

    return reduce_weight(place, product, True, len(grads))


def grad_by_columns(place, inputs, grad):
    def product(core):
        return dot_f32(inputs, core_columns(place, grad, core), TN).astype(jnp.bfloat16)

    return reduce_weight(place, product, False, 1)


def to_clip(place, blocks):
    micro, z_count = blocks.shape[0], place.count["z"]
    z_here = place.index["z"]
    arrived = []
    for step in range(micro):
        block = lax.dynamic_index_in_dim(blocks, lax.rem(z_here + step, micro), 0, keepdims=False)
        arrived.append(lax.ppermute(block, ("core", "z"), clip_pairs(micro, z_count, step)))
    stack = jnp.stack(arrived)
    ordered = [
        lax.dynamic_index_in_dim(stack, lax.rem(z_here - spot + micro, micro), 0, keepdims=False)
        for spot in range(micro)
    ]
    return jnp.concatenate(ordered, axis=0)


def clip_pairs(micro, z_count, step):
    return [
        (core * z_count + z, (z // micro) * z_count + micro * core + (step + z) % micro)
        for core in range(2)
        for z in range(z_count)
    ]


def from_clip(place, rows_in, micro):
    z_count, z_here = place.count["z"], place.index["z"]
    blocks = rows_in.reshape(micro, -1, rows_in.shape[-1])
    arrived = []
    for step in range(micro):
        spot = lax.rem(z_here - step + micro, micro)
        block = lax.dynamic_index_in_dim(blocks, spot, 0, keepdims=False)
        pairs = [(end, start) for start, end in clip_pairs(micro, z_count, step)]
        arrived.append(lax.ppermute(block, ("core", "z"), pairs))
    stack = jnp.stack(arrived)
    return jnp.stack(
        [
            lax.dynamic_index_in_dim(stack, lax.rem(number - z_here % micro + micro, micro), 0, keepdims=False)
            for number in range(micro)
        ]
    )


def all_rows(place, own):
    count = place.count["seq"]
    whole = jnp.zeros((count,) + own.shape, own.dtype)
    for step in range(count):
        block = own if step == 0 else place.turn(own, "seq", step)
        spot = lax.rem(place.index["seq"] - step + count, count)
        whole = lax.dynamic_update_index_in_dim(whole, block, spot, 0)
    return whole.reshape((count * own.shape[0],) + own.shape[1:])


def own_sum(place, partial):
    count = place.count["seq"]
    blocks = partial.reshape(count, -1, partial.shape[-1])
    total = lax.dynamic_index_in_dim(blocks, place.index["seq"], 0, keepdims=False).astype(jnp.float32)
    for step in range(1, count):
        message = lax.dynamic_index_in_dim(blocks, place.after("seq", step), 0, keepdims=False)
        total = total + place.turn(message, "seq", step).astype(jnp.float32)
    return total


def neighbour_rows(place, rows_in, step):
    count = place.count["seq"]
    pairs = [
        place.seq_pair(start, start + step) for start in range(count) if 0 <= start + step < count
    ]
    return lax.ppermute(rows_in, place.names["seq"], pairs)


def feed_forward(inputs, up_weight, down_weight, up_bias, down_bias, gain_row, shift_row):
    normed, normal, inverse = norm_rows(inputs, gain_row, shift_row)
    normed = normed.astype(jnp.bfloat16)
    upper_rows = matmul(normed, up_weight) + up_bias
    hidden = apply_swish(upper_rows).astype(jnp.bfloat16)
    result = matmul(hidden, down_weight) + down_bias
    return (result, (normal, inverse, normed, upper_rows.astype(jnp.bfloat16), hidden))


def feed_back(place, grad_result, stored, up_weight, down_weight, gain_row):
    normal, inverse, normed, upper_rows, hidden = stored
    grad_low = grad_result.astype(jnp.bfloat16)
    grad_down = grad_by_columns(place, hidden, grad_low)
    grad_hidden = dot_f32(grad_low, down_weight, NT)
    grad_upper = (grad_hidden * swish_slope(upper_rows.astype(jnp.float32))).astype(jnp.bfloat16)
    grad_up = grad_by_rows(place, normed, [grad_upper])[0]
    grad_normed = dot_f32(grad_upper, up_weight, NT)
    grad_in, grad_gain, grad_shift = norm_back(grad_normed, normal, inverse, gain_row)
    up_bias_grad = jnp.sum(grad_upper.astype(jnp.float32), axis=0)
    down_bias_grad = jnp.sum(grad_low.astype(jnp.float32), axis=0)
    return (grad_in, (grad_up, grad_down), (grad_gain, grad_shift, up_bias_grad, down_bias_grad))


def body(
    frames,
    cotangent,
    clip_valid,
    frame_counts,
    rel_rows,
    first_up,
    first_down,
    attend_in,
    attend_out,
    pointwise_in,
    pointwise_out,
    second_up,
    second_down,
    vectors,
    distance,
):
    place = Place()
    micro, _, width = frames.shape
    ratio_rows = FF // width
    attend_base = 3 + ratio_rows
    conv_base = attend_base + 5
    second_base = conv_base + 4
    final_base = second_base + 3 + ratio_rows
    taps_base = final_base + 2
    scale = HEAD_DIM ** (-0.5)

    rows_low = to_clip(place, frames)
    vector_wide = lax.all_gather(vectors, ("y", "x", "core"), axis=1, tiled=True).astype(jnp.float32)
    up_one = fetch(place, first_up[None], True)[0]
    down_one = fetch(place, first_down, False)
    attend_mix = fetch(place, attend_in, True)
    attend_back_weight = fetch(place, attend_out, False)
    point_mix = fetch(place, pointwise_in, True)
    point_back = fetch(place, pointwise_out, False)
    up_two = fetch(place, second_up[None], True)[0]
    down_two = fetch(place, second_down, False)
    cot_low = to_clip(place, cotangent)

    row_count = rows_low.shape[0]
    slot_len = row_count * place.count["seq"]
    z_here = place.index["z"]
    own_facts = jnp.stack([clip_valid, frame_counts])
    other_facts = place.turn(own_facts, "core", 1)
    facts = jnp.where(z_here // micro == place.index["core"], own_facts, other_facts)
    facts = lax.dynamic_index_in_dim(facts, lax.rem(z_here, micro), 1, keepdims=False)
    valid_flag = (facts[0] > 0).astype(jnp.float32)
    first_row = place.index["seq"] * row_count
    live = ((first_row + jnp.arange(row_count)) < facts[1]).astype(jnp.float32)[:, None]
    meta = jnp.stack([place.index["seq"] * (row_count // LANES), facts[1]]).astype(jnp.int32)
    pick_rows = (rel_rows[:, None] == jnp.arange(OFFSETS)[None, :]).astype(jnp.bfloat16)
    table = wide_table(matmul(pick_rows, distance).astype(jnp.bfloat16))

    rows_in = rows_low.astype(jnp.float32)
    rows_cot = cot_low.astype(jnp.float32)
    one_out, one_kept = feed_forward(
        rows_in,
        up_one,
        down_one,
        vector_wide[2 : 2 + ratio_rows].reshape(FF),
        vector_wide[2 + ratio_rows],
        vector_wide[0],
        vector_wide[1],
    )
    after_one = rows_in + 0.5 * one_out

    attend_normed, attend_normal, attend_inverse = norm_rows(
        after_one, vector_wide[attend_base], vector_wide[attend_base + 1]
    )
    attend_normed = attend_normed.astype(jnp.bfloat16)
    queries = (matmul(attend_normed, attend_mix[0]) + vector_wide[attend_base + 2]).astype(jnp.bfloat16)
    queries = (queries.astype(jnp.float32) * scale).astype(jnp.bfloat16)
    own_keys = matmul(attend_normed, attend_mix[1]).astype(jnp.bfloat16)
    own_values = (matmul(attend_normed, attend_mix[2]) + vector_wide[attend_base + 3]).astype(jnp.bfloat16)
    key_rows, value_rows = all_rows(place, own_keys), all_rows(place, own_values)
    context, levels = attend(meta, queries, key_rows, value_rows, table)
    after_two = after_one + matmul(context, attend_back_weight) + vector_wide[attend_base + 4]

    conv_normed, conv_normal, conv_inverse = norm_rows(
        after_two, vector_wide[conv_base], vector_wide[conv_base + 1]
    )
    conv_normed = conv_normed.astype(jnp.bfloat16)
    linear = matmul(conv_normed, point_mix[0])
    logistic = jax.nn.sigmoid(matmul(conv_normed, point_mix[1]))
    gated = linear * logistic * live
    taps = vector_wide[taps_base : taps_base + KERNEL]
    reach = KERNEL - 1
    padded = jnp.concatenate([neighbour_rows(place, gated[-reach:], 1), gated], axis=0)
    depth_out = jnp.zeros_like(gated)
    for offset in range(KERNEL):
        depth_out = depth_out + taps[offset] * padded[offset : offset + row_count]
    deep_gain = vector_wide[conv_base + 2]
    deep_norm, deep_normal, deep_inverse = norm_rows(depth_out, deep_gain, vector_wide[conv_base + 3])
    activated = apply_swish(deep_norm).astype(jnp.bfloat16)
    after_three = after_two + matmul(activated, point_back)

    two_out, two_kept = feed_forward(
        after_three,
        up_two,
        down_two,
        vector_wide[second_base + 2 : second_base + 2 + ratio_rows].reshape(FF),
        vector_wide[second_base + 2 + ratio_rows],
        vector_wide[second_base],
        vector_wide[second_base + 1],
    )
    after_four = after_three + 0.5 * two_out
    final_rows, final_normal, final_inverse = norm_rows(
        after_four, vector_wide[final_base], vector_wide[final_base + 1]
    )
    frames_out = from_clip(
        place, jnp.where(valid_flag > 0, final_rows, rows_in).astype(jnp.bfloat16), micro
    )

    grad_four, final_gain_grad, final_shift_grad = norm_back(
        rows_cot * valid_flag, final_normal, final_inverse, vector_wide[final_base]
    )
    grad_two_in, two_weights, two_parts = feed_back(
        place, 0.5 * grad_four, two_kept, up_two, down_two, vector_wide[second_base]
    )
    grad_three = grad_four + grad_two_in

    conv_low = grad_three.astype(jnp.bfloat16)
    grad_point_back = grad_by_columns(place, activated, conv_low)
    grad_deep = dot_f32(conv_low, point_back, NT) * swish_slope(deep_norm)
    grad_depth, deep_gain_grad, deep_shift_grad = norm_back(
        grad_deep, deep_normal, deep_inverse, deep_gain
    )
    extended = jnp.concatenate([grad_depth, neighbour_rows(place, grad_depth[:reach], -1)], axis=0)
    grad_gated = jnp.zeros_like(grad_depth)
    tap_grads = []
    for offset in range(KERNEL):
        tap_grads.append(jnp.sum(padded[offset : offset + row_count] * grad_depth, axis=0))
        grad_gated = grad_gated + taps[offset] * extended[reach - offset : reach - offset + row_count]
    grad_gated = grad_gated * live
    grad_linear = (grad_gated * logistic).astype(jnp.bfloat16)
    grad_gate = (grad_gated * linear * logistic * (1.0 - logistic)).astype(jnp.bfloat16)
    grad_point_mix = grad_by_rows(place, conv_normed, [grad_linear, grad_gate])
    grad_conv_normed = dot_f32(grad_linear, point_mix[0], NT) + dot_f32(grad_gate, point_mix[1], NT)
    grad_conv_in, conv_gain_grad, conv_shift_grad = norm_back(
        grad_conv_normed, conv_normal, conv_inverse, vector_wide[conv_base]
    )
    grad_two = grad_three + grad_conv_in

    attend_low = grad_two.astype(jnp.bfloat16)
    grad_attend_back = grad_by_columns(place, context, attend_low)
    grad_context = dot_f32(attend_low, attend_back_weight, NT).astype(jnp.bfloat16)
    grad_queries, part_keys, part_values, grad_table = attend_back(
        meta, queries, key_rows, value_rows, table, grad_context, context, levels
    )
    grad_keys = own_sum(place, part_keys).astype(jnp.bfloat16)
    grad_values = own_sum(place, part_values).astype(jnp.bfloat16)
    grad_attend_mix = grad_by_rows(place, attend_normed, [grad_queries, grad_keys, grad_values])
    grad_attend_normed = (
        dot_f32(grad_queries, attend_mix[0], NT)
        + dot_f32(grad_keys, attend_mix[1], NT)
        + dot_f32(grad_values, attend_mix[2], NT)
    )
    grad_attend_in, attend_gain_grad, attend_shift_grad = norm_back(
        grad_attend_normed, attend_normal, attend_inverse, vector_wide[attend_base]
    )
    grad_one = grad_two + grad_attend_in

    grad_one_in, one_weights, one_parts = feed_back(
        place, 0.5 * grad_one, one_kept, up_one, down_one, vector_wide[0]
    )
    grad_rows = grad_one + grad_one_in + (1.0 - valid_flag) * rows_cot
    frames_grad = from_clip(place, grad_rows.astype(jnp.bfloat16), micro)

    def column_sum(rows):
        return jnp.sum(rows.astype(jnp.float32), axis=0)

    vector_part = jnp.concatenate(
        [
            jnp.stack([one_parts[0], one_parts[1]]),
            one_parts[2].reshape(ratio_rows, width),
            jnp.stack(
                [
                    one_parts[3],
                    attend_gain_grad,
                    attend_shift_grad,
                    column_sum(grad_queries),
                    column_sum(grad_values),
                    column_sum(attend_low),
                    conv_gain_grad,
                    conv_shift_grad,
                    deep_gain_grad,
                    deep_shift_grad,
                    two_parts[0],
                    two_parts[1],
                ]
            ),
            two_parts[2].reshape(ratio_rows, width),
            jnp.stack([two_parts[3], final_gain_grad, final_shift_grad]),
            jnp.stack(tap_grads),
        ],
        axis=0,
    )
    everywhere = ("y", "x", "core", "far", "z")
    grad_vectors = lax.psum_scatter(vector_part, everywhere, scatter_dimension=1, tiled=True)
    local_distance = jnp.dot(
        pick_rows.astype(jnp.float32).T, table_grad(grad_table), precision=lax.Precision.HIGHEST
    )
    grad_distance = lax.psum(local_distance, everywhere)
    return (
        frames_out,
        frames_grad,
        one_weights[0],
        one_weights[1],
        grad_attend_mix,
        grad_attend_back,
        grad_point_mix,
        grad_point_back,
        two_weights[0],
        two_weights[1],
        grad_vectors,
        grad_distance,
    )


def solution(mesh):
    dp_count, tensor_count = mesh.shape["dp"], mesh.shape["tensor"]

    def program(*arrays):
        group = 2 * (arrays[0].shape[0] // dp_count)
        parted = Mesh(
            mesh.devices.reshape(dp_count // 4, 2, 2, tensor_count // group, group),
            ("y", "x", "core", "far", "z"),
        )
        dp, tensor = ("y", "x", "core"), TENSOR
        return jax.shard_map(
            body,
            mesh=parted,
            in_specs=(
                P(dp, tensor, None),
                P(dp, tensor, None),
                P(dp),
                P(dp),
                P(),
                P(dp, tensor),
                P(tensor, dp),
                P(None, dp, tensor),
                P(tensor, dp),
                P(None, dp, tensor),
                P(tensor, dp),
                P(dp, tensor),
                P(tensor, dp),
                P(None, dp),
                P(),
            ),
            out_specs=(
                P(dp, tensor, None),
                P(dp, tensor, None),
                P(dp, tensor),
                P(tensor, dp),
                P(None, dp, tensor),
                P(tensor, dp),
                P(None, dp, tensor),
                P(tensor, dp),
                P(dp, tensor),
                P(tensor, dp),
                P(None, dp + tensor),
                P(),
            ),
            check_vma=False,
        )(*arrays)

    return program
```

time: 3140 us -> 1300 us (0.41)
  waiting for transfers between devices: 1950 us -> 339 us
  local copies, waits for them, and re-layouts: 472 us -> 140 us
  starting transfers between devices: 3.46 us -> 314 us
  matrix products: 363 us -> 151 us
  Pallas kernels: 0 us -> 117 us
  blocking collectives: 141 us -> 67.5 us
  other arithmetic: 174 us -> 134 us
    all_gather x28 -> x0, waiting for transfers between devices: 934 us -> none  [the longest x8 376 us: spread(): return lax.all_gather(row_block, 'tensor', axis=0, tiled=True)]
    reduce_scatter x21 -> x0, waiting for transfers between devices: 919 us -> none  [the longest x8 340 us: collect_term(): lax.psum_scatter(term(0, total_rows).astype(jnp.bfloat16), 'tensor', scat...]
    ppermute x0 -> x263, waiting for transfers between devices: none -> 339 us  [the longest x253 327 us: turn(): return lax.ppermute(block, self.names.get(axis, axis), pairs)]
    ppermute x0 -> x263, starting transfers between devices: none -> 314 us  [the longest x253 297 us: turn(): return lax.ppermute(block, self.names.get(axis, axis), pairs)]
    while x525 -> x0, local copies, waits for them, and re-layouts: 255 us -> none
    dot_general x90 -> x46, matrix products: 363 us -> 151 us  [the longest x45 151 us: dot_f32(): lax.dot_general(left_side, right_side, dims, preferred_element_type=jnp.f...]
    reshape x12 -> x2, local copies, waits for them, and re-layouts: 120 us -> 0.02 us  [the longest x1 0.01 us: body(): two_parts[2].reshape(ratio_rows, width)]
    pallas_call x0 -> x10, Pallas kernels: none -> 117 us  [the longest x1 54.7 us: attend_back(): pl.pallas_call(attend_back_kernel, grid_spec=pltpu.PrefetchScalarGridSpec...]
  transfers between devices with their start and end apart: 53 -> 264, of which waited for: 52 -> 79; matrix products, arithmetic and copies ran while one was open for 6% -> 23% of each run, Pallas kernels for 0% -> 6%
where the time goes in v1:
time: 1300 us; the launch traced here: 1290 us
  waiting for transfers between devices  339 us (26%)
  starting transfers between devices  314 us (24%)
  matrix products  151 us (12%)
  local copies, waits for them, and re-layouts  140 us (11%)
  other arithmetic  134 us (10%)
  Pallas kernels  117 us (9%)
  blocking collectives  67.5 us (5%)
  between operations  21.5 us (2%)
    ppermute x253, waiting for transfers between devices, turn(): return lax.ppermute(block, self.names.get(axis, axis), pairs)  327 us
    ppermute x253, starting transfers between devices, turn(): return lax.ppermute(block, self.names.get(axis, axis), pairs)  297 us
    dot_general x45, matrix products, dot_f32(): lax.dot_general(left_side, right_side, dims, preferred_element_type=jnp.f...  151 us
    unnamed x994, local copies, waits for them, and re-layouts  70.3 us
    pallas_call x1, Pallas kernels, attend_back(): pl.pallas_call(attend_back_kernel, grid_spec=pltpu.PrefetchScalarGridSpec...  54.7 us
    psum x1, blocking collectives, body(): grad_distance = lax.psum(local_distance, everywhere)  43.9 us
    pallas_call x1, Pallas kernels, attend(): pl.pallas_call(attend_kernel, grid_spec=pltpu.PrefetchScalarGridSpec(num_...  35.6 us
    convert_element_type x52, other arithmetic, reduce_half(): message = place.turn(added(picked).astype(jnp.bfloat16), axis, step)  27.6 us
  transfers between devices with their start and end apart: 264, of which 79 were waited for; matrix products, arithmetic and copies ran while one was open for 23% of the time, Pallas kernels for 6%

profile of v1, /device:TPU:0, one launch (start us, length us, event | category | flops | bytes accessed | tf_op | source)
XLA Modules:
  0.0 1285.1 jit_solution(15144771974757291698)
XLA Ops:
  61.6 10.1 collective-permute-start.3
  232.4 16.4 %collective-permute-start.102 = (bf16[4,2,64,256]{3,2,1,0:T(8,128)(2,1)}, bf16[4,2,64,256]{3,2,1,0:T(8,128)(2,1)S(1)}, u32[]{:S(2)}, u32[]{:S(2)}) collective-permute-start(bf16[4,2,64,256]{3,2,1,0:T(8,128)(2,1)} %collective-permute-done.98.refs_9_), channel_id=1, source_target_pairs={{0,4},{4,0},{1,5},{5,1},{2,6},{6,2},{3,7},{7,3},{8,12},{12,8},{9,1... | collective-permute-start | bytes 786440 | tf_op jit(solution)/shard_map/ppermute | solution.py:336
  289.5 23.6 %all_gather.3 = bf16[56,1024]{1,0:T(8,128)(2,1)S(1)} all-gather(bf16[56,128]{1,0:T(8,128)(2,1)S(1)} %copy-done.466), channel_id=1, replica_groups=mesh['y'=2,'x'=2,'core'=2,'far'=1,'z'=4] {'y','x','core'}, dimensions={1}, use_global_device_ids=true | all-gather | bytes 129024 | tf_op jit(solution)/shard_map/all_gather | solution.py:668
  408.2 16.8 %multiply_convert_fusion.1 = (bf16[512,4096]{1,0:T(8,128)(2,1)}, f32[512,4096]{1,0:T(8,128)}) fusion(f32[4096]{0:T(1024)S(1)} %bitcast.1237, bf16[512,1024]{1,0:T(8,128)(2,1)S(1)} %fusion.37, bf16[1,1024,4096]{2,1,0:T(8,128)(2,1)S(1)} %assemble.8), kind=kOutput, calls=%fused_computation.88 | convolution fusion | flops 4307550208 | bytes 22036480 | tf_op jit(solution)/shard_map/dot_general | solution.py:25
  496.4 35.6 %attend.1 = (bf16[512,1024]{1,0:T(8,128)(2,1)S(1)}, f32[512,128]{1,0:T(8,128)S(1)}) custom-call(s32[2]{0:T(128)S(1)} %pad_add_fusion.2.meta_ref, bf16[512,1024]{1,0:T(8,128)(2,1)S(1)} %multiply_convert_fusion.6.q_ref, bf16[1024,1024]{1,0:T(8,128)(2,1)S(1)} %bitcast.1030, bf16[1024,1024]{1,0:T(8,128)(2,1)} %bitcast.1050, bf16[256,128]{1,0:T(8,128)(2,1)S(1)} %copy-done.22), custom_call_target="tpu_custom_call" | custom-call | tf_op jit(solution)/shard_map/attend/pallas_call | solution.py:202
  542.7 9.1 fusion.534
  578.6 11.1 convert_reduce_fusion
  589.7 8.7 multiply_reduce_fusion.31
  635.0 20.2 %multiply_convert_fusion.4 = (bf16[512,1024]{1,0:T(8,128)(2,1)S(1)}, f32[512,1024]{1,0:T(8,128)S(1)}) fusion(f32[512,1024]{1,0:T(8,128)S(1)} %copy-done.170, f32[512]{0:T(512)S(1)} %copy-done.415, f32[512,1024]{1,0:T(8,128)S(1)} %copy-done.162, f32[1024]{0:T(1024)S(1)} %bitcast.1150, f32[30,1024]{1,0:T(8,128)S(1)} %collective-permute-done.170, ...), kind=kLoop, calls=%fused_computation.341 | loop fusion | flops 49283072 | bytes 7591936 | tf_op jit(solution)/shard_map/convert_element_type | solution.py:774
  668.8 54.7 %attend_back.1 = (bf16[512,1024]{1,0:T(8,128)(2,1)S(1)}, bf16[1024,1024]{1,0:T(8,128)(2,1)}, bf16[1024,1024]{1,0:T(8,128)(2,1)}, f32[128,256]{1,0:T(8,128)S(1)}) custom-call(s32[2]{0:T(128)S(1)} %pad_add_fusion.2.meta_ref, bf16[512,1024]{1,0:T(8,128)(2,1)S(1)} %multiply_convert_fusion.6.q_ref, bf16[1024,1024]{1,0:T(8,128)(2,1)} %bitcast.1031, ...), custom_call_target="tpu_custom_call" | custom-call | tf_op jit(solution)/shard_map/attend_back/pallas_call | solution.py:231
  746.5 43.9 %psum.7 = f32[73,64]{0,1:T(8,128)} all-reduce(f32[73,64]{0,1:T(8,128)S(1)} %fusion.489), channel_id=1, replica_groups=mesh['y'=2,'x'=2,'core'=2,'far'=1,'z'=4] {'y','x','core','far','z'}, use_global_device_ids=true, to_apply=%region_75.76 | all-reduce | flops 4672 | bytes 37376 | tf_op jit(solution)/shard_map/psum | solution.py:842
  810.8 10.3 convert_reduce_fusion.1
  936.3 9.8 collective-permute-done.167
  948.7 14.3 %collective-permute-start.234 = (bf16[1,128,128]{2,1,0:T(8,128)(2,1)S(1)}, bf16[1,128,128]{2,1,0:T(8,128)(2,1)S(1)}, u32[]{:S(2)}, u32[]{:S(2)}) collective-permute-start(bf16[1,128,128]{2,1,0:T(8,128)(2,1)S(1)} %get-tuple-element.195), channel_id=1, source_target_pairs={{0,2},{1,3},{2,0},{3,1},{4,6},{5,7},{6,4},{7,5},{8,10},{9,11},{10,... | collective-permute-start | bytes 98312 | tf_op jit(solution)/shard_map/ppermute | solution.py:336
  963.2 10.3 collective-permute-start.174
  987.0 10.3 collective-permute-done.225
  1038.3 9.6 collective-permute-done.198
  1051.8 9.5 collective-permute-done.247
  1062.4 11.6 collective-permute-done.242
  1138.4 12.5 collective-permute-done.192
  1153.8 14.8 %collective-permute-done.258 = bf16[4,512,256]{2,1,0:T(8,128)(2,1)S(1)} collective-permute-done((bf16[4,512,256]{2,1,0:T(8,128)(2,1)S(1)}, bf16[4,512,256]{2,1,0:T(8,128)(2,1)S(1)}, u32[]{:S(2)}, u32[]{:S(2)}) %collective-permute-start.258) | collective-permute-done | bytes 1048608 | tf_op jit(solution)/shard_map/ppermute | solution.py:336
  1171.7 14.8 %collective-permute-done.253 = bf16[4,512,256]{2,1,0:T(8,128)(2,1)S(1)} collective-permute-done((bf16[4,512,256]{2,1,0:T(8,128)(2,1)S(1)}, bf16[4,512,256]{2,1,0:T(8,128)(2,1)S(1)}, u32[]{:S(2)}, u32[]{:S(2)}) %collective-permute-start.253) | collective-permute-done | bytes 1048608 | tf_op jit(solution)/shard_map/ppermute | solution.py:336
  1188.3 9.4 collective-permute-done.182
  1199.8 9.2 collective-permute-done.193
  (1786 shorter events, 867.1 us)
Async XLA Ops:
  7.2 1270.6 %reduce-scatter.4.cloned.1.call-start = ((), (), s32[]{:S(2)}) async-start(), calls=%async_computation.1 | async-start | bytes 540672
  277.2 35.9 %collective-permute-start.29 = (bf16[4,512,128]{2,1,0:T(8,128)(2,1)S(1)}, bf16[4,512,128]{2,1,0:T(8,128)(2,1)S(1)}, u32[]{:S(2)}, u32[]{:S(2)}) collective-permute-start(bf16[4,512,128]{2,1,0:T(8,128)(2,1)S(1)} %pad_maximum_fusion.11.refs_0_), channel_id=1, source_target_pairs={{0,4},{4,0},{1,5},{5,1},{2,6},{6,2},{3,7},{7,3},{8,12},{12,8},{9,1... | collective-permute-start | bytes 1572872 | tf_op jit(solution)/shard_map/ppermute | solution.py:336
  279.6 36.2 %collective-permute-start.36 = (bf16[4,512,128]{2,1,0:T(8,128)(2,1)S(1)}, bf16[4,512,128]{2,1,0:T(8,128)(2,1)S(1)}, u32[]{:S(2)}, u32[]{:S(2)}) collective-permute-start(bf16[4,512,128]{2,1,0:T(8,128)(2,1)S(1)} %pad_maximum_fusion.12.refs_8_), channel_id=1, source_target_pairs={{0,16},{16,0},{1,17},{17,1},{2,18},{18,2},{3,19},{19,3},{4,20},{20... | collective-permute-start | bytes 1572872 | tf_op jit(solution)/shard_map/ppermute | solution.py:336
  281.0 35.0 %collective-permute-start.37 = (bf16[4,512,128]{2,1,0:T(8,128)(2,1)S(1)}, bf16[4,512,128]{2,1,0:T(8,128)(2,1)S(1)}, u32[]{:S(2)}, u32[]{:S(2)}) collective-permute-start(bf16[4,512,128]{2,1,0:T(8,128)(2,1)S(1)} %pad_maximum_fusion.12.refs_8_), channel_id=1, source_target_pairs={{0,8},{8,0},{1,9},{9,1},{2,10},{10,2},{3,11},{11,3},{4,12},{12,4},... | collective-permute-start | bytes 1572872 | tf_op jit(solution)/shard_map/ppermute | solution.py:336
  615.0 402.4 %collective-permute-start.241 = (bf16[1,512,4096]{2,1,0:T(8,128)(2,1)}, bf16[1,512,4096]{2,1,0:T(8,128)(2,1)}, u32[]{:S(2)}, u32[]{:S(2)}) collective-permute-start(bf16[1,512,4096]{2,1,0:T(8,128)(2,1)} %fusion.23), channel_id=1, source_target_pairs={{0,4},{4,0},{1,5},{5,1},{2,6},{6,2},{3,7},{7,3},{8,12},{12,8},{9,1... | collective-permute-start | bytes 12582920 | tf_op jit(solution)/shard_map/ppermute | solution.py:336
  726.0 71.9 %collective-permute-start.172 = (bf16[512,1024]{1,0:T(8,128)(2,1)}, bf16[512,1024]{1,0:T(8,128)(2,1)}, u32[]{:S(2)}, u32[]{:S(2)}) collective-permute-start(bf16[512,1024]{1,0:T(8,128)(2,1)} %dynamic-slice_bitcast_fusion), channel_id=1, source_target_pairs={{0,4},{4,0},{1,5},{5,1},{2,6},{6,2},{3,7},{7,3},{8,12},{12,8},{9,1... | collective-permute-start | bytes 3145736 | tf_op jit(solution)/shard_map/ppermute | solution.py:336
  727.2 64.1 %collective-permute-start.171 = (bf16[512,1024]{1,0:T(8,128)(2,1)}, bf16[512,1024]{1,0:T(8,128)(2,1)}, u32[]{:S(2)}, u32[]{:S(2)}) collective-permute-start(bf16[512,1024]{1,0:T(8,128)(2,1)} %dynamic-slice_bitcast_fusion.1), channel_id=1, source_target_pairs={{0,4},{4,0},{1,5},{5,1},{2,6},{6,2},{3,7},{7,3},{8,12},{12,8},{9,1... | collective-permute-start | bytes 3145736 | tf_op jit(solution)/shard_map/ppermute | solution.py:336
  729.3 117.6 %collective-permute-start.208 = (bf16[1024,512]{1,0:T(8,128)(2,1)}, bf16[1024,512]{1,0:T(8,128)(2,1)}, u32[]{:S(2)}, u32[]{:S(2)}) collective-permute-start(bf16[1024,512]{1,0:T(8,128)(2,1)} %convolution_convert_fusion.15), channel_id=1, source_target_pairs={{0,4},{4,0},{1,5},{5,1},{2,6},{6,2},{3,7},{7,3},{8,12},{12,8},{9,1... | collective-permute-start | bytes 3145736 | tf_op jit(solution)/shard_map/ppermute | solution.py:336
  732.5 201.2 %collective-permute-start.219 = (bf16[2,512,1024]{2,1,0:T(8,128)(2,1)}, bf16[2,512,1024]{2,1,0:T(8,128)(2,1)}, u32[]{:S(2)}, u32[]{:S(2)}) collective-permute-start(bf16[2,512,1024]{2,1,0:T(8,128)(2,1)} %pad_maximum_fusion.4), channel_id=1, source_target_pairs={{0,4},{4,0},{1,5},{5,1},{2,6},{6,2},{3,7},{7,3},{8,12},{12,8},{9,1... | collective-permute-start | bytes 6291464 | tf_op jit(solution)/shard_map/ppermute | solution.py:336
  791.2 67.6 %collective-permute-start.230 = (bf16[1024,512]{1,0:T(8,128)(2,1)}, bf16[1024,512]{1,0:T(8,128)(2,1)}, u32[]{:S(2)}, u32[]{:S(2)}) collective-permute-start(bf16[1024,512]{1,0:T(8,128)(2,1)} %convolution_convert_fusion.9), channel_id=1, source_target_pairs={{0,4},{4,0},{1,5},{5,1},{2,6},{6,2},{3,7},{7,3},{8,12},{12,8},{9,1... | collective-permute-start | bytes 3145736 | tf_op jit(solution)/shard_map/ppermute | solution.py:336
  849.9 42.1 %collective-permute-start.214 = (bf16[4,128,256]{2,1,0:T(8,128)(2,1)}, bf16[4,128,256]{2,1,0:T(8,128)(2,1)}, u32[]{:S(2)}, u32[]{:S(2)}) collective-permute-start(bf16[4,128,256]{2,1,0:T(8,128)(2,1)} %add_convert_fusion.23), channel_id=1, source_target_pairs={{0,8},{8,0},{1,9},{9,1},{2,10},{10,2},{3,11},{11,3},{4,12},{12,4},... | collective-permute-start | bytes 786440 | tf_op jit(solution)/shard_map/ppermute | solution.py:336
  853.0 37.8 %collective-permute-start.209 = (bf16[4,128,256]{2,1,0:T(8,128)(2,1)}, bf16[4,128,256]{2,1,0:T(8,128)(2,1)}, u32[]{:S(2)}, u32[]{:S(2)}) collective-permute-start(bf16[4,128,256]{2,1,0:T(8,128)(2,1)} %fusion.313), channel_id=1, source_target_pairs={{0,16},{16,0},{1,17},{17,1},{2,18},{18,2},{3,19},{19,3},{4,20},{20... | collective-permute-start | bytes 786440 | tf_op jit(solution)/shard_map/ppermute | solution.py:336
  892.0 123.4 %collective-permute-start.197 = (bf16[3,512,1024]{2,1,0:T(8,128)(2,1)S(1)}, bf16[3,512,1024]{2,1,0:T(8,128)(2,1)S(1)}, u32[]{:S(2)}, u32[]{:S(2)}) collective-permute-start(bf16[3,512,1024]{2,1,0:T(8,128)(2,1)S(1)} %pad_maximum_fusion.1), channel_id=1, source_target_pairs={{0,4},{4,0},{1,5},{5,1},{2,6},{6,2},{3,7},{7,3},{8,12},{12,8},{9,1... | collective-permute-start | bytes 9437192 | tf_op jit(solution)/shard_map/ppermute | solution.py:336
  933.7 51.0 %collective-permute-start.173 = (bf16[256,1024]{1,0:T(8,128)(2,1)S(1)}, bf16[256,1024]{1,0:T(8,128)(2,1)S(1)}, u32[]{:S(2)}, u32[]{:S(2)}) collective-permute-start(bf16[256,1024]{1,0:T(8,128)(2,1)S(1)} %copy-done.280), channel_id=1, source_target_pairs={{0,0},{1,1},{4,2},{5,3},{2,4},{3,5},{6,6},{7,7},{8,8},{9,9},{12,10... | collective-permute-start | bytes 1572872 | tf_op jit(solution)/shard_map/ppermute | solution.py:579
  1010.4 70.0 %collective-permute-start.175 = (bf16[1,512,4096]{2,1,0:T(8,128)(2,1)S(1)}, bf16[1,512,4096]{2,1,0:T(8,128)(2,1)S(1)}, u32[]{:S(2)}, u32[]{:S(2)}) collective-permute-start(bf16[1,512,4096]{2,1,0:T(8,128)(2,1)S(1)} %fusion.22), channel_id=1, source_target_pairs={{0,4},{4,0},{1,5},{5,1},{2,6},{6,2},{3,7},{7,3},{8,12},{12,8},{9,1... | collective-permute-start | bytes 12582920 | tf_op jit(solution)/shard_map/ppermute | solution.py:336
  1013.5 62.1 %collective-permute-start.186 = (bf16[4096,512]{1,0:T(8,128)(2,1)}, bf16[4096,512]{1,0:T(8,128)(2,1)S(1)}, u32[]{:S(2)}, u32[]{:S(2)}) collective-permute-start(bf16[4096,512]{1,0:T(8,128)(2,1)} %convolution_convert_fusion.4), channel_id=1, source_target_pairs={{0,4},{4,0},{1,5},{5,1},{2,6},{6,2},{3,7},{7,3},{8,12},{12,8},{9,1... | collective-permute-start | bytes 12582920 | tf_op jit(solution)/shard_map/ppermute | solution.py:336
  1021.7 60.8 %collective-permute-start.252 = (bf16[4096,512]{1,0:T(8,128)(2,1)}, bf16[4096,512]{1,0:T(8,128)(2,1)}, u32[]{:S(2)}, u32[]{:S(2)}) collective-permute-start(bf16[4096,512]{1,0:T(8,128)(2,1)} %convolution_convert_fusion), channel_id=1, source_target_pairs={{0,4},{4,0},{1,5},{5,1},{2,6},{6,2},{3,7},{7,3},{8,12},{12,8},{9,1... | collective-permute-start | bytes 12582920 | tf_op jit(solution)/shard_map/ppermute | solution.py:336
  1097.8 39.5 %collective-permute-start.181 = (bf16[1,2,1,64,4096]{4,3,2,1,0:T(8,128)(2,1)S(1)}, bf16[1,2,1,64,4096]{4,3,2,1,0:T(8,128)(2,1)S(1)}, u32[]{:S(2)}, u32[]{:S(2)}) collective-permute-start(bf16[1,2,1,64,4096]{4,3,2,1,0:T(8,128)(2,1)S(1)} %fusion.192), channel_id=1, source_target_pairs={{0,8},{8,0},{1,9},{9,1},{2,10},{10,2},{3,11},{11,3},{4,12},{12,4},... | collective-permute-start | bytes 3145736 | tf_op jit(solution)/shard_map/ppermute | solution.py:336
  1133.6 37.6 %collective-permute-start.187 = (bf16[4,512,256]{2,1,0:T(8,128)(2,1)S(1)}, bf16[4,512,256]{2,1,0:T(8,128)(2,1)S(1)}, u32[]{:S(2)}, u32[]{:S(2)}) collective-permute-start(bf16[4,512,256]{2,1,0:T(8,128)(2,1)S(1)} %fusion.193), channel_id=1, source_target_pairs={{0,16},{16,0},{1,17},{17,1},{2,18},{18,2},{3,19},{19,3},{4,20},{20... | collective-permute-start | bytes 3145736 | tf_op jit(solution)/shard_map/ppermute | solution.py:336
  1137.4 49.2 %collective-permute-start.253 = (bf16[4,512,256]{2,1,0:T(8,128)(2,1)S(1)}, bf16[4,512,256]{2,1,0:T(8,128)(2,1)S(1)}, u32[]{:S(2)}, u32[]{:S(2)}) collective-permute-start(bf16[4,512,256]{2,1,0:T(8,128)(2,1)S(1)} %fusion.196), channel_id=1, source_target_pairs={{0,16},{16,0},{1,17},{17,1},{2,18},{18,2},{3,19},{19,3},{4,20},{20... | collective-permute-start | bytes 3145736 | tf_op jit(solution)/shard_map/ppermute | solution.py:336
  1150.9 46.8 %collective-permute-start.182 = (bf16[1,1,1,64,4096]{4,3,2,1,0:T(8,128)(2,1)S(1)}, bf16[1,1,1,64,4096]{4,3,2,1,0:T(8,128)(2,1)S(1)}, u32[]{:S(2)}, u32[]{:S(2)}) collective-permute-start(bf16[1,1,1,64,4096]{4,3,2,1,0:T(8,128)(2,1)S(1)} %fusion.202), channel_id=1, source_target_pairs={{0,16},{16,0},{1,17},{17,1},{2,18},{18,2},{3,19},{19,3},{4,20},{20... | collective-permute-start | bytes 1572872 | tf_op jit(solution)/shard_map/ppermute | solution.py:336
  1151.5 57.5 %collective-permute-start.193 = (bf16[4,512,128]{2,1,0:T(8,128)(2,1)S(1)}, bf16[4,512,128]{2,1,0:T(8,128)(2,1)S(1)}, u32[]{:S(2)}, u32[]{:S(2)}) collective-permute-start(bf16[4,512,128]{2,1,0:T(8,128)(2,1)S(1)} %add_convert_fusion.20), channel_id=1, source_target_pairs={{0,16},{16,0},{1,17},{17,1},{2,18},{18,2},{3,19},{19,3},{4,20},{20... | collective-permute-start | bytes 1572872 | tf_op jit(solution)/shard_map/ppermute | solution.py:336
  1168.6 48.0 %collective-permute-start.177 = (bf16[1,1,1,64,4096]{4,3,2,1,0:T(8,128)(2,1)S(1)}, bf16[1,1,1,64,4096]{4,3,2,1,0:T(8,128)(2,1)S(1)}, u32[]{:S(2)}, u32[]{:S(2)}) collective-permute-start(bf16[1,1,1,64,4096]{4,3,2,1,0:T(8,128)(2,1)S(1)} %fusion.203), channel_id=1, source_target_pairs={{0,8},{8,0},{1,9},{9,1},{2,10},{10,2},{3,11},{11,3},{4,12},{12,4},... | collective-permute-start | bytes 1572872 | tf_op jit(solution)/shard_map/ppermute | solution.py:336
  1171.2 43.5 %collective-permute-start.259 = (bf16[4,512,128]{2,1,0:T(8,128)(2,1)S(1)}, bf16[4,512,128]{2,1,0:T(8,128)(2,1)S(1)}, u32[]{:S(2)}, u32[]{:S(2)}) collective-permute-start(bf16[4,512,128]{2,1,0:T(8,128)(2,1)S(1)} %add_convert_fusion.17), channel_id=1, source_target_pairs={{0,16},{16,0},{1,17},{17,1},{2,18},{18,2},{3,19},{19,3},{4,20},{20... | collective-permute-start | bytes 1572872 | tf_op jit(solution)/shard_map/ppermute | solution.py:336
  (736 other events, 8884.8 us)
Sparse Core Ops, SparseCore 0:
  874.2 140.0 reduce-scatter.3

commit v2 on v1

--- a/solution.py
+++ b/solution.py
@@ -311,18 +311,30 @@
     return (grad_in, jnp.sum(grad_out * normal, axis=0), jnp.sum(grad_out, axis=0))
 
 
+def fence(*values):
+    return lax.optimization_barrier(values)
+
+
 TENSOR = ("far", "z")
 
 
 class Place:
     def __init__(self):
-        self.count = {axis: lax.axis_size(axis) for axis in ("y", "x", "core", "far", "z")}
-        self.index = {axis: lax.axis_index(axis) for axis in ("y", "x", "core", "far", "z")}
-        self.count["t"] = self.count["far"] * self.count["z"]
-        self.index["t"] = self.index["far"] * self.count["z"] + self.index["z"]
-        self.count["seq"] = self.count["far"] * 2
-        self.index["seq"] = self.index["far"] * 2 + self.index["core"]
+        axes = ("y", "x", "core", "far", "z")
+        self.count = {axis: lax.axis_size(axis) for axis in axes}
+        self.index = {axis: lax.axis_index(axis) for axis in axes}
+        count, index = self.count, self.index
+        count["t"] = count["far"] * count["z"]
+        index["t"] = index["far"] * count["z"] + index["z"]
+        count["seq"] = count["far"] * 2
+        index["seq"] = index["far"] * 2 + index["core"]
+        count["a"], count["b"] = count["x"], count["y"]
+        self.mixed = count["x"] == count["y"]
+        self.swapped = (index["core"] == 1) if self.mixed else jnp.zeros((), bool)
+        index["a"] = jnp.where(self.swapped, index["y"], index["x"])
+        index["b"] = jnp.where(self.swapped, index["x"], index["y"])
         self.names = {"t": TENSOR, "seq": ("core", "far")}
+        self.dp_count = count["y"] * count["x"] * 2
 
     def seq_pair(self, start, end):
         far = self.count["far"]
@@ -333,189 +345,240 @@
         pairs = [(start, (start + step) % size) for start in range(size)]
         if axis == "seq":
             pairs = [self.seq_pair(*pair) for pair in pairs]
+        if axis in ("a", "b"):
+            y_count, x_count = self.count["y"], self.count["x"]
+            pairs = []
+            for y in range(y_count):
+                for x in range(x_count):
+                    for core in range(2):
+                        along_x = (axis == "a") != (self.mixed and core == 1)
+                        new_y = y if along_x else (y + step) % y_count
+                        new_x = (x + step) % x_count if along_x else x
+                        pairs.append(
+                            ((y * x_count + x) * 2 + core, (new_y * x_count + new_x) * 2 + core)
+                        )
+            return lax.ppermute(block, ("y", "x", "core"), pairs)
         return lax.ppermute(block, self.names.get(axis, axis), pairs)
 
     def after(self, axis, step):
         return lax.rem(self.index[axis] + step, self.count[axis])
 
-
-def steps(place, axis):
-    return range(1, place.count[axis])
-
-
-def halves_of(shard, by_rows):
-    row_dim = 1 if by_rows else 0
-    half = shard.shape[row_dim] // 2
-    return [lax.slice_in_dim(shard, number * half, (number + 1) * half, axis=row_dim) for number in range(2)]
-
-
-def gather_half(place, block, order):
-    stack = jnp.stack([block] + [place.turn(block, "t", step) for step in steps(place, "t")])
-    pieces = {(0, 0, 0): stack}
-    for axis in order:
-        where = ("y", "x", "core").index(axis)
-        for key, piece in list(pieces.items()):
-            for step in steps(place, axis):
-                new_key = key[:where] + (step,) + key[where + 1 :]
-                pieces[new_key] = place.turn(piece, axis, step)
-    return pieces
-
-
-ORDERS = (("x", "y", "core"), ("y", "x", "core"))
-
-
-def assemble(place, halves, by_rows):
-    keys = [(number, key) for number, pieces in enumerate(halves) for key in pieces]
-    arrays = [halves[number][key] for number, key in keys]
-    counts = place.count
-    tensor_count = counts["t"]
-    dp_count = counts["y"] * counts["x"] * counts["core"]
-    dtype = arrays[0].dtype
-    if by_rows:
-        _, depth, half_rows, columns = arrays[0].shape
-        shard_rows = half_rows * len(halves)
-        out_shape = (depth, shard_rows * dp_count, columns * tensor_count)
-    else:
-        _, half_rows, columns = arrays[0].shape
-        shard_rows = half_rows * len(halves)
-        aligned = columns % LANES == 0
-        if aligned:
-            out_shape = (shard_rows * tensor_count, columns * dp_count)
+    def block(self, a_index, b_index):
+        x_count = self.count["x"]
+        return jnp.where(self.swapped, a_index * x_count + b_index, b_index * x_count + a_index)
+
+    def steps(self, axis):
+        return range(1, self.count[axis])
+
+
+def packed(shard):
+    rows, columns = shard.shape
+    blocks = shard.reshape(rows // columns, columns, columns)
+    return blocks.transpose(1, 0, 2).reshape(columns, rows)
+
+
+def unpacked(block):
+    columns, rows = block.shape
+    blocks = block.reshape(columns, rows // columns, columns)
+    return blocks.transpose(1, 0, 2).reshape(rows, columns)
+
+
+def gather_t(place, shard):
+    return jnp.stack([shard] + [place.turn(shard, "t", step) for step in place.steps("t")])
+
+
+def gather_a(place, stack):
+    return jnp.concatenate([stack] + [place.turn(stack, "a", step) for step in place.steps("a")])
+
+
+def gather_b(place, stack):
+    return [stack] + [place.turn(stack, "b", step) for step in place.steps("b")]
+
+
+def gather_core(place, stacks):
+    return stacks + [place.turn(stack, "core", 1) for stack in stacks]
+
+
+def assemble(place, stacks, targets):
+    counts, dp_count, t_count = place.count, place.dp_count, place.count["t"]
+    dtype = stacks[0].dtype
+    shard_shape = stacks[0].shape[1:]
+    rows, columns = shard_shape[-2:]
+    shapes, copy_counts = [], 0
+    for target in targets:
+        if target[0] == "rows":
+            shapes.append((target[2], target[3] * dp_count, columns * t_count))
+            copy_counts += dp_count * t_count
+        elif target[0] == "columns":
+            aligned = columns % LANES == 0
+            shape = (rows * t_count, columns * dp_count)
+            shapes.append(shape if aligned else (dp_count, rows * t_count, columns))
+            copy_counts += dp_count * t_count
+        elif target[0] == "packed":
+            aligned = rows % LANES == 0
+            shape = (columns * t_count, rows * dp_count)
+            shapes.append(shape if aligned else (dp_count, t_count, rows, columns))
+            copy_counts += dp_count * t_count * (columns // rows if aligned else 1)
         else:
-            out_shape = (dp_count, shard_rows * tensor_count, columns)
+            shapes.append((dp_count, target[2], columns))
+            copy_counts += dp_count
 
     def kernel(meta_ref, *refs):
-        piece_refs, out_ref, sem = refs[: len(keys)], refs[len(keys)], refs[len(keys) + 1]
+        stack_refs = refs[: len(stacks)]
+        out_refs = refs[len(stacks) : len(stacks) + len(targets)]
+        sem = refs[-1]
         copies = []
-        for (number, key), piece_ref in zip(keys, piece_refs):
-            spot = [
-                lax.rem(meta_ref[i] - key[i] + counts[axis], counts[axis])
-                for i, axis in enumerate(("y", "x", "core"))
-            ]
-            dp_spot = (spot[0] * counts["x"] + spot[1]) * counts["core"] + spot[2]
-            for step in range(tensor_count):
-                t_spot = lax.rem(meta_ref[3] - step + tensor_count, tensor_count)
-                if by_rows:
-                    rows = pl.ds(
-                        pl.multiple_of(dp_spot * shard_rows + number * half_rows, half_rows), half_rows
-                    )
-                    target = out_ref.at[:, rows, pl.ds(pl.multiple_of(t_spot * columns, columns), columns)]
-                else:
-                    rows = pl.ds(
-                        pl.multiple_of(t_spot * shard_rows + number * half_rows, half_rows), half_rows
-                    )
-                    if aligned:
-                        target = out_ref.at[rows, pl.ds(pl.multiple_of(dp_spot * columns, columns), columns)]
-                    else:
-                        target = out_ref.at[dp_spot, rows, :]
-                copy = pltpu.make_async_copy(piece_ref.at[step], target, sem.at[len(copies)])
-                copy.start()
-                copies.append(copy)
+
+        def send(source, target):
+            copy = pltpu.make_async_copy(source, target, sem.at[len(copies)])
+            copy.start()
+            copies.append(copy)
+
+        b_count = counts["b"]
+        for number, stack_ref in enumerate(stack_refs):
+            other, b_step = number // b_count, number % b_count
+            core = lax.rem(meta_ref[2] + other, 2)
+            for a_step in range(counts["a"]):
+                y_spot = lax.rem(meta_ref[0] - b_step + counts["y"], counts["y"])
+                x_spot = lax.rem(meta_ref[1] - a_step + counts["x"], counts["x"])
+                if place.mixed:
+                    y_other = lax.rem(meta_ref[0] - a_step + counts["y"], counts["y"])
+                    x_other = lax.rem(meta_ref[1] - b_step + counts["x"], counts["x"])
+                    y_spot = jnp.where(core == 1, y_other, y_spot)
+                    x_spot = jnp.where(core == 1, x_other, x_spot)
+                dp_spot = (y_spot * counts["x"] + x_spot) * 2 + core
+                for t_step in range(t_count):
+                    t_spot = lax.rem(meta_ref[3] - t_step + t_count, t_count)
+                    shard_ref = stack_ref.at[a_step * t_count + t_step]
+                    for target, out_ref in zip(targets, out_refs):
+                        t_columns = pl.ds(pl.multiple_of(t_spot * columns, columns), columns)
+                        if target[0] == "rows":
+                            first, depth, count = target[1:]
+                            source = shard_ref.at[first : first + depth, 0:count, :]
+                            here = pl.ds(pl.multiple_of(dp_spot * count, count), count)
+                            send(source, out_ref.at[:, here, t_columns])
+                        elif target[0] == "columns":
+                            here = pl.ds(pl.multiple_of(t_spot * rows, rows), rows)
+                            if columns % LANES == 0:
+                                there = pl.ds(pl.multiple_of(dp_spot * columns, columns), columns)
+                                send(shard_ref, out_ref.at[here, there])
+                            else:
+                                send(shard_ref, out_ref.at[dp_spot, here, :])
+                        elif target[0] == "packed":
+                            if rows % LANES == 0:
+                                there = pl.ds(pl.multiple_of(dp_spot * rows, rows), rows)
+                                for part in range(columns // rows):
+                                    here = pl.ds(
+                                        pl.multiple_of(t_spot * columns + part * rows, rows), rows
+                                    )
+                                    send(
+                                        shard_ref.at[target[1], :, part * rows : (part + 1) * rows],
+                                        out_ref.at[here, there],
+                                    )
+                            else:
+                                send(shard_ref.at[target[1]], out_ref.at[dp_spot, t_spot])
+                        elif t_step == 0:
+                            first_row, count = target[1:]
+                            send(shard_ref.at[0, first_row : first_row + count, :], out_ref.at[dp_spot])
         for copy in copies:
             copy.wait()
 
     meta = jnp.stack([place.index[axis] for axis in ("y", "x", "core", "t")]).astype(jnp.int32)
-    whole = pl.pallas_call(
+    results = pl.pallas_call(
         kernel,
         grid_spec=pltpu.PrefetchScalarGridSpec(
             num_scalar_prefetch=1,
             grid=(),
-            in_specs=[pl.BlockSpec(memory_space=pl.ANY)] * len(keys),
-            out_specs=pl.BlockSpec(memory_space=pltpu.VMEM),
-            scratch_shapes=[pltpu.SemaphoreType.DMA((len(keys) * tensor_count,))],
+            in_specs=[pl.BlockSpec(memory_space=pl.ANY)] * len(stacks),
+            out_specs=[pl.BlockSpec(memory_space=pltpu.VMEM)] * len(targets),
+            scratch_shapes=[pltpu.SemaphoreType.DMA((copy_counts,))],
         ),
-        out_shape=jax.ShapeDtypeStruct(out_shape, dtype),
+        out_shape=[jax.ShapeDtypeStruct(shape, dtype) for shape in shapes],
         compiler_params=pltpu.CompilerParams(vmem_limit_bytes=20 * 2**20),
         name="assemble",
-    )(meta, *arrays)
-    if not by_rows and not aligned:
-        whole = whole.transpose(1, 0, 2).reshape(shard_rows * tensor_count, columns * dp_count)
-    return whole
-
-
-def fetch(place, shard, by_rows):
-    halves = [
-        gather_half(place, half, order) for half, order in zip(halves_of(shard, by_rows), ORDERS)
-    ]
-    return assemble(place, halves, by_rows)
-
-
-class Part:
-    def __init__(self, array, by_rows, spans):
-        self.array, self.by_rows, self.spans = array, by_rows, spans
-
-    def pick(self, axis, index):
-        spans = dict(self.spans)
-        count = spans[axis]
-        if count == 1:
-            return self
-        spans[axis] = 1
-        array = self.array
-        if self.by_rows:
-            if axis == "t":
-                width = array.shape[-1] // count
-                array = lax.dynamic_slice_in_dim(array, index * width, width, axis=4)
-            else:
-                array = lax.dynamic_slice_in_dim(array, index, 1, axis={"y": 1, "x": 2}[axis])
-        elif axis == "t":
-            array = lax.dynamic_slice_in_dim(array, index, 1, axis=0)
-        else:
-            width = array.shape[-1] // (self.spans["y"] * self.spans["x"])
-            if axis == "y":
-                width = width * self.spans["x"]
-                array = lax.dynamic_slice_in_dim(array, index * width, width, axis=2)
-            else:
-                array = jnp.concatenate(
-                    [
-                        lax.dynamic_slice_in_dim(array, (row * count + index) * width, width, axis=2)
-                        for row in range(self.spans["y"])
-                    ],
-                    axis=2,
-                )
-        return Part(array, self.by_rows, spans)
-
-
-def added(parts):
-    total = parts[0].array.astype(jnp.float32)
-    for part in parts[1:]:
-        total = total + part.array.astype(jnp.float32)
+    )(meta, *stacks)
+    finished = []
+    for target, whole in zip(targets, results):
+        if target[0] == "columns" and columns % LANES:
+            whole = whole.transpose(1, 0, 2).reshape(rows * t_count, columns * dp_count)
+        if target[0] == "packed" and rows % LANES:
+            whole = whole.reshape(dp_count, t_count, rows, columns // rows, rows)
+            whole = whole.transpose(1, 3, 2, 0, 4).reshape(columns * t_count, rows * dp_count)
+        finished.append(whole)
+    return finished
+
+
+def pick_blocks(array, numbers, count):
+    if array.ndim == 4:
+        return jnp.concatenate([lax.dynamic_slice_in_dim(array, one, 1, axis=1) for one in numbers], axis=1)
+    width = array.shape[1] // count
+    return jnp.concatenate(
+        [lax.dynamic_slice_in_dim(array, one * width, width, axis=1) for one in numbers], axis=1
+    )
+
+
+def pick_t(array, number, count):
+    axis = 3 if array.ndim == 4 else 0
+    width = array.shape[axis] // count
+    return lax.dynamic_slice_in_dim(array, number * width, width, axis=axis)
+
+
+def added(arrays):
+    total = arrays[0].astype(jnp.float32)
+    for array in arrays[1:]:
+        total = total + array.astype(jnp.float32)
     return total
 
 
-def reduce_half(place, parts, order):
-    for axis in order:
-        arrived = []
-        for step in steps(place, axis):
-            picked = [part.pick(axis, place.after(axis, step)) for part in parts]
-            message = place.turn(added(picked).astype(jnp.bfloat16), axis, step)
-            arrived.append(Part(message, picked[0].by_rows, picked[0].spans))
-        parts = [part.pick(axis, place.index[axis]) for part in parts] + arrived
-    return added(parts)
-
-
-BACK_ORDERS = (("y", "x", "t"), ("x", "y", "t"))
-
-
-def reduce_weight(place, product, by_rows, depth):
-    counts = place.count
-    spans = {"y": counts["y"], "x": counts["x"], "t": counts["t"]}
+def reduce_core(place, product):
     other = place.turn(product(1 - place.index["core"]), "core", 1)
-    mine = product(place.index["core"])
-    results = []
-    for number, order in enumerate(BACK_ORDERS):
-        parts = []
-        for array in (mine, other):
-            if by_rows:
-                block = array.reshape(
-                    depth, counts["y"], counts["x"], 2, -1, array.shape[-1]
-                )[:, :, :, number]
-            else:
-                block = array.reshape(counts["t"], 2, -1, array.shape[-1])[:, number]
-            parts.append(Part(block, by_rows, spans))
-        results.append(reduce_half(place, parts, order))
-    if by_rows:
-        return jnp.concatenate([one[:, 0, 0] for one in results], axis=1)
-    return jnp.concatenate([one[0] for one in results], axis=0)
+    return [product(place.index["core"]), other]
+
+
+def reduce_b(place, parts):
+    blocks = place.count["a"] * place.count["b"]
+    arrived = []
+    for step in place.steps("b"):
+        numbers = [
+            place.block(number, place.after("b", step)) for number in range(place.count["a"])
+        ]
+        message = added([pick_blocks(part, numbers, blocks) for part in parts])
+        arrived.append(place.turn(message.astype(parts[0].dtype), "b", step))
+    return (parts, arrived)
+
+
+def reduce_a(place, state):
+    parts, from_b = state
+    blocks, a_count = place.count["a"] * place.count["b"], place.count["a"]
+    arrived = []
+    for step in place.steps("a"):
+        there = place.after("a", step)
+        number = place.block(there, place.index["b"])
+        message = added(
+            [pick_blocks(part, [number], blocks) for part in parts]
+            + [pick_blocks(part, [there], a_count) for part in from_b]
+        )
+        arrived.append(place.turn(message.astype(parts[0].dtype), "a", step))
+    return (parts, from_b, arrived)
+
+
+def reduce_t(place, state):
+    parts, from_b, from_a = state
+    blocks, a_count, t_count = place.count["a"] * place.count["b"], place.count["a"], place.count["t"]
+    number = place.block(place.index["a"], place.index["b"])
+    mine = [pick_blocks(part, [number], blocks) for part in parts]
+    mine += [pick_blocks(part, [place.index["a"]], a_count) for part in from_b]
+    mine += from_a
+    arrived = []
+    for step in place.steps("t"):
+        message = added([pick_t(part, place.after("t", step), t_count) for part in mine])
+        arrived.append(place.turn(message.astype(parts[0].dtype), "t", step))
+    return ([pick_t(part, place.index["t"], t_count) for part in mine], arrived)
+
+
+def reduce_end(state):
+    total = added(state[0] + state[1])
+    return total[:, 0] if total.ndim == 4 else total
 
 
 def core_columns(place, rows_in, core):
@@ -530,19 +593,46 @@
     )
 
 
-def grad_by_rows(place, inputs, grads):
+def term_by_rows(place, inputs, grads, extra=None):
+    blocks = place.count["y"] * place.count["x"]
+
     def product(core):
         left_side = core_columns(place, inputs, core)
-        return jnp.stack([dot_f32(left_side, grad, TN).astype(jnp.bfloat16) for grad in grads])
-
-    return reduce_weight(place, product, True, len(grads))
-
-
-def grad_by_columns(place, inputs, grad):
+        terms = [dot_f32(left_side, grad, TN).astype(jnp.bfloat16) for grad in grads]
+        terms = [term.reshape(blocks, -1, term.shape[-1]) for term in terms]
+        if extra is not None:
+            term = dot_f32(extra[0], core_columns(place, extra[1], core), TN).astype(jnp.bfloat16)
+            width = term.shape[1] // blocks
+            term = term.reshape(-1, width, blocks, width).transpose(2, 1, 0, 3)
+            terms.append(term.reshape(blocks, width, -1))
+        return jnp.stack(terms)
+
+    return product
+
+
+def term_by_columns(place, inputs, grad):
     def product(core):
         return dot_f32(inputs, core_columns(place, grad, core), TN).astype(jnp.bfloat16)
 
-    return reduce_weight(place, product, False, 1)
+    return product
+
+
+def term_of_vectors(place, rows_in):
+    blocks = place.count["y"] * place.count["x"]
+
+    def product(core):
+        mine = core_columns(place, rows_in, core)
+        return mine.reshape(rows_in.shape[0], blocks, -1).transpose(1, 0, 2)[None]
+
+    return product
+
+
+def clip_pairs(micro, z_count, step):
+    return [
+        (core * z_count + z, (z // micro) * z_count + micro * core + (step + z) % micro)
+        for core in range(2)
+        for z in range(z_count)
+    ]
 
 
 def to_clip(place, blocks):
@@ -552,20 +642,17 @@
     for step in range(micro):
         block = lax.dynamic_index_in_dim(blocks, lax.rem(z_here + step, micro), 0, keepdims=False)
         arrived.append(lax.ppermute(block, ("core", "z"), clip_pairs(micro, z_count, step)))
+    return arrived
+
+
+def ordered_clip(place, arrived):
+    micro, z_here = len(arrived), place.index["z"]
     stack = jnp.stack(arrived)
     ordered = [
         lax.dynamic_index_in_dim(stack, lax.rem(z_here - spot + micro, micro), 0, keepdims=False)
         for spot in range(micro)
     ]
     return jnp.concatenate(ordered, axis=0)
-
-
-def clip_pairs(micro, z_count, step):
-    return [
-        (core * z_count + z, (z // micro) * z_count + micro * core + (step + z) % micro)
-        for core in range(2)
-        for z in range(z_count)
-    ]
 
 
 def from_clip(place, rows_in, micro):
@@ -577,10 +664,17 @@
         block = lax.dynamic_index_in_dim(blocks, spot, 0, keepdims=False)
         pairs = [(end, start) for start, end in clip_pairs(micro, z_count, step)]
         arrived.append(lax.ppermute(block, ("core", "z"), pairs))
+    return arrived
+
+
+def own_clips(place, arrived):
+    micro, z_here = len(arrived), place.index["z"]
     stack = jnp.stack(arrived)
     return jnp.stack(
         [
-            lax.dynamic_index_in_dim(stack, lax.rem(number - z_here % micro + micro, micro), 0, keepdims=False)
+            lax.dynamic_index_in_dim(
+                stack, lax.rem(number - lax.rem(z_here, micro) + micro, micro), 0, keepdims=False
+            )
             for number in range(micro)
         ]
     )
@@ -614,27 +708,22 @@
     return lax.ppermute(rows_in, place.names["seq"], pairs)
 
 
-def feed_forward(inputs, up_weight, down_weight, up_bias, down_bias, gain_row, shift_row):
+def feed_up(inputs, up_weight, up_bias, gain_row, shift_row):
     normed, normal, inverse = norm_rows(inputs, gain_row, shift_row)
     normed = normed.astype(jnp.bfloat16)
     upper_rows = matmul(normed, up_weight) + up_bias
     hidden = apply_swish(upper_rows).astype(jnp.bfloat16)
-    result = matmul(hidden, down_weight) + down_bias
-    return (result, (normal, inverse, normed, upper_rows.astype(jnp.bfloat16), hidden))
-
-
-def feed_back(place, grad_result, stored, up_weight, down_weight, gain_row):
-    normal, inverse, normed, upper_rows, hidden = stored
+    return (hidden, (normal, inverse, normed, upper_rows.astype(jnp.bfloat16)))
+
+
+def feed_back_down(grad_result, stored, down_weight):
+    upper_rows = stored[3]
     grad_low = grad_result.astype(jnp.bfloat16)
-    grad_down = grad_by_columns(place, hidden, grad_low)
     grad_hidden = dot_f32(grad_low, down_weight, NT)
     grad_upper = (grad_hidden * swish_slope(upper_rows.astype(jnp.float32))).astype(jnp.bfloat16)
-    grad_up = grad_by_rows(place, normed, [grad_upper])[0]
-    grad_normed = dot_f32(grad_upper, up_weight, NT)
-    grad_in, grad_gain, grad_shift = norm_back(grad_normed, normal, inverse, gain_row)
     up_bias_grad = jnp.sum(grad_upper.astype(jnp.float32), axis=0)
     down_bias_grad = jnp.sum(grad_low.astype(jnp.float32), axis=0)
-    return (grad_in, (grad_up, grad_down), (grad_gain, grad_shift, up_bias_grad, down_bias_grad))
+    return (grad_low, grad_upper, up_bias_grad, down_bias_grad)
 
 
 def body(
@@ -664,23 +753,46 @@
     taps_base = final_base + 2
     scale = HEAD_DIM ** (-0.5)
 
-    rows_low = to_clip(place, frames)
-    vector_wide = lax.all_gather(vectors, ("y", "x", "core"), axis=1, tiled=True).astype(jnp.float32)
-    up_one = fetch(place, first_up[None], True)[0]
-    down_one = fetch(place, first_down, False)
-    attend_mix = fetch(place, attend_in, True)
-    attend_back_weight = fetch(place, attend_out, False)
-    point_mix = fetch(place, pointwise_in, True)
-    point_back = fetch(place, pointwise_out, False)
-    up_two = fetch(place, second_up[None], True)[0]
-    down_two = fetch(place, second_down, False)
-    cot_low = to_clip(place, cotangent)
-
-    row_count = rows_low.shape[0]
-    slot_len = row_count * place.count["seq"]
-    z_here = place.index["z"]
+    up_rows, up_columns = first_up.shape
+    vector_rows = 16
+    vector_parts = up_columns // vectors.shape[1]
+    padded_vectors = jnp.pad(vectors, ((0, vector_rows * vector_parts - vectors.shape[0]), (0, 0)))
+    vector_shard = (
+        padded_vectors.reshape(vector_parts, vector_rows, -1).transpose(1, 0, 2).reshape(vector_rows, -1)
+    )
+    shard_up_one = jnp.concatenate([first_up, vector_shard], axis=0)[None]
+    shard_attend = jnp.concatenate([attend_in, packed(attend_out)[None]])
+    shard_point = jnp.concatenate([pointwise_in, packed(pointwise_out)[None]])
+
     own_facts = jnp.stack([clip_valid, frame_counts])
     other_facts = place.turn(own_facts, "core", 1)
+    up_one = gather_t(place, shard_up_one)
+    rows_low = to_clip(place, frames)
+    up_one, first_down, frames_, shard_attend = fence(up_one, first_down, frames, shard_attend)
+    up_one = gather_a(place, up_one)
+    down_one = gather_t(place, first_down)
+    up_one, down_one, rows_low, shard_attend = fence(up_one, down_one, rows_low, shard_attend)
+    up_one = gather_b(place, up_one)
+    down_one = gather_a(place, down_one)
+    attend_mix = gather_t(place, shard_attend)
+    up_one, down_one, attend_mix, shard_point, rows_low = fence(
+        up_one, down_one, attend_mix, shard_point, rows_low
+    )
+    up_one = gather_core(place, up_one)
+    down_one = gather_b(place, down_one)
+    attend_mix = gather_a(place, attend_mix)
+    point_mix = gather_t(place, shard_point)
+    up_one, vector_slabs = assemble(
+        place, up_one, [("rows", 0, 1, up_rows), ("slabs", up_rows, vector_rows)]
+    )
+    up_one = up_one[0]
+    vector_wide = vector_slabs.reshape(place.dp_count, vector_rows, vector_parts, -1)
+    vector_wide = vector_wide.transpose(2, 1, 0, 3).reshape(vector_rows * vector_parts, width)
+    vector_wide = vector_wide[: vectors.shape[0]].astype(jnp.float32)
+
+    rows_in = ordered_clip(place, rows_low).astype(jnp.float32)
+    row_count = rows_in.shape[0]
+    z_here = place.index["z"]
     facts = jnp.where(z_here // micro == place.index["core"], own_facts, other_facts)
     facts = lax.dynamic_index_in_dim(facts, lax.rem(z_here, micro), 1, keepdims=False)
     valid_flag = (facts[0] > 0).astype(jnp.float32)
@@ -690,31 +802,49 @@
     pick_rows = (rel_rows[:, None] == jnp.arange(OFFSETS)[None, :]).astype(jnp.bfloat16)
     table = wide_table(matmul(pick_rows, distance).astype(jnp.bfloat16))
 
-    rows_in = rows_low.astype(jnp.float32)
-    rows_cot = cot_low.astype(jnp.float32)
-    one_out, one_kept = feed_forward(
+    one_hidden, one_kept = feed_up(
         rows_in,
         up_one,
-        down_one,
         vector_wide[2 : 2 + ratio_rows].reshape(FF),
-        vector_wide[2 + ratio_rows],
         vector_wide[0],
         vector_wide[1],
     )
-    after_one = rows_in + 0.5 * one_out
-
+    (down_one, attend_mix, point_mix, second_up, one_hidden, one_kept, up_one, table) = fence(
+        down_one, attend_mix, point_mix, second_up, one_hidden, one_kept, up_one, table
+    )
+    down_one = gather_core(place, down_one)
+    attend_mix = gather_b(place, attend_mix)
+    point_mix = gather_a(place, point_mix)
+    up_two = gather_t(place, second_up[None])
+    (down_one,) = assemble(place, down_one, [("columns",)])
+    after_one = rows_in + 0.5 * (matmul(one_hidden, down_one) + vector_wide[2 + ratio_rows])
     attend_normed, attend_normal, attend_inverse = norm_rows(
         after_one, vector_wide[attend_base], vector_wide[attend_base + 1]
     )
     attend_normed = attend_normed.astype(jnp.bfloat16)
+    (attend_mix, point_mix, up_two, second_down, after_one, attend_normed, attend_normal, attend_inverse) = fence(
+        attend_mix, point_mix, up_two, second_down, after_one, attend_normed, attend_normal, attend_inverse
+    )
+    attend_mix = gather_core(place, attend_mix)
+    point_mix = gather_b(place, point_mix)
+    up_two = gather_a(place, up_two)
+    down_two = gather_t(place, second_down)
+    attend_mix, attend_back_weight = assemble(place, attend_mix, [("rows", 0, 3, up_rows), ("packed", 3)])
     queries = (matmul(attend_normed, attend_mix[0]) + vector_wide[attend_base + 2]).astype(jnp.bfloat16)
     queries = (queries.astype(jnp.float32) * scale).astype(jnp.bfloat16)
     own_keys = matmul(attend_normed, attend_mix[1]).astype(jnp.bfloat16)
     own_values = (matmul(attend_normed, attend_mix[2]) + vector_wide[attend_base + 3]).astype(jnp.bfloat16)
     key_rows, value_rows = all_rows(place, own_keys), all_rows(place, own_values)
     context, levels = attend(meta, queries, key_rows, value_rows, table)
+    (point_mix, up_two, down_two, cotangent, context, levels, after_one) = fence(
+        point_mix, up_two, down_two, cotangent, context, levels, after_one
+    )
+    point_mix = gather_core(place, point_mix)
+    up_two = gather_b(place, up_two)
+    down_two = gather_a(place, down_two)
+    cot_low = to_clip(place, cotangent)
+    point_mix, point_back = assemble(place, point_mix, [("rows", 0, 2, up_rows), ("packed", 2)])
     after_two = after_one + matmul(context, attend_back_weight) + vector_wide[attend_base + 4]
-
     conv_normed, conv_normal, conv_inverse = norm_rows(
         after_two, vector_wide[conv_base], vector_wide[conv_base + 1]
     )
@@ -724,7 +854,8 @@
     gated = linear * logistic * live
     taps = vector_wide[taps_base : taps_base + KERNEL]
     reach = KERNEL - 1
-    padded = jnp.concatenate([neighbour_rows(place, gated[-reach:], 1), gated], axis=0)
+    before = neighbour_rows(place, gated[-reach:], 1)
+    padded = jnp.concatenate([before, gated], axis=0)
     depth_out = jnp.zeros_like(gated)
     for offset in range(KERNEL):
         depth_out = depth_out + taps[offset] * padded[offset : offset + row_count]
@@ -732,63 +863,106 @@
     deep_norm, deep_normal, deep_inverse = norm_rows(depth_out, deep_gain, vector_wide[conv_base + 3])
     activated = apply_swish(deep_norm).astype(jnp.bfloat16)
     after_three = after_two + matmul(activated, point_back)
-
-    two_out, two_kept = feed_forward(
+    (up_two, down_two, cot_low, after_three, padded, deep_norm, deep_normal, activated) = fence(
+        up_two, down_two, cot_low, after_three, padded, deep_norm, deep_normal, activated
+    )
+    up_two = gather_core(place, up_two)
+    down_two = gather_b(place, down_two)
+    (up_two,) = assemble(place, up_two, [("rows", 0, 1, up_rows)])
+    up_two = up_two[0]
+    two_hidden, two_kept = feed_up(
         after_three,
         up_two,
-        down_two,
         vector_wide[second_base + 2 : second_base + 2 + ratio_rows].reshape(FF),
-        vector_wide[second_base + 2 + ratio_rows],
         vector_wide[second_base],
         vector_wide[second_base + 1],
     )
+    (down_two, two_hidden, two_kept, up_two) = fence(down_two, two_hidden, two_kept, up_two)
+    down_two = gather_core(place, down_two)
+    (down_two,) = assemble(place, down_two, [("columns",)])
+    two_out = matmul(two_hidden, down_two) + vector_wide[second_base + 2 + ratio_rows]
     after_four = after_three + 0.5 * two_out
     final_rows, final_normal, final_inverse = norm_rows(
         after_four, vector_wide[final_base], vector_wide[final_base + 1]
     )
-    frames_out = from_clip(
-        place, jnp.where(valid_flag > 0, final_rows, rows_in).astype(jnp.bfloat16), micro
-    )
-
+    row_out = jnp.where(valid_flag > 0, final_rows, rows_in).astype(jnp.bfloat16)
+    rows_cot = ordered_clip(place, cot_low).astype(jnp.float32)
     grad_four, final_gain_grad, final_shift_grad = norm_back(
         rows_cot * valid_flag, final_normal, final_inverse, vector_wide[final_base]
     )
-    grad_two_in, two_weights, two_parts = feed_back(
-        place, 0.5 * grad_four, two_kept, up_two, down_two, vector_wide[second_base]
+    grad_low, grad_upper, two_up_bias, two_down_bias = feed_back_down(
+        0.5 * grad_four, two_kept, down_two
+    )
+    sum_down_two = reduce_core(place, term_by_columns(place, two_hidden, grad_low))
+    (sum_down_two, grad_four, grad_upper, row_out) = fence(sum_down_two, grad_four, grad_upper, row_out)
+    sum_down_two = reduce_b(place, sum_down_two)
+    frames_out = from_clip(place, row_out, micro)
+    sum_up_two = reduce_core(place, term_by_rows(place, two_kept[2], [grad_upper]))
+    grad_normed = dot_f32(grad_upper, up_two, NT)
+    grad_two_in, two_gain, two_shift = norm_back(
+        grad_normed, two_kept[0], two_kept[1], vector_wide[second_base]
     )
     grad_three = grad_four + grad_two_in
-
     conv_low = grad_three.astype(jnp.bfloat16)
-    grad_point_back = grad_by_columns(place, activated, conv_low)
     grad_deep = dot_f32(conv_low, point_back, NT) * swish_slope(deep_norm)
     grad_depth, deep_gain_grad, deep_shift_grad = norm_back(
         grad_deep, deep_normal, deep_inverse, deep_gain
     )
-    extended = jnp.concatenate([grad_depth, neighbour_rows(place, grad_depth[:reach], -1)], axis=0)
+    after = neighbour_rows(place, grad_depth[:reach], -1)
+    (sum_down_two, frames_out, sum_up_two, grad_three, conv_low, grad_depth, after) = fence(
+        sum_down_two, frames_out, sum_up_two, grad_three, conv_low, grad_depth, after
+    )
+    sum_down_two = reduce_a(place, sum_down_two)
+    sum_up_two = reduce_b(place, sum_up_two)
+    extended = jnp.concatenate([grad_depth, after], axis=0)
     grad_gated = jnp.zeros_like(grad_depth)
     tap_grads = []
     for offset in range(KERNEL):
         tap_grads.append(jnp.sum(padded[offset : offset + row_count] * grad_depth, axis=0))
         grad_gated = grad_gated + taps[offset] * extended[reach - offset : reach - offset + row_count]
+    tap_grads = jnp.stack(tap_grads)
     grad_gated = grad_gated * live
     grad_linear = (grad_gated * logistic).astype(jnp.bfloat16)
     grad_gate = (grad_gated * linear * logistic * (1.0 - logistic)).astype(jnp.bfloat16)
-    grad_point_mix = grad_by_rows(place, conv_normed, [grad_linear, grad_gate])
+    (sum_down_two, sum_up_two, grad_linear, grad_gate, tap_grads) = fence(
+        sum_down_two, sum_up_two, grad_linear, grad_gate, tap_grads
+    )
+    sum_down_two = reduce_t(place, sum_down_two)
+    sum_up_two = reduce_a(place, sum_up_two)
+    sum_point = reduce_core(
+        place, term_by_rows(place, conv_normed, [grad_linear, grad_gate], (activated, conv_low))
+    )
     grad_conv_normed = dot_f32(grad_linear, point_mix[0], NT) + dot_f32(grad_gate, point_mix[1], NT)
     grad_conv_in, conv_gain_grad, conv_shift_grad = norm_back(
         grad_conv_normed, conv_normal, conv_inverse, vector_wide[conv_base]
     )
     grad_two = grad_three + grad_conv_in
-
     attend_low = grad_two.astype(jnp.bfloat16)
-    grad_attend_back = grad_by_columns(place, context, attend_low)
     grad_context = dot_f32(attend_low, attend_back_weight, NT).astype(jnp.bfloat16)
+    (sum_down_two, sum_up_two, sum_point, grad_two, attend_low, grad_context) = fence(
+        sum_down_two, sum_up_two, sum_point, grad_two, attend_low, grad_context
+    )
+    grad_second_down = reduce_end(sum_down_two)
+    sum_up_two = reduce_t(place, sum_up_two)
+    sum_point = reduce_b(place, sum_point)
     grad_queries, part_keys, part_values, grad_table = attend_back(
         meta, queries, key_rows, value_rows, table, grad_context, context, levels
     )
+    (sum_up_two, sum_point, grad_queries, part_keys, part_values, grad_table) = fence(
+        sum_up_two, sum_point, grad_queries, part_keys, part_values, grad_table
+    )
+    grad_second_up = reduce_end(sum_up_two)[0]
+    sum_point = reduce_a(place, sum_point)
     grad_keys = own_sum(place, part_keys).astype(jnp.bfloat16)
     grad_values = own_sum(place, part_values).astype(jnp.bfloat16)
-    grad_attend_mix = grad_by_rows(place, attend_normed, [grad_queries, grad_keys, grad_values])
+    sum_distance = jnp.dot(
+        pick_rows.astype(jnp.float32).T, table_grad(grad_table), precision=lax.Precision.HIGHEST
+    )
+    sum_distance = sum_distance + place.turn(sum_distance, "core", 1)
+    sum_attend = reduce_core(
+        place,
+        term_by_rows(place, attend_normed, [grad_queries, grad_keys, grad_values], (context, attend_low)),
+    )
     grad_attend_normed = (
         dot_f32(grad_queries, attend_mix[0], NT)
         + dot_f32(grad_keys, attend_mix[1], NT)
@@ -798,23 +972,38 @@
         grad_attend_normed, attend_normal, attend_inverse, vector_wide[attend_base]
     )
     grad_one = grad_two + grad_attend_in
-
-    grad_one_in, one_weights, one_parts = feed_back(
-        place, 0.5 * grad_one, one_kept, up_one, down_one, vector_wide[0]
-    )
+    (sum_point, sum_attend, sum_distance, grad_one) = fence(sum_point, sum_attend, sum_distance, grad_one)
+    sum_point = reduce_t(place, sum_point)
+    sum_attend = reduce_b(place, sum_attend)
+    sum_distance = sum(
+        (place.turn(sum_distance, "b", step) for step in place.steps("b")), sum_distance
+    )
+    grad_low, grad_upper, one_up_bias, one_down_bias = feed_back_down(0.5 * grad_one, one_kept, down_one)
+    sum_down_one = reduce_core(place, term_by_columns(place, one_hidden, grad_low))
+    (sum_point, sum_attend, sum_distance, sum_down_one, grad_upper) = fence(
+        sum_point, sum_attend, sum_distance, sum_down_one, grad_upper
+    )
+    grad_point = reduce_end(sum_point)
+    sum_attend = reduce_a(place, sum_attend)
+    sum_down_one = reduce_b(place, sum_down_one)
+    sum_distance = sum(
+        (place.turn(sum_distance, "a", step) for step in place.steps("a")), sum_distance
+    )
+    sum_up_one = reduce_core(place, term_by_rows(place, one_kept[2], [grad_upper]))
+    grad_normed = dot_f32(grad_upper, up_one, NT)
+    grad_one_in, one_gain, one_shift = norm_back(grad_normed, one_kept[0], one_kept[1], vector_wide[0])
     grad_rows = grad_one + grad_one_in + (1.0 - valid_flag) * rows_cot
-    frames_grad = from_clip(place, grad_rows.astype(jnp.bfloat16), micro)
 
     def column_sum(rows):
         return jnp.sum(rows.astype(jnp.float32), axis=0)
 
     vector_part = jnp.concatenate(
         [
-            jnp.stack([one_parts[0], one_parts[1]]),
-            one_parts[2].reshape(ratio_rows, width),
+            jnp.stack([one_gain, one_shift]),
+            one_up_bias.reshape(ratio_rows, width),
             jnp.stack(
                 [
-                    one_parts[3],
+                    one_down_bias,
                     attend_gain_grad,
                     attend_shift_grad,
                     column_sum(grad_queries),
@@ -824,35 +1013,57 @@
                     conv_shift_grad,
                     deep_gain_grad,
                     deep_shift_grad,
-                    two_parts[0],
-                    two_parts[1],
+                    two_gain,
+                    two_shift,
                 ]
             ),
-            two_parts[2].reshape(ratio_rows, width),
-            jnp.stack([two_parts[3], final_gain_grad, final_shift_grad]),
-            jnp.stack(tap_grads),
+            two_up_bias.reshape(ratio_rows, width),
+            jnp.stack([two_down_bias, final_gain_grad, final_shift_grad]),
+            tap_grads,
         ],
         axis=0,
     )
-    everywhere = ("y", "x", "core", "far", "z")
-    grad_vectors = lax.psum_scatter(vector_part, everywhere, scatter_dimension=1, tiled=True)
-    local_distance = jnp.dot(
-        pick_rows.astype(jnp.float32).T, table_grad(grad_table), precision=lax.Precision.HIGHEST
-    )
-    grad_distance = lax.psum(local_distance, everywhere)
+    grad_rows = grad_rows.astype(jnp.bfloat16)
+    sum_vectors = reduce_core(place, term_of_vectors(place, vector_part))
+    (sum_attend, sum_down_one, sum_distance, sum_up_one, sum_vectors, grad_rows) = fence(
+        sum_attend, sum_down_one, sum_distance, sum_up_one, sum_vectors, grad_rows
+    )
+    sum_up_one = reduce_b(place, sum_up_one)
+    sum_down_one = reduce_a(place, sum_down_one)
+    sum_attend = reduce_t(place, sum_attend)
+    sum_vectors = reduce_b(place, sum_vectors)
+    sum_distance = sum(
+        (place.turn(sum_distance, "t", step) for step in place.steps("t")), sum_distance
+    )
+    frames_grad = from_clip(place, grad_rows, micro)
+    (sum_up_one, sum_down_one, sum_attend, sum_vectors, sum_distance) = fence(
+        sum_up_one, sum_down_one, sum_attend, sum_vectors, sum_distance
+    )
+    grad_attend = reduce_end(sum_attend)
+    sum_up_one = reduce_a(place, sum_up_one)
+    sum_down_one = reduce_t(place, sum_down_one)
+    sum_vectors = reduce_a(place, sum_vectors)
+    (sum_up_one, sum_down_one, sum_vectors, frames_grad) = fence(
+        sum_up_one, sum_down_one, sum_vectors, frames_grad
+    )
+    grad_first_down = reduce_end(sum_down_one)
+    sum_up_one = reduce_t(place, sum_up_one)
+    sum_vectors = reduce_t(place, sum_vectors)
+    grad_first_up = reduce_end(sum_up_one)[0]
+    grad_vectors = reduce_end(sum_vectors)[0]
     return (
-        frames_out,
-        frames_grad,
-        one_weights[0],
-        one_weights[1],
-        grad_attend_mix,
-        grad_attend_back,
-        grad_point_mix,
-        grad_point_back,
-        two_weights[0],
-        two_weights[1],
+        own_clips(place, frames_out),
+        own_clips(place, frames_grad),
+        grad_first_up,
+        grad_first_down,
+        grad_attend[:3],
+        unpacked(grad_attend[3]),
+        grad_point[:2],
+        unpacked(grad_point[2]),
+        grad_second_up,
+        grad_second_down,
         grad_vectors,
-        grad_distance,
+        sum_distance,
     )
 
 

time: 1300 us -> 914 us (0.70)
  starting transfers between devices: 314 us -> 164 us
  waiting for transfers between devices: 339 us -> 196 us
  blocking collectives: 67.5 us -> 0 us
  other arithmetic: 134 us -> 168 us
  matrix products: 151 us -> 131 us
  local copies, waits for them, and re-layouts: 140 us -> 122 us
  between operations: 21.5 us -> 5.62 us
    ppermute x253 -> x67, waiting for transfers between devices: 327 us -> 99.3 us  [turn(): return lax.ppermute(block, self.names.get(axis, axis), pairs)]
    ppermute x253 -> x67, starting transfers between devices: 297 us -> 91.9 us  [turn(): return lax.ppermute(block, self.names.get(axis, axis), pairs)]
    ppermute x0 -> x28, waiting for transfers between devices: none -> 80 us  [turn(): return lax.ppermute(block, ('y', 'x', 'core'), pairs)]
    ppermute x0 -> x28, starting transfers between devices: none -> 45.5 us  [turn(): return lax.ppermute(block, ('y', 'x', 'core'), pairs)]
    psum x1 -> x0, blocking collectives: 43.9 us -> none  [body(): grad_distance = lax.psum(local_distance, everywhere)]
    unnamed x994 -> x558, local copies, waits for them, and re-layouts: 70.3 us -> 28.3 us
    dynamic_slice x8 -> x34, local copies, waits for them, and re-layouts: 6.06 us -> 40.4 us  [the longest x20 31.5 us: pick_t(): return lax.dynamic_slice_in_dim(array, number * width, width, axis=axis)]
    convert_element_type x56 -> x22, other arithmetic: 30.6 us -> 55.7 us  [the longest x6 22.9 us: reduce_t(): arrived.append(place.turn(message.astype(parts[0].dtype), 't', step))]
  transfers between devices with their start and end apart: 264 -> 105, of which waited for: 79 -> 37; matrix products, arithmetic and copies ran while one was open for 23% -> 37% of each run, Pallas kernels for 6% -> 12%
where the time goes in v2:
time: 914 us; the launch traced here: 901 us
  waiting for transfers between devices  196 us (21%)
  other arithmetic  168 us (18%)
  starting transfers between devices  164 us (18%)
  matrix products  131 us (14%)
  local copies, waits for them, and re-layouts  122 us (13%)
  Pallas kernels  114 us (12%)
    dot_general x45, matrix products, dot_f32(): lax.dot_general(left_side, right_side, dims, preferred_element_type=jnp.f...  131 us
    ppermute x67, waiting for transfers between devices, turn(): return lax.ppermute(block, self.names.get(axis, axis), pairs)  99.3 us
    ppermute x67, starting transfers between devices, turn(): return lax.ppermute(block, self.names.get(axis, axis), pairs)  91.9 us
    ppermute x28, waiting for transfers between devices, turn(): return lax.ppermute(block, ('y', 'x', 'core'), pairs)  80 us
    pallas_call x1, Pallas kernels, attend_back(): pl.pallas_call(attend_back_kernel, grid_spec=pltpu.PrefetchScalarGridSpec...  54.3 us
    ppermute x28, starting transfers between devices, turn(): return lax.ppermute(block, ('y', 'x', 'core'), pairs)  45.5 us
    pallas_call x1, Pallas kernels, attend(): pl.pallas_call(attend_kernel, grid_spec=pltpu.PrefetchScalarGridSpec(num_...  35.6 us
    dynamic_slice x20, local copies, waits for them, and re-layouts, pick_t(): return lax.dynamic_slice_in_dim(array, number * width, width, axis=axis)  31.5 us
  transfers between devices with their start and end apart: 105, of which 37 were waited for; matrix products, arithmetic and copies ran while one was open for 37% of the time, Pallas kernels for 12%

profile of v2, /device:TPU:0, one launch (start us, length us, event | category | flops | bytes accessed | tf_op | source)
XLA Modules:
  0.0 900.6 jit_solution(8050044158429698289)
XLA Ops:
  15.6 11.8 %collective-permute-done.1 = bf16[1,144,1024]{2,1,0:T(8,128)(2,1)S(1)} collective-permute-done((bf16[1,144,1024]{2,1,0:T(8,128)(2,1)S(1)}, bf16[1,144,1024]{2,1,0:T(8,128)(2,1)S(1)}, u32[]{:S(2)}, u32[]{:S(2)}) %collective-permute-start.1) | collective-permute-done | bytes 294944 | tf_op jit(solution)/shard_map/ppermute | solution.py:361
  30.8 6.8 collective-permute-start.4
  47.0 8.4 collective-permute-done.5
  59.9 7.2 collective-permute-done.8
  67.0 16.8 %collective-permute-start.9 = (bf16[8,1,144,1024]{3,2,1,0:T(8,128)(2,1)S(1)}, bf16[8,1,144,1024]{3,2,1,0:T(8,128)(2,1)}, u32[]{:S(2)}, u32[]{:S(2)}) collective-permute-start(bf16[8,1,144,1024]{3,2,1,0:T(8,128)(2,1)S(1)} %pad_maximum_fusion.5.refs_0_), channel_id=1, source_target_pairs={{0,16},{4,12},{8,24},{12,4},{16,0},{20,28},{24,8},{28,20},{1,17},{... | collective-permute-start | bytes 7077896 | tf_op jit(solution)/shard_map/ppermute | solution.py:360
  92.9 9.4 %collective-permute-done.12 = bf16[4,128,256]{2,1,0:T(8,128)(2,1)} collective-permute-done((bf16[4,128,256]{2,1,0:T(8,128)(2,1)S(1)}, bf16[4,128,256]{2,1,0:T(8,128)(2,1)}, u32[]{:S(2)}, u32[]{:S(2)}) %collective-permute-start.12) | collective-permute-done | bytes 262176 | tf_op jit(solution)/shard_map/ppermute | solution.py:361
  130.3 7.4 collective-permute-done.17
  149.7 7.0 add_convert_fusion.1
  156.7 7.0 collective-permute-done.14.refs_1_
  181.9 8.2 collective-permute-done.24
  204.1 12.3 %collective-permute-done.21.refs_1_ = bf16[8,4,128,256]{3,2,1,0:T(8,128)(2,1)} collective-permute-done((bf16[8,4,128,256]{3,2,1,0:T(8,128)(2,1)}, bf16[8,4,128,256]{3,2,1,0:T(8,128)(2,1)}, u32[]{:S(2)}, u32[]{:S(2)}) %collective-permute-start.21) | collective-permute-done | bytes 2097184 | tf_op jit(solution)/shard_map/ppermute | solution.py:360
  248.8 7.2 collective-permute-done.29
  260.5 35.6 %attend.1 = (bf16[512,1024]{1,0:T(8,128)(2,1)S(1)}, f32[512,128]{1,0:T(8,128)S(1)}) custom-call(s32[2]{0:T(128)S(1)} %pad_add_fusion.2.meta_ref, bf16[512,1024]{1,0:T(8,128)(2,1)S(1)} %multiply_convert_fusion.7.q_ref, bf16[1024,1024]{1,0:T(8,128)(2,1)S(1)} %bitcast.433, bf16[1024,1024]{1,0:T(8,128)(2,1)} %bitcast.448, ...), custom_call_target="tpu_custom_call" | custom-call | tf_op jit(solution)/shard_map/attend/pallas_call | solution.py:202
  324.1 9.8 %fusion.348 = (f32[512]{0:T(512)S(1)}, f32[512,1024]{1,0:T(8,128)S(1)}) fusion(f32[512,1024]{1,0:T(8,128)S(1)} %get-tuple-element.705, f32[1024]{0:T(1024)S(1)} %bitcast.530, f32[1024]{0:T(1024)S(1)} %bitcast.532, f32[1024]{0:T(1024)S(1)} %bitcast.534, f32[1024]{0:T(1024)S(1)} %bitcast.536, f32[1024]{0:T(1024)S(1)} %bitcast.538, f32[1024]{0:T(1024)S(1)} %bitcast.540, ...), kind=kLoop, calls=%fused_computation.801 | loop fusion | flops 48233984 | bytes 4446208 | tf_op jit(solution)/shard_map/reduce_sum | solution.py:297
  355.9 7.8 add_convert_fusion
  405.9 7.2 convert_reduce_fusion
  428.6 7.4 multiply_reduce_fusion.1
  468.7 10.6 %multiply_convert_fusion.3 = (bf16[512,1024]{1,0:T(8,128)(2,1)}, f32[512,1024]{1,0:T(8,128)}) fusion(f32[512,1024]{1,0:T(8,128)S(1)} %copy-done.31, f32[512,1024]{1,0:T(8,128)S(1)} %copy-done.52, f32[512]{0:T(512)} %fusion.319, f32[512,1024]{1,0:T(8,128)S(1)} %subtract_multiply_fusion, f32[1024]{0:T(1024)S(1)} %bitcast.531, ...), kind=kLoop, calls=%fused_computation.328 | loop fusion | flops 35127296 | bytes 72480768 | tf_op jit(solution)/shard_map/convert_element_type | solution.py:926
  561.9 54.3 %attend_back.1 = (bf16[512,1024]{1,0:T(8,128)(2,1)S(1)}, bf16[1024,1024]{1,0:T(8,128)(2,1)}, bf16[1024,1024]{1,0:T(8,128)(2,1)}, f32[128,256]{1,0:T(8,128)S(1)}) custom-call(s32[2]{0:T(128)S(1)} %copy-done.20, bf16[512,1024]{1,0:T(8,128)(2,1)S(1)} %copy-done.8, bf16[1024,1024]{1,0:T(8,128)(2,1)} %bitcast.434, bf16[1024,1024]{1,0:T(8,128)(2,1)} %bitcast.449, ...), custom_call_target="tpu_custom_call" | custom-call | tf_op jit(solution)/shard_map/attend_back/pallas_call | solution.py:231
  677.7 9.7 %convert_reduce_fusion.1 = (f32[4096]{0:T(1024)S(1)}, bf16[512,4096]{1,0:T(8,128)(2,1)}) fusion(bf16[512,4096]{1,0:T(8,128)(2,1)} %get-tuple-element.330, bf16[512,1024]{1,0:T(8,128)(2,1)S(1)} %get-tuple-element.485, bf16[4096,1024]{1,0:T(8,128)(2,1)S(1)} %bitcast.436), kind=kOutput, calls=%fused_computation.51 | convolution fusion | flops 4320129024 | bytes 17842176 | tf_op jit(solution)/shard_map/dot_general | solution.py:25
  747.4 17.1 %collective-permute-done.78 = bf16[4,1,128,1024]{3,2,0,1:T(8,128)(2,1)S(1)} collective-permute-done((bf16[4,1,128,1024]{3,2,0,1:T(8,128)(2,1)S(1)}, bf16[4,1,128,1024]{3,2,0,1:T(8,128)(2,1)S(1)}, u32[]{:S(2)}, u32[]{:S(2)}) %collective-permute-start.78) | collective-permute-done | bytes 1048608 | tf_op jit(solution)/shard_map/ppermute | solution.py:360
  795.4 11.1 %collective-permute-done.88 = f32[1,2,56,128]{3,2,1,0:T(8,128)S(1)} collective-permute-done((f32[1,2,56,128]{3,2,1,0:T(8,128)S(1)}, f32[1,2,56,128]{3,2,1,0:T(8,128)S(1)}, u32[]{:S(2)}, u32[]{:S(2)}) %collective-permute-start.88) | collective-permute-done | bytes 57376 | tf_op jit(solution)/shard_map/ppermute | solution.py:360
  825.7 6.8 collective-permute-start.98
  844.4 9.5 %collective-permute-done.98 = bf16[256,1024]{1,0:T(8,128)(2,1)S(1)} collective-permute-done((bf16[256,1024]{1,0:T(8,128)(2,1)}, bf16[256,1024]{1,0:T(8,128)(2,1)S(1)}, u32[]{:S(2)}, u32[]{:S(2)}) %collective-permute-start.98) | collective-permute-done | bytes 524320 | tf_op jit(solution)/shard_map/ppermute | solution.py:666
  (1023 shorter events, 598.7 us)
Async XLA Ops:
  67.0 51.2 %collective-permute-start.9 = (bf16[8,1,144,1024]{3,2,1,0:T(8,128)(2,1)S(1)}, bf16[8,1,144,1024]{3,2,1,0:T(8,128)(2,1)}, u32[]{:S(2)}, u32[]{:S(2)}) collective-permute-start(bf16[8,1,144,1024]{3,2,1,0:T(8,128)(2,1)S(1)} %pad_maximum_fusion.5.refs_0_), channel_id=1, source_target_pairs={{0,16},{4,12},{8,24},{12,4},{16,0},{20,28},{24,8},{28,20},{1,17},{... | collective-permute-start | bytes 7077896 | tf_op jit(solution)/shard_map/ppermute | solution.py:360
  163.7 29.7 %collective-permute-start.26 = (bf16[8,1024,128]{2,1,0:T(8,128)(2,1)S(1)}, bf16[8,1024,128]{2,1,0:T(8,128)(2,1)S(1)}, u32[]{:S(2)}, u32[]{:S(2)}) collective-permute-start(bf16[8,1024,128]{2,1,0:T(8,128)(2,1)S(1)} %copy-done.6), channel_id=1, source_target_pairs={{0,4},{4,0},{1,5},{5,1},{2,6},{6,2},{3,7},{7,3},{8,12},{12,8},{9,1... | collective-permute-start | bytes 6291464 | tf_op jit(solution)/shard_map/ppermute | solution.py:361
  163.7 29.7 %collective-permute-start.27 = (bf16[8,1024,128]{2,1,0:T(8,128)(2,1)S(1)}, bf16[8,1024,128]{2,1,0:T(8,128)(2,1)S(1)}, u32[]{:S(2)}, u32[]{:S(2)}) collective-permute-start(bf16[8,1024,128]{2,1,0:T(8,128)(2,1)S(1)} %collective-permute-done.14.refs_1_), channel_id=1, source_target_pairs={{0,4},{4,0},{1,5},{5,1},{2,6},{6,2},{3,7},{7,3},{8,12},{12,8},{9,1... | collective-permute-start | bytes 6291464 | tf_op jit(solution)/shard_map/ppermute | solution.py:361
  164.2 29.1 %collective-permute-start.22 = (bf16[4,3,128,256]{3,2,1,0:T(8,128)(2,1)S(1)}, bf16[4,3,128,256]{3,2,1,0:T(8,128)(2,1)S(1)}, u32[]{:S(2)}, u32[]{:S(2)}) collective-permute-start(bf16[4,3,128,256]{3,2,1,0:T(8,128)(2,1)S(1)} %pad_maximum_fusion.20), channel_id=1, source_target_pairs={{0,8},{4,20},{8,0},{12,28},{16,24},{20,4},{24,16},{28,12},{1,9},{5... | collective-permute-start | bytes 2359304 | tf_op jit(solution)/shard_map/ppermute | solution.py:360
  231.2 65.0 %collective-permute-start.28 = (bf16[8,3,128,256]{3,2,1,0:T(8,128)(2,1)S(1)}, bf16[8,3,128,256]{3,2,1,0:T(8,128)(2,1)S(1)}, u32[]{:S(2)}, u32[]{:S(2)}) collective-permute-start(bf16[8,3,128,256]{3,2,1,0:T(8,128)(2,1)S(1)} %pad_maximum_fusion.10.refs_0_), channel_id=1, source_target_pairs={{0,16},{4,12},{8,24},{12,4},{16,0},{20,28},{24,8},{28,20},{1,17},{... | collective-permute-start | bytes 4718600 | tf_op jit(solution)/shard_map/ppermute | solution.py:360
  298.2 44.0 %collective-permute-start.38 = (bf16[8,1,128,1024]{3,2,1,0:T(8,128)(2,1)}, bf16[8,1,128,1024]{3,2,1,0:T(8,128)(2,1)}, u32[]{:S(2)}, u32[]{:S(2)}) collective-permute-start(bf16[8,1,128,1024]{3,2,1,0:T(8,128)(2,1)} %pad_maximum_fusion.8.refs_0_), channel_id=1, source_target_pairs={{0,16},{4,12},{8,24},{12,4},{16,0},{20,28},{24,8},{28,20},{1,17},{... | collective-permute-start | bytes 6291464 | tf_op jit(solution)/shard_map/ppermute | solution.py:360
  299.7 42.5 %collective-permute-start.40 = (bf16[256,1024]{1,0:T(8,128)(2,1)}, bf16[256,1024]{1,0:T(8,128)(2,1)S(1)}, u32[]{:S(2)}, u32[]{:S(2)}) collective-permute-start(bf16[256,1024]{1,0:T(8,128)(2,1)} %get-tuple-element.627), channel_id=1, source_target_pairs={{0,0},{1,1},{2,4},{3,5},{4,2},{5,3},{6,6},{7,7},{8,8},{9,9},{10,12... | collective-permute-start | bytes 1572872 | tf_op jit(solution)/shard_map/ppermute | solution.py:644
  304.7 37.5 %collective-permute-start.41 = (bf16[256,1024]{1,0:T(8,128)(2,1)}, bf16[256,1024]{1,0:T(8,128)(2,1)}, u32[]{:S(2)}, u32[]{:S(2)}) collective-permute-start(bf16[256,1024]{1,0:T(8,128)(2,1)} %get-tuple-element.626), channel_id=1, source_target_pairs={{0,1},{1,0},{2,5},{3,4},{4,3},{5,2},{6,7},{7,6},{8,9},{9,8},{10,13... | collective-permute-start | bytes 1572872 | tf_op jit(solution)/shard_map/ppermute | solution.py:644
  417.5 31.2 %collective-permute-start.54 = (bf16[1,4,128,4096]{3,2,1,0:T(8,128)(2,1)}, bf16[1,4,128,4096]{3,2,1,0:T(8,128)(2,1)}, u32[]{:S(2)}, u32[]{:S(2)}) collective-permute-start(bf16[1,4,128,4096]{3,2,1,0:T(8,128)(2,1)} %bitcast.124), channel_id=1, source_target_pairs={{0,4},{4,0},{1,5},{5,1},{2,6},{6,2},{3,7},{7,3},{8,12},{12,8},{9,1... | collective-permute-start | bytes 12582920 | tf_op jit(solution)/shard_map/ppermute | solution.py:361
  461.5 46.4 %collective-permute-start.57 = (bf16[1,2,128,4096]{3,2,1,0:T(8,128)(2,1)}, bf16[1,2,128,4096]{3,2,1,0:T(8,128)(2,1)}, u32[]{:S(2)}, u32[]{:S(2)}) collective-permute-start(bf16[1,2,128,4096]{3,2,1,0:T(8,128)(2,1)} %add_convert_fusion.5), channel_id=1, source_target_pairs={{0,16},{4,12},{8,24},{12,4},{16,0},{20,28},{24,8},{28,20},{1,17},{... | collective-permute-start | bytes 6291464 | tf_op jit(solution)/shard_map/ppermute | solution.py:360
  465.7 42.2 %collective-permute-start.56 = (bf16[4096,128]{1,0:T(8,128)(2,1)}, bf16[4096,128]{1,0:T(8,128)(2,1)}, u32[]{:S(2)}, u32[]{:S(2)}) collective-permute-start(bf16[4096,128]{1,0:T(8,128)(2,1)} %add_convert_fusion.12), channel_id=1, source_target_pairs={{0,8},{4,20},{8,0},{12,28},{16,24},{20,4},{24,16},{28,12},{1,9},{5... | collective-permute-start | bytes 3145736 | tf_op jit(solution)/shard_map/ppermute | solution.py:360
  510.7 33.0 %collective-permute-start.62 = (bf16[3,4,128,1024]{3,2,0,1:T(8,128)(2,1)S(1)}, bf16[3,4,128,1024]{3,2,0,1:T(8,128)(2,1)S(1)}, u32[]{:S(2)}, u32[]{:S(2)}) collective-permute-start(bf16[3,4,128,1024]{3,2,0,1:T(8,128)(2,1)S(1)} %pad_maximum_fusion.4), channel_id=1, source_target_pairs={{0,4},{4,0},{1,5},{5,1},{2,6},{6,2},{3,7},{7,3},{8,12},{12,8},{9,1... | collective-permute-start | bytes 9437192 | tf_op jit(solution)/shard_map/ppermute | solution.py:361
  514.8 28.9 %collective-permute-start.61 = (bf16[1,1,128,4096]{3,2,1,0:T(8,128)(2,1)S(1)}, bf16[1,1,128,4096]{3,2,1,0:T(8,128)(2,1)S(1)}, u32[]{:S(2)}, u32[]{:S(2)}) collective-permute-start(bf16[1,1,128,4096]{3,2,1,0:T(8,128)(2,1)S(1)} %add_convert_fusion.11), channel_id=1, source_target_pairs={{0,8},{4,20},{8,0},{12,28},{16,24},{20,4},{24,16},{28,12},{1,9},{5... | collective-permute-start | bytes 3145736 | tf_op jit(solution)/shard_map/ppermute | solution.py:360
  548.4 76.6 %collective-permute-start.66 = (bf16[3,2,128,1024]{3,2,0,1:T(8,128)(2,1)}, bf16[3,2,128,1024]{3,2,0,1:T(8,128)(2,1)}, u32[]{:S(2)}, u32[]{:S(2)}) collective-permute-start(bf16[3,2,128,1024]{3,2,0,1:T(8,128)(2,1)} %add_convert_fusion.7), channel_id=1, source_target_pairs={{0,16},{4,12},{8,24},{12,4},{16,0},{20,28},{24,8},{28,20},{1,17},{... | collective-permute-start | bytes 4718600 | tf_op jit(solution)/shard_map/ppermute | solution.py:360
  556.2 68.7 %collective-permute-start.63 = (bf16[1,1,128,1024]{3,2,1,0:T(8,128)(2,1)S(1)}, bf16[1,1,128,1024]{3,2,1,0:T(8,128)(2,1)S(1)}, u32[]{:S(2)}, u32[]{:S(2)}) collective-permute-start(bf16[1,1,128,1024]{3,2,1,0:T(8,128)(2,1)S(1)} %get-tuple-element.514), channel_id=1, source_target_pairs={{0,1},{1,2},{2,3},{3,0},{4,5},{5,6},{6,7},{7,4},{8,9},{9,10},{10,1... | collective-permute-start | bytes 786440 | tf_op jit(solution)/shard_map/ppermute | solution.py:361
  558.1 66.9 %collective-permute-start.64 = (bf16[1,1,128,1024]{3,2,1,0:T(8,128)(2,1)S(1)}, bf16[1,1,128,1024]{3,2,1,0:T(8,128)(2,1)S(1)}, u32[]{:S(2)}, u32[]{:S(2)}) collective-permute-start(bf16[1,1,128,1024]{3,2,1,0:T(8,128)(2,1)S(1)} %get-tuple-element.513), channel_id=1, source_target_pairs={{0,2},{1,3},{2,0},{3,1},{4,6},{5,7},{6,4},{7,5},{8,10},{9,11},{10,... | collective-permute-start | bytes 786440 | tf_op jit(solution)/shard_map/ppermute | solution.py:361
  560.1 64.9 %collective-permute-start.65 = (bf16[1,1,128,1024]{3,2,1,0:T(8,128)(2,1)S(1)}, bf16[1,1,128,1024]{3,2,1,0:T(8,128)(2,1)S(1)}, u32[]{:S(2)}, u32[]{:S(2)}) collective-permute-start(bf16[1,1,128,1024]{3,2,1,0:T(8,128)(2,1)S(1)} %get-tuple-element.512), channel_id=1, source_target_pairs={{0,3},{1,0},{2,1},{3,2},{4,7},{5,4},{6,5},{7,6},{8,11},{9,8},{10,9... | collective-permute-start | bytes 786440 | tf_op jit(solution)/shard_map/ppermute | solution.py:361
  673.2 41.9 %collective-permute-start.77 = (bf16[4096,512]{1,0:T(8,128)(2,1)}, bf16[4096,512]{1,0:T(8,128)(2,1)}, u32[]{:S(2)}, u32[]{:S(2)}) collective-permute-start(bf16[4096,512]{1,0:T(8,128)(2,1)} %convolution_convert_fusion.2), channel_id=1, source_target_pairs={{0,4},{4,0},{1,5},{5,1},{2,6},{6,2},{3,7},{7,3},{8,12},{12,8},{9,1... | collective-permute-start | bytes 12582920 | tf_op jit(solution)/shard_map/ppermute | solution.py:361
  676.8 38.3 %collective-permute-start.75 = (bf16[4,2,128,1024]{3,2,0,1:T(8,128)(2,1)}, bf16[4,2,128,1024]{3,2,0,1:T(8,128)(2,1)}, u32[]{:S(2)}, u32[]{:S(2)}) collective-permute-start(bf16[4,2,128,1024]{3,2,0,1:T(8,128)(2,1)} %add_convert_fusion.4), channel_id=1, source_target_pairs={{0,16},{4,12},{8,24},{12,4},{16,0},{20,28},{24,8},{28,20},{1,17},{... | collective-permute-start | bytes 6291464 | tf_op jit(solution)/shard_map/ppermute | solution.py:360
  722.5 43.3 %collective-permute-start.81 = (bf16[1,4,128,4096]{3,2,1,0:T(8,128)(2,1)}, bf16[1,4,128,4096]{3,2,1,0:T(8,128)(2,1)}, u32[]{:S(2)}, u32[]{:S(2)}) collective-permute-start(bf16[1,4,128,4096]{3,2,1,0:T(8,128)(2,1)} %bitcast.192), channel_id=1, source_target_pairs={{0,4},{4,0},{1,5},{5,1},{2,6},{6,2},{3,7},{7,3},{8,12},{12,8},{9,1... | collective-permute-start | bytes 12582920 | tf_op jit(solution)/shard_map/ppermute | solution.py:361
  727.8 38.0 %collective-permute-start.79 = (bf16[4096,256]{1,0:T(8,128)(2,1)}, bf16[4096,256]{1,0:T(8,128)(2,1)}, u32[]{:S(2)}, u32[]{:S(2)}) collective-permute-start(bf16[4096,256]{1,0:T(8,128)(2,1)} %add_convert_fusion.3), channel_id=1, source_target_pairs={{0,16},{4,12},{8,24},{12,4},{16,0},{20,28},{24,8},{28,20},{1,17},{... | collective-permute-start | bytes 6291464 | tf_op jit(solution)/shard_map/ppermute | solution.py:360
  768.6 49.2 %collective-permute-start.83 = (bf16[1,2,128,4096]{3,2,1,0:T(8,128)(2,1)S(1)}, bf16[1,2,128,4096]{3,2,1,0:T(8,128)(2,1)S(1)}, u32[]{:S(2)}, u32[]{:S(2)}) collective-permute-start(bf16[1,2,128,4096]{3,2,1,0:T(8,128)(2,1)S(1)} %add_convert_fusion.2), channel_id=1, source_target_pairs={{0,16},{4,12},{8,24},{12,4},{16,0},{20,28},{24,8},{28,20},{1,17},{... | collective-permute-start | bytes 6291464 | tf_op jit(solution)/shard_map/ppermute | solution.py:360
  781.1 36.7 %collective-permute-start.84 = (bf16[4096,128]{1,0:T(8,128)(2,1)S(1)}, bf16[4096,128]{1,0:T(8,128)(2,1)S(1)}, u32[]{:S(2)}, u32[]{:S(2)}) collective-permute-start(bf16[4096,128]{1,0:T(8,128)(2,1)S(1)} %add_convert_fusion.9), channel_id=1, source_target_pairs={{0,8},{4,20},{8,0},{12,28},{16,24},{20,4},{24,16},{28,12},{1,9},{5... | collective-permute-start | bytes 3145736 | tf_op jit(solution)/shard_map/ppermute | solution.py:360
  820.0 46.2 %collective-permute-start.92 = (bf16[1,1,128,4096]{3,2,1,0:T(8,128)(2,1)S(1)}, bf16[1,1,128,4096]{3,2,1,0:T(8,128)(2,1)}, u32[]{:S(2)}, u32[]{:S(2)}) collective-permute-start(bf16[1,1,128,4096]{3,2,1,0:T(8,128)(2,1)S(1)} %add_convert_fusion.8), channel_id=1, source_target_pairs={{0,8},{4,20},{8,0},{12,28},{16,24},{20,4},{24,16},{28,12},{1,9},{5... | collective-permute-start | bytes 3145736 | tf_op jit(solution)/shard_map/ppermute | solution.py:360
  (356 other events, 5961.1 us)

commit v3 on v2

v3 whole, which is shorter than its diff:
```python
import jax
import jax.numpy as jnp
from jax import lax
from jax.experimental import pallas as pl
from jax.experimental.pallas import tpu as pltpu
from jax.sharding import Mesh
from jax.sharding import PartitionSpec as P

HEADS = 16
HEAD_DIM = 64
FF = 4096
KERNEL = 31
LEFT = 64
OFFSETS = 73
EPSILON = 1e-05

LANES = 128
SOFT_ROWS = 32
SLOPE_ROWS = 16
RIGHT = OFFSETS - 1 - LEFT
NT = (((1,), (1,)), ((), ()))
NN = (((1,), (0,)), ((), ()))
TN = (((0,), (0,)), ((), ()))


def dot_f32(left_side, right_side, dims):
    return lax.dot_general(left_side, right_side, dims, preferred_element_type=jnp.float32)


def band_distance():
    shape = (LANES, 3 * LANES)
    return (
        lax.broadcasted_iota(jnp.int32, shape, 1)
        - LANES
        - lax.broadcasted_iota(jnp.int32, shape, 0)
    )


LAST_ROWS = 8


def add_band(score_ref, half, source, distance, block, number):
    rows = slice(number * LANES, (number + 1) * LANES)
    own = source[rows]
    left_col = own[:, 2 * LANES - LEFT : 2 * LANES - LEFT + 1]
    right_col = own[:, RIGHT : RIGHT + 1]
    rolled = pltpu.roll(own - right_col, LANES, 1, stride=1, stride_axis=0)
    window = pl.multiple_of(block * LANES, LANES)
    near = rolled[:LEFT, :LANES] + (right_col - left_col)[:LEFT]
    near = jnp.where(distance[:LEFT, :LANES] > -LEFT, near, 0.0)
    score_ref[half, number * LANES : number * LANES + LEFT, pl.ds(window, LANES)] += near
    score_ref[half, rows, pl.ds(window + LANES, LANES)] += rolled[:, LANES:]
    last = LANES - LAST_ROWS
    after = jnp.where(distance[last:, 2 * LANES :] < RIGHT, rolled[last:, :LANES], 0.0)
    score_ref[half, number * LANES + last : (number + 1) * LANES, pl.ds(window + 2 * LANES, LANES)] += after


def in_half(shape, half):
    lanes = lax.broadcasted_iota(jnp.int32, shape, 1)
    return (lanes < HEAD_DIM) if half == 0 else (lanes >= HEAD_DIM)


def spare_lane(shape):
    return lax.rem(lax.broadcasted_iota(jnp.int32, shape, 1), HEAD_DIM)


def key_marks(meta_ref, key_count, blocks):
    shape = (key_count, LANES)
    spare, keys = spare_lane(shape), lax.broadcasted_iota(jnp.int32, shape, 0)
    before = keys < (meta_ref[0] + spare // 2) * LANES
    side = jnp.where(lax.rem(spare, 2) == 0, before.astype(jnp.float32), 1.0 - before.astype(jnp.float32))
    dead = jnp.where(keys < meta_ref[1], 0.0, -1e30)
    ones = (spare < 2 * blocks + 4).astype(jnp.float32)
    marks = jnp.where(spare < 2 * blocks, side, jnp.where(spare == 2 * blocks, dead, ones))
    return marks.astype(jnp.bfloat16)


def in_parts(column):
    parts = []
    for _ in range(3):
        part = column.astype(jnp.bfloat16).astype(jnp.float32)
        parts.append(part)
        column = column - part
    return parts


def with_marks(rows_half, half, columns_of):
    square = (LANES, LANES)
    spare, mine = spare_lane(square), in_half(square, half)
    parts = []
    for number in range(rows_half.shape[0] // LANES):
        own = rows_half[number * LANES : (number + 1) * LANES].astype(jnp.float32)
        marks = jnp.zeros(square, jnp.float32)
        for place, column in columns_of(number):
            marks = jnp.where(spare == place, column, marks)
        parts.append(jnp.where(mine, own, marks).astype(jnp.bfloat16))
    return jnp.concatenate(parts, axis=0)


def marked_queries(q_half, half, source, extra, blocks):
    def columns_of(number):
        rows = slice(number * LANES, (number + 1) * LANES)
        own = source[rows]
        columns = [
            (2 * number, own[:, 2 * LANES - LEFT : 2 * LANES - LEFT + 1]),
            (2 * number + 1, own[:, RIGHT : RIGHT + 1]),
            (2 * blocks, 1.0),
        ]
        return columns + [(2 * blocks + 1 + place, part[rows]) for place, part in enumerate(extra)]

    return with_marks(q_half, half, columns_of)


def attend_kernel(meta_ref, q_ref, k_ref, v_ref, e_ref, c_ref, lse_ref, score_ref, share_ref, marks_ref):
    row_count, key_count = q_ref.shape[0], k_ref.shape[0]
    blocks = row_count // LANES
    pair = pl.program_id(0)
    lanes = lax.broadcasted_iota(jnp.int32, (row_count, LANES), 1)
    distance = band_distance()

    @pl.when(pair == 0)
    def _():
        marks_ref[...] = key_marks(meta_ref, key_count, blocks)

    sources = []
    for half in range(2):
        mine = in_half((row_count, LANES), half)
        q_half = jnp.where(mine, q_ref[...], 0)
        source = dot_f32(q_half, e_ref[...], NT).astype(jnp.bfloat16).astype(jnp.float32)
        sources.append(source)
        queries = marked_queries(q_half, half, source, [], blocks)
        keys = jnp.where(in_half((key_count, LANES), half), k_ref[...], marks_ref[...])
        score_ref[half, :, LANES : LANES + key_count] = dot_f32(queries, keys, NT)
    result = None
    for half in range(2):
        inverses = []
        for number in range(blocks):
            rows = slice(number * LANES, (number + 1) * LANES)
            add_band(score_ref, half, sources[half], distance, meta_ref[0] + number, number)
            for first in range(number * LANES, (number + 1) * LANES, SOFT_ROWS):
                few = slice(first, first + SOFT_ROWS)
                scores = score_ref[half, few, LANES : LANES + key_count]
                peak = jnp.max(scores, axis=1, keepdims=True)
                grown = jnp.exp(scores - peak)
                total = jnp.sum(grown, axis=1, keepdims=True)
                share_ref[half, few] = grown.astype(jnp.bfloat16)
                inverses.append(1.0 / total)
                lse_ref[few] = jnp.where(
                    lanes[few] == 2 * pair + half, peak + jnp.log(total), lse_ref[few]
                )
        context = dot_f32(share_ref[half], v_ref[...], NN) * jnp.concatenate(inverses, axis=0)
        result = context if half == 0 else jnp.where(in_half(context.shape, 1), context, result)
    c_ref[...] = result.astype(jnp.bfloat16)


def attend_back_kernel(
    meta_ref, q_ref, k_ref, v_ref, e_ref, dc_ref, c_ref, lse_ref,
    dq_ref, dk_ref, dv_ref, de_ref,
    score_ref, grad_ref, share_ref, slope_ref, source_ref, wide_ref, marks_ref,
):
    row_count, key_count = q_ref.shape[0], k_ref.shape[0]
    key_blocks, blocks = key_count // LANES, row_count // LANES
    pair = pl.program_id(0)
    lanes = lax.broadcasted_iota(jnp.int32, (row_count, LANES), 1)
    distance = band_distance()
    square = (LANES, LANES)
    flip = (
        lax.broadcasted_iota(jnp.int32, square, 0) + lax.broadcasted_iota(jnp.int32, square, 1)
        == LANES - 1
    ).astype(jnp.float32).astype(jnp.bfloat16)
    spots = lax.broadcasted_iota(jnp.int32, square, 1)

    @pl.when(pair == 0)
    def _():
        shape = (key_count, LANES)
        place = lax.broadcasted_iota(jnp.int32, shape, 1)
        edge = (meta_ref[0] + place // 2) * LANES
        key = lax.broadcasted_iota(jnp.int32, shape, 0)
        before = (key < edge).astype(jnp.float32)
        after = (key >= edge + LANES).astype(jnp.float32)
        wide_ref[:, LANES:] = jnp.where(lax.rem(place, 2) == 0, before, after).astype(jnp.bfloat16)
        for half in range(2):
            slope_ref[half, :, :LANES] = jnp.zeros((row_count, LANES), jnp.bfloat16)
            slope_ref[half, :, LANES + key_count :] = jnp.zeros((row_count, LANES), jnp.bfloat16)
        de_ref[...] = jnp.zeros(de_ref.shape, jnp.float32)
        marks_ref[0] = key_marks(meta_ref, key_count, blocks)
        marks_ref[1] = (spare_lane(shape) < 3).astype(jnp.float32).astype(jnp.bfloat16)

    wide_ref[:, :LANES] = k_ref[...]
    inner_all = dc_ref[...].astype(jnp.float32) * c_ref[...].astype(jnp.float32)
    sources, q_halves, dc_halves = [], [], []
    for half in range(2):
        mine, mine_keys = in_half((row_count, LANES), half), in_half((key_count, LANES), half)
        q_half = jnp.where(mine, q_ref[...], 0)
        dc_half = jnp.where(mine, dc_ref[...], 0)
        source = dot_f32(q_half, e_ref[...], NT).astype(jnp.bfloat16).astype(jnp.float32)
        inner = jnp.sum(jnp.where(mine, inner_all, 0.0), axis=1, keepdims=True)
        level = jnp.sum(
            jnp.where(lanes == 2 * pair + half, lse_ref[...], 0.0), axis=1, keepdims=True
        )
        queries = marked_queries(q_half, half, source, in_parts(-level), blocks)
        keys = jnp.where(mine_keys, k_ref[...], marks_ref[0])
        score_ref[half, :, LANES : LANES + key_count] = dot_f32(queries, keys, NT)
        inner_parts = in_parts(-inner)
        grads = with_marks(
            dc_half,
            half,
            lambda number, parts=inner_parts: [
                (place, part[number * LANES : (number + 1) * LANES])
                for place, part in enumerate(parts)
            ],
        )
        values = jnp.where(mine_keys, v_ref[...], marks_ref[1])
        grad_ref[half] = dot_f32(grads, values, NT)
        sources.append(source)
        q_halves.append(q_half)
        dc_halves.append(dc_half)
    grad_q = grad_k = grad_v = None
    for half in range(2):
        for number in range(blocks):
            rows = slice(number * LANES, (number + 1) * LANES)
            add_band(score_ref, half, sources[half], distance, meta_ref[0] + number, number)
            for first in range(number * LANES, (number + 1) * LANES, SLOPE_ROWS):
                few = slice(first, first + SLOPE_ROWS)
                shares = jnp.exp(score_ref[half, few, LANES : LANES + key_count])
                share_ref[half, few] = shares.astype(jnp.bfloat16)
                slope_ref[half, few, LANES : LANES + key_count] = (
                    shares * grad_ref[half, few]
                ).astype(jnp.bfloat16)
    for half in range(2):
        mine = in_half((row_count, LANES), half)
        slopes = slope_ref[half, :, LANES : LANES + key_count]
        wide = dot_f32(slopes, wide_ref[...], NN)
        before = wide[:, LANES:]
        for number in range(blocks):
            rows = slice(number * LANES, (number + 1) * LANES)
            window = pl.multiple_of((meta_ref[0] + number) * LANES, LANES)
            first, last = number * LANES, (number + 1) * LANES - LAST_ROWS
            near = slope_ref[half, first : first + LEFT, pl.ds(window, LANES)].astype(jnp.float32)
            near = jnp.where(distance[:LEFT, :LANES] > -LEFT, near, 0.0)
            final = slope_ref[half, last - 8 : last + 8, pl.ds(window + 2 * LANES, LANES)]
            final = final.astype(jnp.float32)[8:]
            final = jnp.where(distance[LANES - LAST_ROWS :, 2 * LANES :] < RIGHT, final, 0.0)
            middle = slope_ref[half, rows, pl.ds(window + LANES, LANES)]
            gap = jnp.zeros((LANES - LEFT - LAST_ROWS, LANES), jnp.float32)
            edges = jnp.concatenate([near, gap, final], axis=0)
            inner_sum = jnp.sum(edges, axis=1, keepdims=True)
            first_rows = lax.broadcasted_iota(jnp.int32, (LANES, 1), 0) < LEFT
            far_left = before[rows, 2 * number : 2 * number + 1] - jnp.where(first_rows, inner_sum, 0.0)
            far_right = before[rows, 2 * number + 1 : 2 * number + 2] - jnp.where(
                first_rows, 0.0, inner_sum
            )
            band = jnp.concatenate([edges.astype(jnp.bfloat16), middle], axis=1)
            turned = dot_f32(flip, band, NN)
            turned = pltpu.roll(turned, 1, 1, stride=1, stride_axis=0)
            turned = dot_f32(flip, turned.astype(jnp.bfloat16), NN)
            turned = jnp.concatenate(
                [
                    turned[:, :LANES] + jnp.where(spots == RIGHT, far_right, 0.0),
                    turned[:, LANES:] + jnp.where(spots == 0, far_left, 0.0),
                ],
                axis=1,
            )
            source_ref[half, rows] = turned.astype(jnp.bfloat16)
        q_part = wide[:, :LANES] + dot_f32(source_ref[half], e_ref[...], NN)
        k_part = dot_f32(q_halves[half], slopes, TN)
        v_part = dot_f32(dc_halves[half], share_ref[half], TN)
        de_ref[...] += dot_f32(q_halves[half], source_ref[half], TN)
        grad_q = q_part if half == 0 else jnp.where(mine, q_part, grad_q)
        grad_k = k_part if half == 0 else grad_k + k_part
        grad_v = v_part if half == 0 else grad_v + v_part
    dq_ref[...] = (grad_q * HEAD_DIM ** (-0.5)).astype(jnp.bfloat16)
    dk_ref[...] = grad_k.T.astype(jnp.bfloat16)
    dv_ref[...] = grad_v.T.astype(jnp.bfloat16)


def pair_spec(row_count):
    return pl.BlockSpec((row_count, LANES), lambda pair, meta: (0, pair))


def fixed_spec(row_count, column_count):
    return pl.BlockSpec((row_count, column_count), lambda pair, meta: (0, 0))


def attend(meta, queries, key_rows, value_rows, table):
    row_count, width = queries.shape
    key_count = key_rows.shape[0]
    return pl.pallas_call(
        attend_kernel,
        grid_spec=pltpu.PrefetchScalarGridSpec(
            num_scalar_prefetch=1,
            grid=(width // LANES,),
            in_specs=[
                pair_spec(row_count),
                pair_spec(key_count),
                pair_spec(key_count),
                fixed_spec(2 * LANES, LANES),
            ],
            out_specs=[pair_spec(row_count), fixed_spec(row_count, LANES)],
            scratch_shapes=[
                pltpu.VMEM((2, row_count, key_count + 2 * LANES), jnp.float32),
                pltpu.VMEM((2, row_count, key_count), jnp.bfloat16),
                pltpu.VMEM((key_count, LANES), jnp.bfloat16),
            ],
        ),
        out_shape=[
            jax.ShapeDtypeStruct((row_count, width), jnp.bfloat16),
            jax.ShapeDtypeStruct((row_count, LANES), jnp.float32),
        ],
        compiler_params=pltpu.CompilerParams(vmem_limit_bytes=48 * 2**20),
        name="attend",
    )(meta, queries, key_rows, value_rows, table)


def attend_back(meta, queries, key_rows, value_rows, table, grad_context, context, levels):
    row_count, width = queries.shape
    key_count = key_rows.shape[0]
    return pl.pallas_call(
        attend_back_kernel,
        grid_spec=pltpu.PrefetchScalarGridSpec(
            num_scalar_prefetch=1,
            grid=(width // LANES,),
            in_specs=[
                pair_spec(row_count),
                pair_spec(key_count),
                pair_spec(key_count),
                fixed_spec(2 * LANES, LANES),
                pair_spec(row_count),
                pair_spec(row_count),
                fixed_spec(row_count, LANES),
            ],
            out_specs=[
                pair_spec(row_count),
                pair_spec(key_count),
                pair_spec(key_count),
                fixed_spec(LANES, 2 * LANES),
            ],
            scratch_shapes=[
                pltpu.VMEM((2, row_count, key_count + 2 * LANES), jnp.float32),
                pltpu.VMEM((2, row_count, key_count), jnp.float32),
                pltpu.VMEM((2, row_count, key_count), jnp.bfloat16),
                pltpu.VMEM((2, row_count, key_count + 2 * LANES), jnp.bfloat16),
                pltpu.VMEM((2, row_count, 2 * LANES), jnp.bfloat16),
                pltpu.VMEM((key_count, 2 * LANES), jnp.bfloat16),
                pltpu.VMEM((2, key_count, LANES), jnp.bfloat16),
            ],
        ),
        out_shape=[
            jax.ShapeDtypeStruct((row_count, width), jnp.bfloat16),
            jax.ShapeDtypeStruct((key_count, width), jnp.bfloat16),
            jax.ShapeDtypeStruct((key_count, width), jnp.bfloat16),
            jax.ShapeDtypeStruct((LANES, 2 * LANES), jnp.float32),
        ],
        compiler_params=pltpu.CompilerParams(vmem_limit_bytes=48 * 2**20),
        name="attend_back",
    )(meta, queries, key_rows, value_rows, table, grad_context, context, levels)


def wide_table(table_low):
    places = jnp.arange(2 * LANES)
    offsets = jnp.clip(jnp.where(places < LANES, places, places - 2 * LANES) + LEFT, 0, OFFSETS - 1)
    rows = table_low[offsets]
    return jnp.concatenate([rows, rows], axis=1)


def table_grad(wide_grad):
    folded = (wide_grad[:HEAD_DIM] + wide_grad[HEAD_DIM:]).T
    first = jnp.sum(folded[LANES : 2 * LANES - LEFT + 1], axis=0, keepdims=True)
    last = jnp.sum(folded[RIGHT:LANES], axis=0, keepdims=True)
    return jnp.concatenate([first, folded[2 * LANES - LEFT + 1 :], folded[:RIGHT], last], axis=0)


def sigmoid(values):
    return 0.5 * jnp.tanh(0.5 * values) + 0.5


def swish_slope(values, logistic):
    return logistic + values * logistic * (1.0 - logistic)


def matmul(left_side, right_side):
    return dot_f32(left_side, right_side, NN)


def norm_rows(values, gain_row, shift_row):
    centred = values - jnp.mean(values, axis=-1, keepdims=True)
    variance = jnp.mean(centred * centred, axis=-1, keepdims=True)
    inverse = lax.rsqrt(variance + EPSILON)
    normal = centred * inverse
    return (normal * gain_row + shift_row, normal, inverse)


def norm_back(grad_out, normal, inverse, gain_row):
    grad_normal = grad_out * gain_row
    grad_in = inverse * (
        grad_normal
        - jnp.mean(grad_normal, axis=-1, keepdims=True)
        - normal * jnp.mean(grad_normal * normal, axis=-1, keepdims=True)
    )
    return (grad_in, jnp.sum(grad_out * normal, axis=0), jnp.sum(grad_out, axis=0))


CHUNK = 64
HALO = 32


def tap_slices(window, offsets):
    length = window.shape[0]
    slices = {}
    for rest in range(8):
        wanted = [offset for offset in offsets if offset % 8 == rest]
        if wanted:
            turned = pltpu.roll(window, length - rest, 0) if rest else window
            for offset in wanted:
                slices[offset] = turned[offset - rest : offset - rest + CHUNK]
    return slices


def convolve_kernel(before_ref, gated_ref, taps_ref, gain_ref, shift_ref, deep_ref, low_ref, padded_ref):
    row_count, width = gated_ref.shape
    lead = HALO - (KERNEL - 1)
    padded_ref[:HALO] = before_ref[...]
    padded_ref[HALO:] = gated_ref[...]

    @pl.loop(0, width // LANES)
    def _(column):
        lanes = pl.ds(pl.multiple_of(column * LANES, LANES), LANES)
        taps = [taps_ref[tap : tap + 1, lanes] for tap in range(KERNEL)]

        @pl.loop(0, row_count // CHUNK)
        def _(chunk):
            first = pl.multiple_of(chunk * CHUNK, CHUNK)
            window = padded_ref[pl.ds(first, CHUNK + HALO), lanes]
            slices = tap_slices(window, [tap + lead for tap in range(KERNEL)])
            total = taps[0] * slices[lead]
            for tap in range(1, KERNEL):
                total = total + taps[tap] * slices[tap + lead]
            deep_ref[pl.ds(first, CHUNK), lanes] = total

    @pl.loop(0, row_count // CHUNK)
    def _(chunk):
        rows = pl.ds(pl.multiple_of(chunk * CHUNK, CHUNK), CHUNK)
        deep_norm, _, _ = norm_rows(deep_ref[rows, :], gain_ref[...], shift_ref[...])
        low_ref[rows, :] = (deep_norm * sigmoid(deep_norm)).astype(jnp.bfloat16)


def convolve(before, gated, taps, gain_row, shift_row):
    shape = gated.shape
    return pl.pallas_call(
        convolve_kernel,
        in_specs=[pl.BlockSpec(memory_space=pltpu.VMEM)] * 5,
        out_specs=[pl.BlockSpec(memory_space=pltpu.VMEM)] * 2,
        out_shape=[
            jax.ShapeDtypeStruct(shape, jnp.float32),
            jax.ShapeDtypeStruct(shape, jnp.bfloat16),
        ],
        scratch_shapes=[pltpu.VMEM((shape[0] + HALO, shape[1]), jnp.float32)],
        compiler_params=pltpu.CompilerParams(vmem_limit_bytes=32 * 2**20),
        name="convolve",
    )(before, gated, taps, gain_row[None], shift_row[None])


def convolve_back_kernel(
    meta_ref, grad_ref, after_ref, before_ref, gated_ref, taps_ref, linear_ref, logistic_ref,
    pair_ref, tap_grad_ref, padded_ref, extended_ref,
):
    row_count, width = gated_ref.shape
    lead = HALO - (KERNEL - 1)
    padded_ref[:HALO] = before_ref[...]
    padded_ref[HALO:] = gated_ref[...]
    extended_ref[:row_count] = grad_ref[...]
    extended_ref[row_count:] = after_ref[...]
    live_rows = meta_ref[1] - meta_ref[0] * LANES

    @pl.loop(0, width // LANES)
    def _(column):
        start = pl.multiple_of(column * LANES, LANES)
        lanes = pl.ds(start, LANES)
        taps = [taps_ref[tap : tap + 1, lanes] for tap in range(KERNEL)]

        @pl.loop(0, row_count // CHUNK)
        def _(chunk):
            first = pl.multiple_of(chunk * CHUNK, CHUNK)
            rows = pl.ds(first, CHUNK)
            window = extended_ref[pl.ds(first, CHUNK + HALO), lanes]
            slices = tap_slices(window, [KERNEL - 1 - tap for tap in range(KERNEL)])
            total = taps[0] * slices[KERNEL - 1]
            for tap in range(1, KERNEL):
                total = total + taps[tap] * slices[KERNEL - 1 - tap]
            places = first + lax.broadcasted_iota(jnp.int32, (CHUNK, LANES), 0)
            logistic = logistic_ref[rows, lanes]
            grad_linear = jnp.where(places < live_rows, total, 0.0) * logistic
            pair_ref[rows, lanes] = grad_linear.astype(jnp.bfloat16)
            grad_gate = grad_linear * linear_ref[rows, lanes] * (1.0 - logistic)
            gate_lanes = pl.ds(pl.multiple_of(width + start, LANES), LANES)
            pair_ref[rows, gate_lanes] = grad_gate.astype(jnp.bfloat16)

        def tap_step(chunk, totals):
            first = pl.multiple_of(chunk * CHUNK, CHUNK)
            window = padded_ref[pl.ds(first, CHUNK + HALO), lanes]
            slices = tap_slices(window, [tap + lead for tap in range(KERNEL)])
            grad = extended_ref[pl.ds(first, CHUNK), lanes]
            added_up = []
            for tap in range(KERNEL):
                product = slices[tap + lead] * grad
                part = product[:8]
                for piece in range(1, CHUNK // 8):
                    part = part + product[8 * piece : 8 * piece + 8]
                added_up.append(totals[tap] + part)
            return tuple(added_up)

        zero = jnp.zeros((8, LANES), jnp.float32)
        totals = lax.fori_loop(0, row_count // CHUNK, tap_step, (zero,) * KERNEL)
        for tap in range(KERNEL):
            tap_grad_ref[tap : tap + 1, lanes] = jnp.sum(totals[tap], axis=0, keepdims=True)


def convolve_back(meta, grad_depth, after, before, gated, taps, linear, logistic):
    row_count, width = gated.shape
    vmem = pl.BlockSpec(memory_space=pltpu.VMEM)
    return pl.pallas_call(
        convolve_back_kernel,
        grid_spec=pltpu.PrefetchScalarGridSpec(
            num_scalar_prefetch=1,
            grid=(),
            in_specs=[vmem] * 7,
            out_specs=[vmem] * 2,
            scratch_shapes=[pltpu.VMEM((row_count + HALO, width), jnp.float32)] * 2,
        ),
        out_shape=[
            jax.ShapeDtypeStruct((row_count, 2 * width), jnp.bfloat16),
            jax.ShapeDtypeStruct(taps.shape, jnp.float32),
        ],
        compiler_params=pltpu.CompilerParams(vmem_limit_bytes=40 * 2**20),
        name="convolve_back",
    )(meta, grad_depth, after, before, gated, taps, linear, logistic)


def fence(*values):
    return lax.optimization_barrier(values)


TENSOR = ("far", "z")


class Place:
    def __init__(self):
        axes = ("y", "x", "core", "far", "z")
        self.count = {axis: lax.axis_size(axis) for axis in axes}
        self.index = {axis: lax.axis_index(axis) for axis in axes}
        count, index = self.count, self.index
        count["t"] = count["far"] * count["z"]
        index["t"] = index["far"] * count["z"] + index["z"]
        count["seq"] = count["far"] * 2
        index["seq"] = index["far"] * 2 + index["core"]
        count["a"], count["b"] = count["x"], count["y"]
        self.mixed = count["x"] == count["y"]
        self.names = {"t": TENSOR, "seq": ("core", "far")}
        self.dp_count = count["y"] * count["x"] * 2

    def seq_pair(self, start, end):
        far = self.count["far"]
        return ((start % 2) * far + start // 2, (end % 2) * far + end // 2)

    def turn(self, block, axis, step):
        size = self.count[axis]
        pairs = [(start, (start + step) % size) for start in range(size)]
        if axis == "seq":
            pairs = [self.seq_pair(*pair) for pair in pairs]
        if axis in ("a", "b"):
            y_count, x_count = self.count["y"], self.count["x"]
            pairs = []
            for y in range(y_count):
                for x in range(x_count):
                    for core in range(2):
                        along_x = (axis == "a") != (self.mixed and core == 1)
                        new_y = y if along_x else (y + step) % y_count
                        new_x = (x + step) % x_count if along_x else x
                        pairs.append(
                            ((y * x_count + x) * 2 + core, (new_y * x_count + new_x) * 2 + core)
                        )
            return lax.ppermute(block, ("y", "x", "core"), pairs)
        return lax.ppermute(block, self.names.get(axis, axis), pairs)

    def after(self, axis, step):
        return lax.rem(self.index[axis] + step, self.count[axis])

    def blocks_for(self, core):
        y_count, x_count = self.count["y"], self.count["x"]
        numbers = []
        for b_step in [*self.steps("b"), 0]:
            for a_step in [*self.steps("a"), 0]:
                y = lax.rem(self.index["y"] + b_step, y_count)
                x = lax.rem(self.index["x"] + a_step, x_count)
                if self.mixed:
                    y = jnp.where(core == 1, lax.rem(self.index["y"] + a_step, y_count), y)
                    x = jnp.where(core == 1, lax.rem(self.index["x"] + b_step, x_count), x)
                numbers.append((y * x_count + x) * 2 + core)
        return numbers

    def steps(self, axis):
        return range(1, self.count[axis])


def packed(shard):
    rows, columns = shard.shape
    blocks = shard.reshape(rows // columns, columns, columns)
    return blocks.transpose(1, 0, 2).reshape(columns, rows)


def gather_t(place, shard):
    return lax.all_gather(shard, TENSOR, axis=0)


def gather_a(place, stack):
    return jnp.concatenate([stack] + [place.turn(stack, "a", step) for step in place.steps("a")])


def gather_b(place, stack):
    return [stack] + [place.turn(stack, "b", step) for step in place.steps("b")]


def gather_core(place, stacks):
    return stacks + [place.turn(stack, "core", 1) for stack in stacks]


def assemble(place, stacks, targets):
    counts, dp_count, t_count = place.count, place.dp_count, place.count["t"]
    dtype = stacks[0].dtype
    shard_shape = stacks[0].shape[1:]
    rows, columns = shard_shape[-2:]
    shapes, copy_counts = [], 0
    for target in targets:
        if target[0] == "rows":
            shapes.append((target[2], target[3] * dp_count, columns * t_count))
            copy_counts += dp_count * t_count
        elif target[0] == "columns":
            aligned = columns % LANES == 0
            shape = (rows * t_count, columns * dp_count)
            shapes.append(shape if aligned else (dp_count, rows * t_count, columns))
            copy_counts += dp_count * t_count
        elif target[0] == "packed":
            aligned = rows % LANES == 0
            shape = (columns * t_count, rows * dp_count)
            shapes.append(shape if aligned else (dp_count, t_count, rows, columns))
            copy_counts += dp_count * t_count * (columns // rows if aligned else 1)
        else:
            shapes.append((dp_count, target[2], columns))
            copy_counts += dp_count

    def kernel(meta_ref, *refs):
        stack_refs = refs[: len(stacks)]
        out_refs = refs[len(stacks) : len(stacks) + len(targets)]
        sem = refs[-1]
        copies = []

        def send(source, target):
            copy = pltpu.make_async_copy(source, target, sem.at[len(copies)])
            copy.start()
            copies.append(copy)

        b_count = counts["b"]
        for number, stack_ref in enumerate(stack_refs):
            other, b_step = number // b_count, number % b_count
            core = lax.rem(meta_ref[2] + other, 2)
            for a_step in range(counts["a"]):
                y_spot = lax.rem(meta_ref[0] - b_step + counts["y"], counts["y"])
                x_spot = lax.rem(meta_ref[1] - a_step + counts["x"], counts["x"])
                if place.mixed:
                    y_other = lax.rem(meta_ref[0] - a_step + counts["y"], counts["y"])
                    x_other = lax.rem(meta_ref[1] - b_step + counts["x"], counts["x"])
                    y_spot = jnp.where(core == 1, y_other, y_spot)
                    x_spot = jnp.where(core == 1, x_other, x_spot)
                dp_spot = (y_spot * counts["x"] + x_spot) * 2 + core
                for t_step in range(t_count):
                    t_spot = t_step
                    shard_ref = stack_ref.at[a_step * t_count + t_step]
                    for target, out_ref in zip(targets, out_refs):
                        t_columns = pl.ds(pl.multiple_of(t_spot * columns, columns), columns)
                        if target[0] == "rows":
                            first, depth, count = target[1:]
                            source = shard_ref.at[first : first + depth, 0:count, :]
                            here = pl.ds(pl.multiple_of(dp_spot * count, count), count)
                            send(source, out_ref.at[:, here, t_columns])
                        elif target[0] == "columns":
                            here = pl.ds(pl.multiple_of(t_spot * rows, rows), rows)
                            if columns % LANES == 0:
                                there = pl.ds(pl.multiple_of(dp_spot * columns, columns), columns)
                                send(shard_ref, out_ref.at[here, there])
                            else:
                                send(shard_ref, out_ref.at[dp_spot, here, :])
                        elif target[0] == "packed":
                            if rows % LANES == 0:
                                there = pl.ds(pl.multiple_of(dp_spot * rows, rows), rows)
                                for part in range(columns // rows):
                                    here = pl.ds(
                                        pl.multiple_of(t_spot * columns + part * rows, rows), rows
                                    )
                                    send(
                                        shard_ref.at[target[1], :, part * rows : (part + 1) * rows],
                                        out_ref.at[here, there],
                                    )
                            else:
                                send(shard_ref.at[target[1]], out_ref.at[dp_spot, t_spot])
                        elif t_step == 0:
                            first_row, count = target[1:]
                            send(shard_ref.at[0, first_row : first_row + count, :], out_ref.at[dp_spot])
        for copy in copies:
            copy.wait()

    meta = jnp.stack([place.index[axis] for axis in ("y", "x", "core", "t")]).astype(jnp.int32)
    results = pl.pallas_call(
        kernel,
        grid_spec=pltpu.PrefetchScalarGridSpec(
            num_scalar_prefetch=1,
            grid=(),
            in_specs=[pl.BlockSpec(memory_space=pl.ANY)] * len(stacks),
            out_specs=[pl.BlockSpec(memory_space=pltpu.VMEM)] * len(targets),
            scratch_shapes=[pltpu.SemaphoreType.DMA((copy_counts,))],
        ),
        out_shape=[jax.ShapeDtypeStruct(shape, dtype) for shape in shapes],
        compiler_params=pltpu.CompilerParams(vmem_limit_bytes=20 * 2**20),
        name="assemble",
    )(meta, *stacks)
    finished = []
    for target, whole in zip(targets, results):
        if target[0] == "columns" and columns % LANES:
            whole = whole.transpose(1, 0, 2).reshape(rows * t_count, columns * dp_count)
        if target[0] == "packed" and rows % LANES:
            whole = whole.reshape(dp_count, t_count, rows, columns // rows, rows)
            whole = whole.transpose(1, 3, 2, 0, 4).reshape(columns * t_count, rows * dp_count)
        finished.append(whole)
    return finished


def sent_order(place, width):
    core = place.index["core"]
    numbers = jnp.stack(place.blocks_for(1 - core) + place.blocks_for(core))
    block = width // place.dp_count
    sources = (numbers[:, None] * block + jnp.arange(block)[None, :]).reshape(1, width)
    return (jnp.arange(width)[:, None] == sources).astype(jnp.bfloat16)


def reduce_core(place, pairs):
    group = []
    for inputs, grads in pairs:
        half = inputs.shape[1] // 2
        product = dot_f32(inputs[:, :half], grads, TN).astype(jnp.bfloat16)
        group.append((inputs, grads, place.turn(product, "core", 1)))
    return group


def reduce_b(place, group):
    result = []
    for inputs, grads, other in group:
        half = inputs.shape[1] // 2
        step_rows = half // place.count["b"]
        arrived = []
        for number, step in enumerate([*place.steps("b"), 0]):
            columns = slice(half + number * step_rows, half + (number + 1) * step_rows)
            rows = slice(number * step_rows, (number + 1) * step_rows)
            term = dot_f32(inputs[:, columns], grads, TN) + other[rows].astype(jnp.float32)
            term = term.astype(jnp.bfloat16)
            arrived.append(term if step == 0 else place.turn(term, "b", step))
        result.append(arrived)
    return result


def added(arrays):
    total = arrays[0].astype(jnp.float32)
    for array in arrays[1:]:
        total = total + array.astype(jnp.float32)
    return total


def reduce_a(place, group):
    result = []
    for arrived in group:
        step_rows = arrived[0].shape[0] // place.count["a"]
        kept = []
        for number, step in enumerate([*place.steps("a"), 0]):
            rows = slice(number * step_rows, (number + 1) * step_rows)
            mine = [one[rows] for one in arrived]
            if step == 0:
                kept += mine
            else:
                kept.append(place.turn(added(mine).astype(mine[0].dtype), "a", step))
        result.append(kept)
    return result


def by_tensor(total, count):
    width = total.shape[1] // count
    return [total[:, number * width : (number + 1) * width] for number in range(count)]


def reduce_t(place, group):
    count = place.count["t"]
    blocks = [[] for _ in range(count)]
    for depth, kept in group:
        total = added(kept).astype(jnp.bfloat16)
        for part in by_tensor(total, depth):
            for number, block in enumerate(by_tensor(part, count)):
                blocks[number].append(block)
    stack = jnp.stack([jnp.stack(block) for block in blocks])
    return lax.psum_scatter(stack, TENSOR, scatter_dimension=0)


def reduce_t_vectors(place, kept, vectors):
    count = place.count["t"]
    total = added(kept).astype(jnp.bfloat16)
    vector_count, columns = vectors.shape[0], total.shape[1] // count
    extra_rows = -(-vectors.size // (count * columns) // 16) * 16 if vectors.size else 0
    extra_rows = max(extra_rows, 16)
    width = vectors.shape[1] // count
    blocks = []
    for block, part in zip(by_tensor(total, count), by_tensor(vectors, count)):
        flat = part.astype(jnp.bfloat16).reshape(1, -1)
        flat = jnp.pad(flat, ((0, 0), (0, extra_rows * columns - flat.shape[1])))
        blocks.append(jnp.concatenate([block, flat.reshape(extra_rows, columns)]))
    result = lax.psum_scatter(jnp.stack(blocks), TENSOR, scatter_dimension=0)
    flat = result[-extra_rows:].reshape(-1)[: vector_count * width]
    return (result[:-extra_rows], flat.reshape(vector_count, width).astype(jnp.float32))


def reduce_vectors_core(place, columns):
    half = columns.shape[1] // 2
    total = columns[:, half:] + place.turn(columns[:, :half], "core", 1)
    return total


def reduce_vectors(place, total, axis):
    width = total.shape[1] // place.count[axis]
    arrived = total[:, -width:]
    for number, step in enumerate(place.steps(axis)):
        arrived = arrived + place.turn(total[:, number * width : (number + 1) * width], axis, step)
    return arrived


def clip_pairs(micro, z_count, step):
    return [
        (core * z_count + z, (z // micro) * z_count + micro * core + (step + z) % micro)
        for core in range(2)
        for z in range(z_count)
    ]


def to_clip(place, blocks):
    micro, z_count = blocks.shape[0], place.count["z"]
    z_here = place.index["z"]
    arrived = []
    for step in range(micro):
        block = lax.dynamic_index_in_dim(blocks, lax.rem(z_here + step, micro), 0, keepdims=False)
        arrived.append(lax.ppermute(block, ("core", "z"), clip_pairs(micro, z_count, step)))
    return arrived


def ordered_clip(place, arrived):
    micro, z_here = len(arrived), place.index["z"]
    stack = jnp.stack(arrived)
    ordered = [
        lax.dynamic_index_in_dim(stack, lax.rem(z_here - spot + micro, micro), 0, keepdims=False)
        for spot in range(micro)
    ]
    return jnp.concatenate(ordered, axis=0)


def from_clip(place, rows_in, micro):
    z_count, z_here = place.count["z"], place.index["z"]
    blocks = rows_in.reshape(micro, -1, rows_in.shape[-1])
    arrived = []
    for step in range(micro):
        spot = lax.rem(z_here - step + micro, micro)
        block = lax.dynamic_index_in_dim(blocks, spot, 0, keepdims=False)
        pairs = [(end, start) for start, end in clip_pairs(micro, z_count, step)]
        arrived.append(lax.ppermute(block, ("core", "z"), pairs))
    return arrived


def own_clips(place, arrived):
    micro, z_here = len(arrived), place.index["z"]
    stack = jnp.stack(arrived)
    return jnp.stack(
        [
            lax.dynamic_index_in_dim(
                stack, lax.rem(number - lax.rem(z_here, micro) + micro, micro), 0, keepdims=False
            )
            for number in range(micro)
        ]
    )


def all_rows(place, own):
    count = place.count["seq"]
    whole = jnp.zeros((count,) + own.shape, own.dtype)
    for step in range(count):
        block = own if step == 0 else place.turn(own, "seq", step)
        spot = lax.rem(place.index["seq"] - step + count, count)
        whole = lax.dynamic_update_index_in_dim(whole, block, spot, 0)
    return whole.reshape((count * own.shape[0],) + own.shape[1:])


def own_sum(place, partial):
    count = place.count["seq"]
    blocks = partial.reshape(count, -1, partial.shape[-1])
    total = lax.dynamic_index_in_dim(blocks, place.index["seq"], 0, keepdims=False).astype(jnp.float32)
    for step in range(1, count):
        message = lax.dynamic_index_in_dim(blocks, place.after("seq", step), 0, keepdims=False)
        total = total + place.turn(message, "seq", step).astype(jnp.float32)
    return total


def neighbour_rows(place, rows_in, step):
    count = place.count["seq"]
    pairs = [
        place.seq_pair(start, start + step) for start in range(count) if 0 <= start + step < count
    ]
    return lax.ppermute(rows_in, place.names["seq"], pairs)


def feed_up(inputs, up_weight, up_bias, gain_row, shift_row):
    normed, normal, inverse = norm_rows(inputs, gain_row, shift_row)
    normed = normed.astype(jnp.bfloat16)
    upper_rows = matmul(normed, up_weight) + up_bias
    logistic = sigmoid(upper_rows)
    hidden = (upper_rows * logistic).astype(jnp.bfloat16)
    slope = swish_slope(upper_rows, logistic).astype(jnp.bfloat16)
    return (hidden, (normal, inverse, normed, slope))


def feed_back_down(grad_result, stored, down_weight):
    grad_low = grad_result.astype(jnp.bfloat16)
    grad_hidden = dot_f32(grad_low, down_weight, NT)
    grad_upper = (grad_hidden * stored[3].astype(jnp.float32)).astype(jnp.bfloat16)
    up_bias_grad = jnp.sum(grad_upper.astype(jnp.float32), axis=0)
    down_bias_grad = jnp.sum(grad_low.astype(jnp.float32), axis=0)
    return (grad_low, grad_upper, up_bias_grad, down_bias_grad)


def body(
    frames,
    cotangent,
    clip_valid,
    frame_counts,
    rel_rows,
    first_up,
    first_down,
    attend_in,
    attend_out,
    pointwise_in,
    pointwise_out,
    second_up,
    second_down,
    vectors,
    distance,
):
    place = Place()
    micro, _, width = frames.shape
    ratio_rows = FF // width
    attend_base = 3 + ratio_rows
    conv_base = attend_base + 5
    second_base = conv_base + 4
    final_base = second_base + 3 + ratio_rows
    taps_base = final_base + 2
    scale = HEAD_DIM ** (-0.5)
    order = sent_order(place, width)

    def sent(rows_low):
        return matmul(rows_low, order).astype(jnp.bfloat16)

    up_rows, up_columns = first_up.shape
    vector_rows = 16
    vector_parts = up_columns // vectors.shape[1]
    padded_vectors = jnp.pad(vectors, ((0, vector_rows * vector_parts - vectors.shape[0]), (0, 0)))
    vector_shard = (
        padded_vectors.reshape(vector_parts, vector_rows, -1).transpose(1, 0, 2).reshape(vector_rows, -1)
    )
    shard_up_one = jnp.concatenate([first_up, vector_shard], axis=0)[None]
    shard_mix = jnp.concatenate(
        [attend_in, packed(attend_out)[None], pointwise_in, packed(pointwise_out)[None]]
    )

    own_facts = jnp.stack([clip_valid, frame_counts])
    up_one = gather_t(place, shard_up_one)
    up_one, first_down, own_facts = fence(up_one, first_down, own_facts)
    up_one = gather_a(place, up_one)
    down_one = gather_t(place, first_down)
    other_facts = place.turn(own_facts, "core", 1)
    up_one, frames, shard_mix = fence(up_one, frames, shard_mix)
    up_one = gather_b(place, up_one)
    rows_low = to_clip(place, frames)
    down_one = gather_a(place, down_one)
    both_mix = gather_t(place, shard_mix)
    up_one, down_one, second_up = fence(up_one, down_one, second_up)
    up_one = gather_core(place, up_one)
    down_one = gather_b(place, down_one)
    attend_mix = gather_a(place, both_mix[:, : attend_in.shape[0] + 1])
    point_mix = both_mix[:, attend_in.shape[0] + 1 :]
    up_two = gather_t(place, second_up[None])
    up_one, vector_slabs = assemble(
        place, up_one, [("rows", 0, 1, up_rows), ("slabs", up_rows, vector_rows)]
    )
    up_one = up_one[0]
    vector_wide = vector_slabs.reshape(place.dp_count, vector_rows, vector_parts, -1)
    vector_wide = vector_wide.transpose(2, 1, 0, 3).reshape(vector_rows * vector_parts, width)
    vector_wide = vector_wide[: vectors.shape[0]].astype(jnp.float32)

    rows_in = ordered_clip(place, rows_low).astype(jnp.float32)
    row_count = rows_in.shape[0]
    z_here = place.index["z"]
    facts = jnp.where(z_here // micro == place.index["core"], own_facts, other_facts)
    facts = lax.dynamic_index_in_dim(facts, lax.rem(z_here, micro), 1, keepdims=False)
    valid_flag = (facts[0] > 0).astype(jnp.float32)
    first_row = place.index["seq"] * row_count
    live = ((first_row + jnp.arange(row_count)) < facts[1]).astype(jnp.float32)[:, None]
    meta = jnp.stack([place.index["seq"] * (row_count // LANES), facts[1]]).astype(jnp.int32)
    pick_rows = (rel_rows[:, None] == jnp.arange(OFFSETS)[None, :]).astype(jnp.bfloat16)
    table = wide_table(matmul(pick_rows, distance).astype(jnp.bfloat16))

    one_hidden, one_kept = feed_up(
        rows_in,
        up_one,
        vector_wide[2 : 2 + ratio_rows].reshape(FF),
        vector_wide[0],
        vector_wide[1],
    )
    (down_one, attend_mix, point_mix, second_down, one_hidden, one_kept, up_one, table) = fence(
        down_one, attend_mix, point_mix, second_down, one_hidden, one_kept, up_one, table
    )
    down_one = gather_core(place, down_one)
    attend_mix = gather_b(place, attend_mix)
    point_mix = gather_a(place, point_mix)
    down_two = gather_t(place, second_down)
    (down_one,) = assemble(place, down_one, [("columns",)])
    after_one = rows_in + 0.5 * (matmul(one_hidden, down_one) + vector_wide[2 + ratio_rows])
    attend_normed, attend_normal, attend_inverse = norm_rows(
        after_one, vector_wide[attend_base], vector_wide[attend_base + 1]
    )
    attend_normed = attend_normed.astype(jnp.bfloat16)
    (attend_mix, point_mix, up_two, after_one, attend_normed, attend_normal, attend_inverse) = fence(
        attend_mix, point_mix, up_two, after_one, attend_normed, attend_normal, attend_inverse
    )
    attend_mix = gather_core(place, attend_mix)
    point_mix = gather_b(place, point_mix)
    up_two = gather_a(place, up_two)
    attend_mix, attend_back_weight = assemble(place, attend_mix, [("rows", 0, 3, up_rows), ("packed", 3)])
    queries = (matmul(attend_normed, attend_mix[0]) + vector_wide[attend_base + 2]).astype(jnp.bfloat16)
    queries = (queries.astype(jnp.float32) * scale).astype(jnp.bfloat16)
    own_keys = matmul(attend_normed, attend_mix[1]).astype(jnp.bfloat16)
    own_values = (matmul(attend_normed, attend_mix[2]) + vector_wide[attend_base + 3]).astype(jnp.bfloat16)
    key_rows, value_rows = all_rows(place, own_keys), all_rows(place, own_values)
    (point_mix, up_two, down_two, cotangent, queries, key_rows, value_rows) = fence(
        point_mix, up_two, down_two, cotangent, queries, key_rows, value_rows
    )
    point_mix = gather_core(place, point_mix)
    up_two = gather_b(place, up_two)
    down_two = gather_a(place, down_two)
    cot_low = to_clip(place, cotangent)
    context, levels = attend(meta, queries, key_rows, value_rows, table)
    (point_mix, up_two, down_two, context, levels, after_one) = fence(
        point_mix, up_two, down_two, context, levels, after_one
    )
    down_two = gather_b(place, down_two)
    up_two = gather_core(place, up_two)
    point_mix, point_back = assemble(place, point_mix, [("rows", 0, 2, up_rows), ("packed", 2)])
    after_two = after_one + matmul(context, attend_back_weight) + vector_wide[attend_base + 4]
    conv_normed, conv_normal, conv_inverse = norm_rows(
        after_two, vector_wide[conv_base], vector_wide[conv_base + 1]
    )
    conv_normed = conv_normed.astype(jnp.bfloat16)
    linear = matmul(conv_normed, point_mix[0])
    logistic = sigmoid(matmul(conv_normed, point_mix[1]))
    gated = linear * logistic * live
    taps = vector_wide[taps_base : taps_base + KERNEL]
    before = neighbour_rows(place, gated[-HALO:], 1)
    deep_gain, deep_shift = vector_wide[conv_base + 2], vector_wide[conv_base + 3]
    depth_out, activated = convolve(before, gated, taps, deep_gain, deep_shift)
    after_three = after_two + matmul(activated, point_back)
    (up_two, down_two, cot_low, after_three, depth_out, activated) = fence(
        up_two, down_two, cot_low, after_three, depth_out, activated
    )
    down_two = gather_core(place, down_two)
    (up_two,) = assemble(place, up_two, [("rows", 0, 1, up_rows)])
    up_two = up_two[0]
    two_hidden, two_kept = feed_up(
        after_three,
        up_two,
        vector_wide[second_base + 2 : second_base + 2 + ratio_rows].reshape(FF),
        vector_wide[second_base],
        vector_wide[second_base + 1],
    )
    (down_two, two_hidden, two_kept, up_two) = fence(down_two, two_hidden, two_kept, up_two)
    (down_two,) = assemble(place, down_two, [("columns",)])
    two_out = matmul(two_hidden, down_two) + vector_wide[second_base + 2 + ratio_rows]
    after_four = after_three + 0.5 * two_out
    final_rows, final_normal, final_inverse = norm_rows(
        after_four, vector_wide[final_base], vector_wide[final_base + 1]
    )
    row_out = jnp.where(valid_flag > 0, final_rows, rows_in).astype(jnp.bfloat16)
    rows_cot = ordered_clip(place, cot_low).astype(jnp.float32)
    grad_four, final_gain_grad, final_shift_grad = norm_back(
        rows_cot * valid_flag, final_normal, final_inverse, vector_wide[final_base]
    )
    grad_low, grad_upper, two_up_bias, two_down_bias = feed_back_down(
        0.5 * grad_four, two_kept, down_two
    )
    sum_down_two = reduce_core(place, [(sent(grad_low), two_hidden)])
    (sum_down_two, grad_four, grad_upper, row_out) = fence(sum_down_two, grad_four, grad_upper, row_out)
    sum_down_two = reduce_b(place, sum_down_two)
    frames_out = from_clip(place, row_out, micro)
    sum_up_two = reduce_core(place, [(sent(two_kept[2]), grad_upper)])
    grad_normed = dot_f32(grad_upper, up_two, NT)
    grad_two_in, two_gain, two_shift = norm_back(
        grad_normed, two_kept[0], two_kept[1], vector_wide[second_base]
    )
    grad_three = grad_four + grad_two_in
    conv_low = grad_three.astype(jnp.bfloat16)
    deep_norm, deep_normal, deep_inverse = norm_rows(depth_out, deep_gain, deep_shift)
    grad_deep = dot_f32(conv_low, point_back, NT) * swish_slope(deep_norm, sigmoid(deep_norm))
    grad_depth, deep_gain_grad, deep_shift_grad = norm_back(
        grad_deep, deep_normal, deep_inverse, deep_gain
    )
    after = neighbour_rows(place, grad_depth[:HALO], -1)
    (sum_down_two, sum_up_two, grad_three, conv_low, grad_depth, after, frames_out) = fence(
        sum_down_two, sum_up_two, grad_three, conv_low, grad_depth, after, frames_out
    )
    sum_down_two = reduce_a(place, sum_down_two)
    sum_up_two = reduce_b(place, sum_up_two)
    grad_pair, tap_grads = convolve_back(
        meta, grad_depth, after, before, gated, taps, linear, logistic
    )
    (sum_down_two, sum_up_two, grad_pair) = fence(sum_down_two, sum_up_two, grad_pair)
    sum_down_two = reduce_t(place, [(1, sum_down_two[0])])
    sum_up_two = reduce_a(place, sum_up_two)
    sum_point = reduce_core(
        place,
        [
            (sent(conv_normed), grad_pair),
            (sent(conv_low), activated),
        ],
    )
    grad_conv_normed = dot_f32(grad_pair[:, :width], point_mix[0], NT)
    grad_conv_normed = grad_conv_normed + dot_f32(grad_pair[:, width:], point_mix[1], NT)
    grad_conv_in, conv_gain_grad, conv_shift_grad = norm_back(
        grad_conv_normed, conv_normal, conv_inverse, vector_wide[conv_base]
    )
    grad_two = grad_three + grad_conv_in
    attend_low = grad_two.astype(jnp.bfloat16)
    grad_context = dot_f32(attend_low, attend_back_weight, NT).astype(jnp.bfloat16)
    (sum_up_two, sum_point, grad_two, attend_low, grad_context) = fence(
        sum_up_two, sum_point, grad_two, attend_low, grad_context
    )
    sum_up_two = reduce_t(place, [(1, sum_up_two[0])])
    sum_point = reduce_b(place, sum_point)
    grad_queries, part_keys, part_values, grad_table = attend_back(
        meta, queries, key_rows, value_rows, table, grad_context, context, levels
    )
    (sum_point, grad_queries, part_keys, part_values, grad_table) = fence(
        sum_point, grad_queries, part_keys, part_values, grad_table
    )
    sum_point = reduce_a(place, sum_point)
    grad_keys = own_sum(place, part_keys).astype(jnp.bfloat16)
    grad_values = own_sum(place, part_values).astype(jnp.bfloat16)
    sum_distance = jnp.dot(
        pick_rows.astype(jnp.float32).T, table_grad(grad_table), precision=lax.Precision.HIGHEST
    )
    sum_distance = sum(
        (place.turn(sum_distance, "t", step) for step in place.steps("t")), sum_distance
    )
    sum_attend = reduce_core(
        place,
        [
            (
                sent(attend_normed),
                jnp.concatenate([grad_queries, grad_keys, grad_values], axis=1),
            ),
            (sent(attend_low), context),
        ],
    )
    grad_attend_normed = (
        dot_f32(grad_queries, attend_mix[0], NT)
        + dot_f32(grad_keys, attend_mix[1], NT)
        + dot_f32(grad_values, attend_mix[2], NT)
    )
    grad_attend_in, attend_gain_grad, attend_shift_grad = norm_back(
        grad_attend_normed, attend_normal, attend_inverse, vector_wide[attend_base]
    )
    grad_one = grad_two + grad_attend_in
    (sum_point, sum_attend, sum_distance, grad_one) = fence(sum_point, sum_attend, sum_distance, grad_one)
    sum_point = reduce_t(place, [(2, sum_point[0]), (1, sum_point[1])])
    sum_attend = reduce_b(place, sum_attend)
    sum_distance = sum_distance + place.turn(sum_distance, "core", 1)
    grad_low, grad_upper, one_up_bias, one_down_bias = feed_back_down(0.5 * grad_one, one_kept, down_one)
    sum_down_one = reduce_core(place, [(sent(grad_low), one_hidden)])
    sum_up_one = reduce_core(place, [(sent(one_kept[2]), grad_upper)])
    (sum_attend, sum_down_one, sum_up_one, grad_upper) = fence(
        sum_attend, sum_down_one, sum_up_one, grad_upper
    )
    sum_down_one = reduce_b(place, sum_down_one)
    sum_attend = reduce_a(place, sum_attend)
    sum_up_one = reduce_b(place, sum_up_one)
    sum_distance = sum(
        (place.turn(sum_distance, "b", step) for step in place.steps("b")), sum_distance
    )
    grad_normed = dot_f32(grad_upper, up_one, NT)
    grad_one_in, one_gain, one_shift = norm_back(grad_normed, one_kept[0], one_kept[1], vector_wide[0])
    grad_rows = grad_one + grad_one_in + (1.0 - valid_flag) * rows_cot

    def column_sum(rows):
        return jnp.sum(rows.astype(jnp.float32), axis=0)

    vector_part = jnp.concatenate(
        [
            jnp.stack([one_gain, one_shift]),
            one_up_bias.reshape(ratio_rows, width),
            jnp.stack(
                [
                    one_down_bias,
                    attend_gain_grad,
                    attend_shift_grad,
                    column_sum(grad_queries),
                    column_sum(grad_values),
                    column_sum(attend_low),
                    conv_gain_grad,
                    conv_shift_grad,
                    deep_gain_grad,
                    deep_shift_grad,
                    two_gain,
                    two_shift,
                ]
            ),
            two_up_bias.reshape(ratio_rows, width),
            jnp.stack([two_down_bias, final_gain_grad, final_shift_grad]),
            tap_grads[:KERNEL],
        ],
        axis=0,
    )
    grad_rows = grad_rows.astype(jnp.bfloat16)
    vector_part = jnp.dot(vector_part, order.astype(jnp.float32), precision=lax.Precision.HIGHEST)
    (sum_attend, sum_down_one, sum_up_one, vector_part, grad_rows) = fence(
        sum_attend, sum_down_one, sum_up_one, vector_part, grad_rows
    )
    sum_up_one = reduce_a(place, sum_up_one)
    sum_down_one = reduce_a(place, sum_down_one)
    sum_vectors = reduce_vectors_core(place, vector_part)
    sum_attend = reduce_t(place, [(3, sum_attend[0]), (1, sum_attend[1])])
    sum_distance = sum(
        (place.turn(sum_distance, "a", step) for step in place.steps("a")), sum_distance
    )
    frames_grad = from_clip(place, grad_rows, micro)
    (sum_up_one, sum_down_one, sum_vectors) = fence(sum_up_one, sum_down_one, sum_vectors)
    sum_up_one = reduce_t(place, [(1, sum_up_one[0])])
    sum_vectors = reduce_vectors(place, sum_vectors, "b")
    sum_vectors = reduce_vectors(place, sum_vectors, "a")
    sum_down_one, grad_vectors = reduce_t_vectors(place, sum_down_one[0], sum_vectors)
    wide = jnp.float32
    return (
        own_clips(place, frames_out),
        own_clips(place, frames_grad),
        sum_up_one[0].astype(wide),
        sum_down_one.T.astype(wide),
        sum_attend[:3].astype(wide),
        sum_attend[3].T.astype(wide),
        sum_point[:2].astype(wide),
        sum_point[2].T.astype(wide),
        sum_up_two[0].astype(wide),
        sum_down_two[0].T.astype(wide),
        grad_vectors,
        sum_distance,
    )


def solution(mesh):
    dp_count, tensor_count = mesh.shape["dp"], mesh.shape["tensor"]

    def program(*arrays):
        group = 2 * (arrays[0].shape[0] // dp_count)
        parted = Mesh(
            mesh.devices.reshape(dp_count // 4, 2, 2, tensor_count // group, group),
            ("y", "x", "core", "far", "z"),
        )
        dp, tensor = ("y", "x", "core"), TENSOR
        return jax.shard_map(
            body,
            mesh=parted,
            in_specs=(
                P(dp, tensor, None),
                P(dp, tensor, None),
                P(dp),
                P(dp),
                P(),
                P(dp, tensor),
                P(tensor, dp),
                P(None, dp, tensor),
                P(tensor, dp),
                P(None, dp, tensor),
                P(tensor, dp),
                P(dp, tensor),
                P(tensor, dp),
                P(None, dp),
                P(),
            ),
            out_specs=(
                P(dp, tensor, None),
                P(dp, tensor, None),
                P(dp, tensor),
                P(tensor, dp),
                P(None, dp, tensor),
                P(tensor, dp),
                P(None, dp, tensor),
                P(tensor, dp),
                P(dp, tensor),
                P(tensor, dp),
                P(None, dp + tensor),
                P(),
            ),
            check_vma=False,
        )(*arrays)

    return program
```

time: 914 us -> 834 us (0.912)
  starting transfers between devices: 164 us -> 83.4 us
  local copies, waits for them, and re-layouts: 122 us -> 45.7 us
  matrix products: 131 us -> 197 us
  other arithmetic: 168 us -> 107 us
  waiting for transfers between devices: 196 us -> 237 us
  Pallas kernels: 114 us -> 138 us
  between operations: 5.62 us -> 17.7 us
    ppermute x67 -> x30, waiting for transfers between devices: 99.3 us -> 5.52 us  [turn(): return lax.ppermute(block, self.names.get(axis, axis), pairs)]
    ppermute x67 -> x30, starting transfers between devices: 91.9 us -> 22.6 us  [turn(): return lax.ppermute(block, self.names.get(axis, axis), pairs)]
    dot_general x45 -> x55, matrix products: 131 us -> 194 us  [dot_f32(): lax.dot_general(left_side, right_side, dims, preferred_element_type=jnp.f...]
    ppermute x28 -> x32, waiting for transfers between devices: 80 us -> 135 us  [turn(): return lax.ppermute(block, ('y', 'x', 'core'), pairs)]
    all_gather x0 -> x5, waiting for transfers between devices: none -> 51.5 us  [gather_t(): return lax.all_gather(shard, TENSOR, axis=0)]
    dynamic_slice x43 -> x0, local copies, waits for them, and re-layouts: 46.7 us -> none  [the longest x20 31.5 us: pick_t(): return lax.dynamic_slice_in_dim(array, number * width, width, axis=axis)]
    convert_element_type x21 -> x24, other arithmetic: 65.5 us -> 29.4 us  [the longest x8 10.4 us: reduce_a(): kept.append(place.turn(added(mine).astype(mine[0].dtype), 'a', step))]
    pallas_call x0 -> x2, Pallas kernels: none -> 32.7 us  [the longest x1 17.2 us: convolve(): pl.pallas_call(convolve_kernel, in_specs=[pl.BlockSpec(memory_space=pltpu...]
  transfers between devices with their start and end apart: 105 -> 83, of which waited for: 37 -> 30; matrix products, arithmetic and copies ran while one was open for 37% -> 36% of each run, Pallas kernels for 12% -> 16%
where the time goes in v3:
time: 834 us; the launch traced here: 826 us
  waiting for transfers between devices  237 us (28%)
  matrix products  197 us (24%)
  Pallas kernels  138 us (17%)
  other arithmetic  107 us (13%)
  starting transfers between devices  83.4 us (10%)
  local copies, waits for them, and re-layouts  45.7 us (5%)
  between operations  17.7 us (2%)
    dot_general x55, matrix products, dot_f32(): lax.dot_general(left_side, right_side, dims, preferred_element_type=jnp.f...  194 us
    ppermute x32, waiting for transfers between devices, turn(): return lax.ppermute(block, ('y', 'x', 'core'), pairs)  135 us
    pallas_call x1, Pallas kernels, attend_back(): pl.pallas_call(attend_back_kernel, grid_spec=pltpu.PrefetchScalarGridSpec...  53.4 us
    all_gather x5, waiting for transfers between devices, gather_t(): return lax.all_gather(shard, TENSOR, axis=0)  51.5 us
    ppermute x32, starting transfers between devices, turn(): return lax.ppermute(block, ('y', 'x', 'core'), pairs)  43.4 us
    pallas_call x1, Pallas kernels, attend(): pl.pallas_call(attend_kernel, grid_spec=pltpu.PrefetchScalarGridSpec(num_...  26.7 us
    pallas_call x6, Pallas kernels, assemble(): pl.pallas_call(kernel, grid_spec=pltpu.PrefetchScalarGridSpec(num_scalar_...  25.6 us
    reduce_scatter x1, waiting for transfers between devices, reduce_t_vectors(): result = lax.psum_scatter(jnp.stack(blocks), TENSOR, scatter_dimension=0)  24.5 us
  transfers between devices with their start and end apart: 83, of which 30 were waited for; matrix products, arithmetic and copies ran while one was open for 36% of the time, Pallas kernels for 16%

profile of v3, /device:TPU:0, one launch (start us, length us, event | category | flops | bytes accessed | tf_op | source)
XLA Modules:
  0.0 825.7 jit_solution(4980452874465575209)
XLA Ops:
  11.0 32.4 %all-gather.11.cloned.1.call-done = bf16[576,1024]{1,0:T(8,128)(2,1)} async-done(((bf16[144,1024]{1,0:T(8,128)(2,1)}), bf16[576,1024]{1,0:T(8,128)(2,1)}) %all-gather.11.cloned.1.call-update) | async-done | bytes 1179664 | tf_op jit(solution)/shard_map/all_gather | solution.py:612
  48.6 11.2 %collective-permute-done = bf16[4,1,144,1024]{3,2,1,0:T(8,128)(2,1)} collective-permute-done((bf16[4,1,144,1024]{3,2,1,0:T(8,128)(2,1)}, bf16[4,1,144,1024]{3,2,1,0:T(8,128)(2,1)}, u32[]{:S(2)}, u32[]{:S(2)}) %collective-permute-start) | collective-permute-done | bytes 1179680 | tf_op jit(solution)/shard_map/ppermute | solution.py:582
  63.0 9.0 %all-gather.13.cloned.1.call-done = bf16[4096,128]{1,0:T(8,128)(2,1)} async-done(((bf16[1024,128]{1,0:T(8,128)(2,1)}), bf16[4096,128]{1,0:T(8,128)(2,1)}) %all-gather.13.cloned.1.call-update) | async-done | bytes 1048592 | tf_op jit(solution)/shard_map/all_gather | solution.py:612
  73.5 24.8 %collective-permute-done.2 = bf16[4,1024,128]{2,1,0:T(8,128)(2,1)S(1)} collective-permute-done((bf16[4,1024,128]{2,1,0:T(8,128)(2,1)}, bf16[4,1024,128]{2,1,0:T(8,128)(2,1)S(1)}, u32[]{:S(2)}, u32[]{:S(2)}) %collective-permute-start.2) | collective-permute-done | bytes 1048608 | tf_op jit(solution)/shard_map/ppermute | solution.py:582
  107.1 10.1 %all-gather.15.cloned.1.call-done = bf16[28,128,256]{2,1,0:T(8,128)(2,1)} async-done(((bf16[7,128,256]{2,1,0:T(8,128)(2,1)}), bf16[28,128,256]{2,1,0:T(8,128)(2,1)}) %all-gather.15.cloned.1.call-update) | async-done | bytes 1835024 | tf_op jit(solution)/shard_map/all_gather | solution.py:612
  141.6 8.5 %add_convert_fusion.1 = (bf16[512,4096]{1,0:T(8,128)(2,1)}, bf16[512,4096]{1,0:T(8,128)(2,1)}) fusion(f32[4096]{0:T(1024)S(1)} %bitcast.499, bf16[512,1024]{1,0:T(8,128)(2,1)S(1)} %get-tuple-element.307, bf16[1,1024,4096]{2,1,0:T(8,128)(2,1)S(1)} %get-tuple-element.193), kind=kOutput, calls=%fused_computation.9 | convolution fusion | flops 4315938816 | bytes 17842176 | tf_op jit(solution)/shard_map/dot_general | solution.py:27
  163.1 16.5 %collective-permute-done.10 = bf16[4,3,128,256]{3,2,1,0:T(8,128)(2,1)} collective-permute-done((bf16[4,3,128,256]{3,2,1,0:T(8,128)(2,1)}, bf16[4,3,128,256]{3,2,1,0:T(8,128)(2,1)}, u32[]{:S(2)}, u32[]{:S(2)}) %collective-permute-start.10) | collective-permute-done | bytes 786464 | tf_op jit(solution)/shard_map/ppermute | solution.py:582
  213.4 7.2 collective-permute-done.14
  240.5 26.7 %attend.1 = (bf16[512,1024]{1,0:T(8,128)(2,1)S(1)}, f32[512,128]{1,0:T(8,128)S(1)}) custom-call(s32[2]{0:T(128)S(1)} %pad_add_fusion.2.meta_ref, bf16[512,1024]{1,0:T(8,128)(2,1)S(1)} %multiply_convert_fusion.4.q_ref, bf16[1024,1024]{1,0:T(8,128)(2,1)S(1)} %bitcast.426, bf16[1024,1024]{1,0:T(8,128)(2,1)} %bitcast.442, ...), custom_call_target="tpu_custom_call" | custom-call | tf_op jit(solution)/shard_map/attend/pallas_call | solution.py:288
  296.1 17.2 %convolve.1 = (f32[512,1024]{1,0:T(8,128)S(1)}, bf16[512,1024]{1,0:T(8,128)(2,1)S(1)}) custom-call(f32[32,1024]{1,0:T(8,128)S(1)} %collective-permute-done.29.before_ref, f32[512,1024]{1,0:T(8,128)S(1)} %get-tuple-element.530.gated_ref, f32[31,1024]{1,0:T(8,128)S(1)} %slice.764.taps_ref, f32[1,1024]{1,0:T(1,128)S(1)} %get-tuple-element.505.gain_ref, ...), custom_call_target="tpu_custom_call" | custom-call | tf_op jit(solution)/shard_map/convolve/pallas_call | solution.py:449
  333.6 7.8 add_convert_fusion
  375.7 9.3 %convert_reduce_fusion = (f32[4096]{0:T(1024)S(1)}, bf16[512,4096]{1,0:T(8,128)(2,1)S(1)}) fusion(bf16[512,4096]{1,0:T(8,128)(2,1)} %get-tuple-element.248, bf16[4096,1024]{1,0:T(8,128)(2,1)} %copy-done.12, f32[512,1024]{1,0:T(8,128)S(1)} %copy-done.69), kind=kOutput, calls=%fused_computation.1 | convolution fusion | flops 4306497536 | bytes 18890752 | tf_op jit(solution)/shard_map/dot_general | solution.py:27
  385.0 6.1 convolution_convert_fusion.2
  401.2 8.0 multiply_reduce_fusion.1
  441.9 15.5 %convolve_back.1 = (bf16[512,2048]{1,0:T(8,128)(2,1)S(1)}, f32[31,1024]{1,0:T(8,128)S(1)}) custom-call(s32[2]{0:T(128)S(1)} %pad_add_fusion.2.meta_ref, f32[512,1024]{1,0:T(8,128)S(1)} %copy-done.6, f32[32,1024]{1,0:T(8,128)S(1)} %collective-permute-done.35.after_ref, f32[32,1024]{1,0:T(8,128)S(1)} %collective-permute-done.29.before_ref, ...), custom_call_target="tpu_custom_call" | custom-call | tf_op jit(solution)/shard_map/convolve_back/pallas_call | solution.py:521
  495.4 53.4 %attend_back.1 = (bf16[512,1024]{1,0:T(8,128)(2,1)S(1)}, bf16[1024,1024]{1,0:T(8,128)(2,1)}, bf16[1024,1024]{1,0:T(8,128)(2,1)}, f32[128,256]{1,0:T(8,128)S(1)}) custom-call(s32[2]{0:T(128)S(1)} %pad_add_fusion.2.meta_ref, bf16[512,1024]{1,0:T(8,128)(2,1)S(1)} %copy-done.18, bf16[1024,1024]{1,0:T(8,128)(2,1)} %bitcast.427, bf16[1024,1024]{1,0:T(8,128)(2,1)} %bitcast.443, ...), custom_call_target="tpu_custom_call" | custom-call | tf_op jit(solution)/shard_map/attend_back/pallas_call | solution.py:318
  589.6 9.1 %convert_reduce_fusion.1 = (f32[4096]{0:T(1024)}, bf16[512,4096]{1,0:T(8,128)(2,1)}) fusion(bf16[512,4096]{1,0:T(8,128)(2,1)} %get-tuple-element.308, bf16[4096,1024]{1,0:T(8,128)(2,1)S(1)} %bitcast.429, f32[512,1024]{1,0:T(8,128)} %multiply_add_fusion.2), kind=kOutput, calls=%fused_computation.2 | convolution fusion | flops 4306497536 | bytes 18890752 | tf_op jit(solution)/shard_map/dot_general | solution.py:27
  598.7 6.8 convolution_convert_fusion
  634.2 11.5 %collective-permute-done.54 = bf16[256,3072]{1,0:T(8,128)(2,1)S(1)} collective-permute-done((bf16[256,3072]{1,0:T(8,128)(2,1)}, bf16[256,3072]{1,0:T(8,128)(2,1)S(1)}, u32[]{:S(2)}, u32[]{:S(2)}) %collective-permute-start.54) | collective-permute-done | bytes 1572896 | tf_op jit(solution)/shard_map/ppermute | solution.py:582
  661.7 6.8 multiply_reduce_fusion
  688.4 22.5 %collective-permute-done.60 = bf16[256,4096]{1,0:T(8,128)(2,1)} collective-permute-done((bf16[256,4096]{1,0:T(8,128)(2,1)}, bf16[256,4096]{1,0:T(8,128)(2,1)}, u32[]{:S(2)}, u32[]{:S(2)}) %collective-permute-start.60) | collective-permute-done | bytes 2097184 | tf_op jit(solution)/shard_map/ppermute | solution.py:582
  727.7 11.2 %collective-permute-done.64 = bf16[128,4096]{1,0:T(8,128)(2,1)} collective-permute-done((bf16[128,4096]{1,0:T(8,128)(2,1)}, bf16[128,4096]{1,0:T(8,128)(2,1)}, u32[]{:S(2)}, u32[]{:S(2)}) %collective-permute-start.64) | collective-permute-done | bytes 1048608 | tf_op jit(solution)/shard_map/ppermute | solution.py:582
  766.6 15.9 %collective-permute-done.63 = bf16[256,1024]{1,0:T(8,128)(2,1)S(1)} collective-permute-done((bf16[256,1024]{1,0:T(8,128)(2,1)S(1)}, bf16[256,1024]{1,0:T(8,128)(2,1)S(1)}, u32[]{:S(2)}, u32[]{:S(2)}) %collective-permute-start.63) | collective-permute-done | bytes 524320 | tf_op jit(solution)/shard_map/ppermute | solution.py:876
  790.6 24.5 %reduce-scatter.9.cloned.1.call-done = bf16[1,144,1024]{2,1,0:T(8,128)(2,1)} async-done(((bf16[4,144,1024]{2,1,0:T(8,128)(2,1)}), bf16[1,144,1024]{2,1,0:T(8,128)(2,1)}) %reduce-scatter.9.cloned.1.call-update) | async-done | bytes 294928 | tf_op jit(solution)/shard_map/reduce_scatter | solution.py:821
  (778 shorter events, 435.8 us)
Async XLA Ops:
  7.2 36.2 %all-gather.11.cloned.1.call-start = ((), (), s32[]{:S(2)}) async-start(), calls=%async_computation.12 | async-start | bytes 1474560 | tf_op jit(solution)/shard_map/all_gather | solution.py:612
  9.7 62.3 %all-gather.13.cloned.1.call-start = ((), (), s32[]{:S(2)}) async-start(), calls=%async_computation.13 | async-start | bytes 1310720 | tf_op jit(solution)/shard_map/all_gather | solution.py:612
  44.8 72.3 %all-gather.15.cloned.1.call-start = ((), (), s32[]{:S(2)}) async-start(), calls=%async_computation.14 | async-start | bytes 2293760 | tf_op jit(solution)/shard_map/all_gather | solution.py:612
  61.4 40.2 %collective-permute-start.1 = (bf16[8,1,144,1024]{3,2,1,0:T(8,128)(2,1)S(1)}, bf16[8,1,144,1024]{3,2,1,0:T(8,128)(2,1)}, u32[]{:S(2)}, u32[]{:S(2)}) collective-permute-start(bf16[8,1,144,1024]{3,2,1,0:T(8,128)(2,1)S(1)} %pad_maximum_fusion.1.refs_0_), channel_id=1, source_target_pairs={{0,16},{4,12},{8,24},{12,4},{16,0},{20,28},{24,8},{28,20},{1,17},{... | collective-permute-start | bytes 7077896 | tf_op jit(solution)/shard_map/ppermute | solution.py:582
  62.9 132.1 %all-gather.17.cloned.1.call-start = ((), (), s32[]{:S(2)}) async-start(), calls=%async_computation.15 | async-start | bytes 1310720 | tf_op jit(solution)/shard_map/all_gather | solution.py:612
  161.3 70.1 %all-gather.19.cloned.1.call-start = ((), (), s32[]{:S(2)}) async-start(), calls=%async_computation.16 | async-start | bytes 1310720 | tf_op jit(solution)/shard_map/all_gather | solution.py:612
  197.1 558.2 %reduce-scatter.17.cloned.1.call-start = ((), (), s32[]{:S(2)}) async-start(), calls=%async_computation.11 | async-start | bytes 1310720 | tf_op jit(solution)/shard_map/reduce_scatter | solution.py:806
  231.4 39.3 %collective-permute-start.21 = (bf16[8,1,128,1024]{3,2,1,0:T(8,128)(2,1)}, bf16[8,1,128,1024]{3,2,1,0:T(8,128)(2,1)}, u32[]{:S(2)}, u32[]{:S(2)}) collective-permute-start(bf16[8,1,128,1024]{3,2,1,0:T(8,128)(2,1)} %pad_maximum_fusion.4.refs_0_), channel_id=1, source_target_pairs={{0,16},{4,12},{8,24},{12,4},{16,0},{20,28},{24,8},{28,20},{1,17},{... | collective-permute-start | bytes 6291464 | tf_op jit(solution)/shard_map/ppermute | solution.py:582
  235.1 35.3 %collective-permute-start.19 = (bf16[8,3,128,256]{3,2,1,0:T(8,128)(2,1)}, bf16[8,3,128,256]{3,2,1,0:T(8,128)(2,1)}, u32[]{:S(2)}, u32[]{:S(2)}) collective-permute-start(bf16[8,3,128,256]{3,2,1,0:T(8,128)(2,1)} %pad_maximum_fusion.6.refs_0_), channel_id=1, source_target_pairs={{0,4},{4,0},{1,5},{5,1},{2,6},{6,2},{3,7},{7,3},{8,12},{12,8},{9,1... | collective-permute-start | bytes 4718600 | tf_op jit(solution)/shard_map/ppermute | solution.py:583
  272.6 46.2 %collective-permute-start.24 = (bf16[8,1,128,1024]{3,2,1,0:T(8,128)(2,1)}, bf16[8,1,128,1024]{3,2,1,0:T(8,128)(2,1)}, u32[]{:S(2)}, u32[]{:S(2)}) collective-permute-start(bf16[8,1,128,1024]{3,2,1,0:T(8,128)(2,1)} %pad_maximum_fusion.4.refs_0_), channel_id=1, source_target_pairs={{0,4},{4,0},{1,5},{5,1},{2,6},{6,2},{3,7},{7,3},{8,12},{12,8},{9,1... | collective-permute-start | bytes 6291464 | tf_op jit(solution)/shard_map/ppermute | solution.py:583
  272.7 46.1 %collective-permute-start.25 = (bf16[8,1,128,1024]{3,2,1,0:T(8,128)(2,1)}, bf16[8,1,128,1024]{3,2,1,0:T(8,128)(2,1)}, u32[]{:S(2)}, u32[]{:S(2)}) collective-permute-start(bf16[8,1,128,1024]{3,2,1,0:T(8,128)(2,1)} %collective-permute-done.21.refs_1_), channel_id=1, source_target_pairs={{0,4},{4,0},{1,5},{5,1},{2,6},{6,2},{3,7},{7,3},{8,12},{12,8},{9,1... | collective-permute-start | bytes 6291464 | tf_op jit(solution)/shard_map/ppermute | solution.py:583
  273.2 45.6 %collective-permute-start.26 = (bf16[8,1024,128]{2,1,0:T(8,128)(2,1)}, bf16[8,1024,128]{2,1,0:T(8,128)(2,1)}, u32[]{:S(2)}, u32[]{:S(2)}) collective-permute-start(bf16[8,1024,128]{2,1,0:T(8,128)(2,1)} %pad_maximum_fusion.5.refs_0_), channel_id=1, source_target_pairs={{0,16},{4,12},{8,24},{12,4},{16,0},{20,28},{24,8},{28,20},{1,17},{... | collective-permute-start | bytes 6291464 | tf_op jit(solution)/shard_map/ppermute | solution.py:582
  428.4 37.6 %collective-permute-start.39 = (bf16[256,4096]{1,0:T(8,128)(2,1)}, bf16[256,4096]{1,0:T(8,128)(2,1)}, u32[]{:S(2)}, u32[]{:S(2)}) collective-permute-start(bf16[256,4096]{1,0:T(8,128)(2,1)} %fusion.6), channel_id=1, source_target_pairs={{0,16},{4,12},{8,24},{12,4},{16,0},{20,28},{24,8},{28,20},{1,17},{... | collective-permute-start | bytes 6291464 | tf_op jit(solution)/shard_map/ppermute | solution.py:582
  439.0 48.9 %collective-permute-start.42 = (bf16[512,1024]{1,0:T(8,128)(2,1)}, bf16[512,1024]{1,0:T(8,128)(2,1)}, u32[]{:S(2)}, u32[]{:S(2)}) collective-permute-start(bf16[512,1024]{1,0:T(8,128)(2,1)} %convolution_convert_fusion.8), channel_id=1, source_target_pairs={{0,4},{4,0},{1,5},{5,1},{2,6},{6,2},{3,7},{7,3},{8,12},{12,8},{9,1... | collective-permute-start | bytes 3145736 | tf_op jit(solution)/shard_map/ppermute | solution.py:583
  477.9 283.1 %reduce-scatter.15.cloned.1.call-start = ((), (), s32[]{:S(2)}) async-start(), calls=%async_computation.10 | async-start | bytes 1310720 | tf_op jit(solution)/shard_map/reduce_scatter | solution.py:806
  491.7 64.2 %collective-permute-start.43 = (bf16[256,2048]{1,0:T(8,128)(2,1)S(1)}, bf16[256,2048]{1,0:T(8,128)(2,1)S(1)}, u32[]{:S(2)}, u32[]{:S(2)}) collective-permute-start(bf16[256,2048]{1,0:T(8,128)(2,1)S(1)} %fusion.29), channel_id=1, source_target_pairs={{0,16},{4,12},{8,24},{12,4},{16,0},{20,28},{24,8},{28,20},{1,17},{... | collective-permute-start | bytes 3145736 | tf_op jit(solution)/shard_map/ppermute | solution.py:582
  494.1 61.9 %collective-permute-start.44 = (bf16[256,1024]{1,0:T(8,128)(2,1)S(1)}, bf16[256,1024]{1,0:T(8,128)(2,1)S(1)}, u32[]{:S(2)}, u32[]{:S(2)}) collective-permute-start(bf16[256,1024]{1,0:T(8,128)(2,1)S(1)} %fusion.106), channel_id=1, source_target_pairs={{0,16},{4,12},{8,24},{12,4},{16,0},{20,28},{24,8},{28,20},{1,17},{... | collective-permute-start | bytes 1572872 | tf_op jit(solution)/shard_map/ppermute | solution.py:582
  606.9 38.9 %collective-permute-start.57 = (bf16[512,4096]{1,0:T(8,128)(2,1)}, bf16[512,4096]{1,0:T(8,128)(2,1)}, u32[]{:S(2)}, u32[]{:S(2)}) collective-permute-start(bf16[512,4096]{1,0:T(8,128)(2,1)} %convolution_convert_fusion), channel_id=1, source_target_pairs={{0,4},{4,0},{1,5},{5,1},{2,6},{6,2},{3,7},{7,3},{8,12},{12,8},{9,1... | collective-permute-start | bytes 12582920 | tf_op jit(solution)/shard_map/ppermute | solution.py:583
  615.1 148.3 %reduce-scatter.13.cloned.1.call-start = ((), (), s32[]{:S(2)}) async-start(), calls=%async_computation.9 | async-start | bytes 983040 | tf_op jit(solution)/shard_map/reduce_scatter | solution.py:806
  630.3 155.2 %reduce-scatter.11.cloned.1.call-start = ((), (), s32[]{:S(2)}) async-start(), calls=%async_computation.8 | async-start | bytes 1310720 | tf_op jit(solution)/shard_map/reduce_scatter | solution.py:806
  650.8 37.6 %collective-permute-start.61 = (bf16[256,4096]{1,0:T(8,128)(2,1)}, bf16[256,4096]{1,0:T(8,128)(2,1)}, u32[]{:S(2)}, u32[]{:S(2)}) collective-permute-start(bf16[256,4096]{1,0:T(8,128)(2,1)} %fusion.10), channel_id=1, source_target_pairs={{0,16},{4,12},{8,24},{12,4},{16,0},{20,28},{24,8},{28,20},{1,17},{... | collective-permute-start | bytes 6291464 | tf_op jit(solution)/shard_map/ppermute | solution.py:582
  656.1 54.7 %collective-permute-start.60 = (bf16[256,4096]{1,0:T(8,128)(2,1)}, bf16[256,4096]{1,0:T(8,128)(2,1)}, u32[]{:S(2)}, u32[]{:S(2)}) collective-permute-start(bf16[256,4096]{1,0:T(8,128)(2,1)} %fusion.8), channel_id=1, source_target_pairs={{0,16},{4,12},{8,24},{12,4},{16,0},{20,28},{24,8},{28,20},{1,17},{... | collective-permute-start | bytes 6291464 | tf_op jit(solution)/shard_map/ppermute | solution.py:582
  721.2 67.6 %reduce-scatter.7.cloned.1.call-start = ((), (), s32[]{:S(2)}) async-start(), calls=%async_computation.6 | async-start | bytes 1310720 | tf_op jit(solution)/shard_map/reduce_scatter | solution.py:806
  742.8 72.3 %reduce-scatter.9.cloned.1.call-start = ((), (), s32[]{:S(2)}) async-start(), calls=%async_computation.7 | async-start | bytes 1474560 | tf_op jit(solution)/shard_map/reduce_scatter | solution.py:821
  (237 other events, 2880.4 us)
Sparse Core Ops, SparseCore 0:
  10.2 33.1 all-gather.10
  45.0 26.9 all-gather.12
  74.1 42.9 all-gather.14
  161.4 31.5 all-gather.16
  197.2 32.3 all-gather.18
  478.0 26.4 reduce-scatter.16
  615.2 24.5 reduce-scatter.14
  642.1 21.9 reduce-scatter.12
  721.3 24.4 reduce-scatter.10
  748.0 36.2 reduce-scatter.6
  786.7 28.3 reduce-scatter.8

commit v4 on v3

--- a/solution.py
+++ b/solution.py
@@ -1,3 +1,5 @@
+import functools
+
 import jax
 import jax.numpy as jnp
 from jax import lax
@@ -111,8 +113,18 @@
     return with_marks(q_half, half, columns_of)
 
 
-def attend_kernel(meta_ref, q_ref, k_ref, v_ref, e_ref, c_ref, lse_ref, score_ref, share_ref, marks_ref):
+def key_spot(meta_ref, step, count, row_count):
+    spot = lax.rem(meta_ref[2] - step + count, count)
+    return pl.ds(pl.multiple_of(spot * row_count, row_count), row_count)
+
+
+def attend_kernel(count, meta_ref, q_ref, e_ref, *refs):
+    key_refs, value_refs = refs[:count], refs[count : 2 * count]
+    c_ref, lse_ref, score_ref, share_ref, marks_ref, k_ref, v_ref = refs[2 * count :]
     row_count, key_count = q_ref.shape[0], k_ref.shape[0]
+    for step in range(count):
+        k_ref[key_spot(meta_ref, step, count, row_count)] = key_refs[step][...]
+        v_ref[key_spot(meta_ref, step, count, row_count)] = value_refs[step][...]
     blocks = row_count // LANES
     pair = pl.program_id(0)
     lanes = lax.broadcasted_iota(jnp.int32, (row_count, LANES), 1)
@@ -153,12 +165,17 @@
     c_ref[...] = result.astype(jnp.bfloat16)
 
 
-def attend_back_kernel(
-    meta_ref, q_ref, k_ref, v_ref, e_ref, dc_ref, c_ref, lse_ref,
-    dq_ref, dk_ref, dv_ref, de_ref,
-    score_ref, grad_ref, share_ref, slope_ref, source_ref, wide_ref, marks_ref,
-):
+def attend_back_kernel(count, meta_ref, q_ref, e_ref, dc_ref, c_ref, lse_ref, *refs):
+    key_refs, value_refs = refs[:count], refs[count : 2 * count]
+    dq_ref, de_ref = refs[2 * count : 2 * count + 2]
+    dk_refs, dv_refs = refs[2 * count + 2 : 3 * count + 2], refs[3 * count + 2 : 4 * count + 2]
+    score_ref, grad_ref, share_ref, slope_ref, source_ref, wide_ref, marks_ref, k_ref, v_ref, turn_ref = refs[
+        4 * count + 2 :
+    ]
     row_count, key_count = q_ref.shape[0], k_ref.shape[0]
+    for step in range(count):
+        k_ref[key_spot(meta_ref, step, count, row_count)] = key_refs[step][...]
+        v_ref[key_spot(meta_ref, step, count, row_count)] = value_refs[step][...]
     key_blocks, blocks = key_count // LANES, row_count // LANES
     pair = pl.program_id(0)
     lanes = lax.broadcasted_iota(jnp.int32, (row_count, LANES), 1)
@@ -270,8 +287,11 @@
         grad_k = k_part if half == 0 else grad_k + k_part
         grad_v = v_part if half == 0 else grad_v + v_part
     dq_ref[...] = (grad_q * HEAD_DIM ** (-0.5)).astype(jnp.bfloat16)
-    dk_ref[...] = grad_k.T.astype(jnp.bfloat16)
-    dv_ref[...] = grad_v.T.astype(jnp.bfloat16)
+    for grad, grad_refs in ((grad_k, dk_refs), (grad_v, dv_refs)):
+        turn_ref[...] = grad.T
+        for step in range(count):
+            rows = key_spot(meta_ref, -step, count, row_count)
+            grad_refs[step][...] = turn_ref[rows].astype(jnp.bfloat16)
 
 
 def pair_spec(row_count):
@@ -284,22 +304,21 @@
 
 def attend(meta, queries, key_rows, value_rows, table):
     row_count, width = queries.shape
-    key_count = key_rows.shape[0]
+    count = len(key_rows)
+    key_count = row_count * count
     return pl.pallas_call(
-        attend_kernel,
+        functools.partial(attend_kernel, count),
         grid_spec=pltpu.PrefetchScalarGridSpec(
             num_scalar_prefetch=1,
             grid=(width // LANES,),
-            in_specs=[
-                pair_spec(row_count),
-                pair_spec(key_count),
-                pair_spec(key_count),
-                fixed_spec(2 * LANES, LANES),
-            ],
+            in_specs=[pair_spec(row_count), fixed_spec(2 * LANES, LANES)]
+            + [pair_spec(row_count)] * (2 * count),
             out_specs=[pair_spec(row_count), fixed_spec(row_count, LANES)],
             scratch_shapes=[
                 pltpu.VMEM((2, row_count, key_count + 2 * LANES), jnp.float32),
                 pltpu.VMEM((2, row_count, key_count), jnp.bfloat16),
+                pltpu.VMEM((key_count, LANES), jnp.bfloat16),
+                pltpu.VMEM((key_count, LANES), jnp.bfloat16),
                 pltpu.VMEM((key_count, LANES), jnp.bfloat16),
             ],
         ),
@@ -309,32 +328,29 @@
         ],
         compiler_params=pltpu.CompilerParams(vmem_limit_bytes=48 * 2**20),
         name="attend",
-    )(meta, queries, key_rows, value_rows, table)
+    )(meta, queries, table, *key_rows, *value_rows)
 
 
 def attend_back(meta, queries, key_rows, value_rows, table, grad_context, context, levels):
     row_count, width = queries.shape
-    key_count = key_rows.shape[0]
-    return pl.pallas_call(
-        attend_back_kernel,
+    count = len(key_rows)
+    key_count = row_count * count
+    rows_out = jax.ShapeDtypeStruct((row_count, width), jnp.bfloat16)
+    results = pl.pallas_call(
+        functools.partial(attend_back_kernel, count),
         grid_spec=pltpu.PrefetchScalarGridSpec(
             num_scalar_prefetch=1,
             grid=(width // LANES,),
             in_specs=[
                 pair_spec(row_count),
-                pair_spec(key_count),
-                pair_spec(key_count),
                 fixed_spec(2 * LANES, LANES),
                 pair_spec(row_count),
                 pair_spec(row_count),
                 fixed_spec(row_count, LANES),
-            ],
-            out_specs=[
-                pair_spec(row_count),
-                pair_spec(key_count),
-                pair_spec(key_count),
-                fixed_spec(LANES, 2 * LANES),
-            ],
+            ]
+            + [pair_spec(row_count)] * (2 * count),
+            out_specs=[pair_spec(row_count), fixed_spec(LANES, 2 * LANES)]
+            + [pair_spec(row_count)] * (2 * count),
             scratch_shapes=[
                 pltpu.VMEM((2, row_count, key_count + 2 * LANES), jnp.float32),
                 pltpu.VMEM((2, row_count, key_count), jnp.float32),
@@ -343,17 +359,17 @@
                 pltpu.VMEM((2, row_count, 2 * LANES), jnp.bfloat16),
                 pltpu.VMEM((key_count, 2 * LANES), jnp.bfloat16),
                 pltpu.VMEM((2, key_count, LANES), jnp.bfloat16),
+                pltpu.VMEM((key_count, LANES), jnp.bfloat16),
+                pltpu.VMEM((key_count, LANES), jnp.bfloat16),
+                pltpu.VMEM((key_count, LANES), jnp.float32),
             ],
         ),
-        out_shape=[
-            jax.ShapeDtypeStruct((row_count, width), jnp.bfloat16),
-            jax.ShapeDtypeStruct((key_count, width), jnp.bfloat16),
-            jax.ShapeDtypeStruct((key_count, width), jnp.bfloat16),
-            jax.ShapeDtypeStruct((LANES, 2 * LANES), jnp.float32),
-        ],
+        out_shape=[rows_out, jax.ShapeDtypeStruct((LANES, 2 * LANES), jnp.float32)]
+        + [rows_out] * (2 * count),
         compiler_params=pltpu.CompilerParams(vmem_limit_bytes=48 * 2**20),
         name="attend_back",
-    )(meta, queries, key_rows, value_rows, table, grad_context, context, levels)
+    )(meta, queries, table, grad_context, context, levels, *key_rows, *value_rows)
+    return results[0], results[2 : 2 + count], results[2 + count :], results[1]
 
 
 def wide_table(table_low):
@@ -741,29 +757,34 @@
     return (jnp.arange(width)[:, None] == sources).astype(jnp.bfloat16)
 
 
-def reduce_core(place, pairs):
-    group = []
+def other_terms(place, pairs):
+    result = []
     for inputs, grads in pairs:
-        half = inputs.shape[1] // 2
-        product = dot_f32(inputs[:, :half], grads, TN).astype(jnp.bfloat16)
-        group.append((inputs, grads, place.turn(product, "core", 1)))
-    return group
-
-
-def reduce_b(place, group):
+        product = dot_f32(inputs[:, : inputs.shape[1] // 2], grads, TN).astype(jnp.bfloat16)
+        result.append((inputs, grads, place.turn(product, "core", 1)))
+    return result
+
+
+def chip_terms(place, group):
     result = []
     for inputs, grads, other in group:
         half = inputs.shape[1] // 2
         step_rows = half // place.count["b"]
-        arrived = []
-        for number, step in enumerate([*place.steps("b"), 0]):
+        terms = []
+        for number in range(place.count["b"]):
             columns = slice(half + number * step_rows, half + (number + 1) * step_rows)
             rows = slice(number * step_rows, (number + 1) * step_rows)
             term = dot_f32(inputs[:, columns], grads, TN) + other[rows].astype(jnp.float32)
-            term = term.astype(jnp.bfloat16)
-            arrived.append(term if step == 0 else place.turn(term, "b", step))
-        result.append(arrived)
+            terms.append(term.astype(jnp.bfloat16))
+        result.append(terms)
     return result
+
+
+def send_b(place, group):
+    return [
+        [place.turn(term, "b", step) for term, step in zip(terms, place.steps("b"))] + [terms[-1]]
+        for terms in group
+    ]
 
 
 def added(arrays):
@@ -773,20 +794,28 @@
     return total
 
 
-def reduce_a(place, group):
+def messages_a(place, group):
     result = []
     for arrived in group:
         step_rows = arrived[0].shape[0] // place.count["a"]
-        kept = []
-        for number, step in enumerate([*place.steps("a"), 0]):
+        messages = []
+        for number in range(place.count["a"] - 1):
             rows = slice(number * step_rows, (number + 1) * step_rows)
-            mine = [one[rows] for one in arrived]
-            if step == 0:
-                kept += mine
-            else:
-                kept.append(place.turn(added(mine).astype(mine[0].dtype), "a", step))
-        result.append(kept)
+            messages.append(added([one[rows] for one in arrived]).astype(jnp.bfloat16))
+        result.append((messages, arrived))
     return result
+
+
+def send_a(place, group):
+    return [
+        kept + [place.turn(message, "a", step) for message, step in zip(messages, place.steps("a"))]
+        for messages, kept in group
+    ]
+
+
+def last_rows(kept):
+    rows = kept[-1].shape[0]
+    return added([one[-rows:] for one in kept])
 
 
 def by_tensor(total, count):
@@ -794,21 +823,24 @@
     return [total[:, number * width : (number + 1) * width] for number in range(count)]
 
 
-def reduce_t(place, group):
+def tensor_blocks(place, group):
     count = place.count["t"]
     blocks = [[] for _ in range(count)]
     for depth, kept in group:
-        total = added(kept).astype(jnp.bfloat16)
+        total = last_rows(kept).astype(jnp.bfloat16)
         for part in by_tensor(total, depth):
             for number, block in enumerate(by_tensor(part, count)):
                 blocks[number].append(block)
-    stack = jnp.stack([jnp.stack(block) for block in blocks])
+    return jnp.stack([jnp.stack(block) for block in blocks])
+
+
+def reduce_t(stack):
     return lax.psum_scatter(stack, TENSOR, scatter_dimension=0)
 
 
 def reduce_t_vectors(place, kept, vectors):
     count = place.count["t"]
-    total = added(kept).astype(jnp.bfloat16)
+    total = last_rows(kept).astype(jnp.bfloat16)
     vector_count, columns = vectors.shape[0], total.shape[1] // count
     extra_rows = -(-vectors.size // (count * columns) // 16) * 16 if vectors.size else 0
     extra_rows = max(extra_rows, 16)
@@ -845,14 +877,20 @@
     ]
 
 
+def clip_blocks(place, blocks):
+    micro, z_here = blocks.shape[0], place.index["z"]
+    return [
+        lax.dynamic_index_in_dim(blocks, lax.rem(z_here + step, micro), 0, keepdims=False)
+        for step in range(micro)
+    ]
+
+
 def to_clip(place, blocks):
-    micro, z_count = blocks.shape[0], place.count["z"]
-    z_here = place.index["z"]
-    arrived = []
-    for step in range(micro):
-        block = lax.dynamic_index_in_dim(blocks, lax.rem(z_here + step, micro), 0, keepdims=False)
-        arrived.append(lax.ppermute(block, ("core", "z"), clip_pairs(micro, z_count, step)))
-    return arrived
+    micro, z_count = len(blocks), place.count["z"]
+    return [
+        lax.ppermute(block, ("core", "z"), clip_pairs(micro, z_count, step))
+        for step, block in enumerate(blocks)
+    ]
 
 
 def ordered_clip(place, arrived):
@@ -865,13 +903,19 @@
     return jnp.concatenate(ordered, axis=0)
 
 
-def from_clip(place, rows_in, micro):
-    z_count, z_here = place.count["z"], place.index["z"]
+def own_blocks(place, rows_in, micro):
+    z_here = place.index["z"]
     blocks = rows_in.reshape(micro, -1, rows_in.shape[-1])
+    return [
+        lax.dynamic_index_in_dim(blocks, lax.rem(z_here - step + micro, micro), 0, keepdims=False)
+        for step in range(micro)
+    ]
+
+
+def from_clip(place, blocks):
+    micro, z_count = len(blocks), place.count["z"]
     arrived = []
-    for step in range(micro):
-        spot = lax.rem(z_here - step + micro, micro)
-        block = lax.dynamic_index_in_dim(blocks, spot, 0, keepdims=False)
+    for step, block in enumerate(blocks):
         pairs = [(end, start) for start, end in clip_pairs(micro, z_count, step)]
         arrived.append(lax.ppermute(block, ("core", "z"), pairs))
     return arrived
@@ -891,22 +935,13 @@
 
 
 def all_rows(place, own):
-    count = place.count["seq"]
-    whole = jnp.zeros((count,) + own.shape, own.dtype)
-    for step in range(count):
-        block = own if step == 0 else place.turn(own, "seq", step)
-        spot = lax.rem(place.index["seq"] - step + count, count)
-        whole = lax.dynamic_update_index_in_dim(whole, block, spot, 0)
-    return whole.reshape((count * own.shape[0],) + own.shape[1:])
-
-
-def own_sum(place, partial):
-    count = place.count["seq"]
-    blocks = partial.reshape(count, -1, partial.shape[-1])
-    total = lax.dynamic_index_in_dim(blocks, place.index["seq"], 0, keepdims=False).astype(jnp.float32)
-    for step in range(1, count):
-        message = lax.dynamic_index_in_dim(blocks, place.after("seq", step), 0, keepdims=False)
-        total = total + place.turn(message, "seq", step).astype(jnp.float32)
+    return [own] + [place.turn(own, "seq", step) for step in place.steps("seq")]
+
+
+def own_sum(place, parts):
+    total = parts[0].astype(jnp.float32)
+    for part, step in zip(parts[1:], place.steps("seq")):
+        total = total + place.turn(part, "seq", step).astype(jnp.float32)
     return total
 
 
@@ -988,7 +1023,7 @@
     other_facts = place.turn(own_facts, "core", 1)
     up_one, frames, shard_mix = fence(up_one, frames, shard_mix)
     up_one = gather_b(place, up_one)
-    rows_low = to_clip(place, frames)
+    rows_low = to_clip(place, clip_blocks(place, frames))
     down_one = gather_a(place, down_one)
     both_mix = gather_t(place, shard_mix)
     up_one, down_one, second_up = fence(up_one, down_one, second_up)
@@ -1013,7 +1048,8 @@
     valid_flag = (facts[0] > 0).astype(jnp.float32)
     first_row = place.index["seq"] * row_count
     live = ((first_row + jnp.arange(row_count)) < facts[1]).astype(jnp.float32)[:, None]
-    meta = jnp.stack([place.index["seq"] * (row_count // LANES), facts[1]]).astype(jnp.int32)
+    meta = jnp.stack([place.index["seq"] * (row_count // LANES), facts[1], place.index["seq"]])
+    meta = meta.astype(jnp.int32)
     pick_rows = (rel_rows[:, None] == jnp.arange(OFFSETS)[None, :]).astype(jnp.bfloat16)
     table = wide_table(matmul(pick_rows, distance).astype(jnp.bfloat16))
 
@@ -1024,8 +1060,8 @@
         vector_wide[0],
         vector_wide[1],
     )
-    (down_one, attend_mix, point_mix, second_down, one_hidden, one_kept, up_one, table) = fence(
-        down_one, attend_mix, point_mix, second_down, one_hidden, one_kept, up_one, table
+    (down_one, attend_mix, point_mix, second_down, one_hidden, one_kept, table) = fence(
+        down_one, attend_mix, point_mix, second_down, one_hidden, one_kept, table
     )
     down_one = gather_core(place, down_one)
     attend_mix = gather_b(place, attend_mix)
@@ -1055,7 +1091,7 @@
     point_mix = gather_core(place, point_mix)
     up_two = gather_b(place, up_two)
     down_two = gather_a(place, down_two)
-    cot_low = to_clip(place, cotangent)
+    cot_low = to_clip(place, clip_blocks(place, cotangent))
     context, levels = attend(meta, queries, key_rows, value_rows, table)
     (point_mix, up_two, down_two, context, levels, after_one) = fence(
         point_mix, up_two, down_two, context, levels, after_one
@@ -1104,11 +1140,11 @@
     grad_low, grad_upper, two_up_bias, two_down_bias = feed_back_down(
         0.5 * grad_four, two_kept, down_two
     )
-    sum_down_two = reduce_core(place, [(sent(grad_low), two_hidden)])
+    sum_down_two = other_terms(place, [(sent(grad_low), two_hidden)])
     (sum_down_two, grad_four, grad_upper, row_out) = fence(sum_down_two, grad_four, grad_upper, row_out)
-    sum_down_two = reduce_b(place, sum_down_two)
-    frames_out = from_clip(place, row_out, micro)
-    sum_up_two = reduce_core(place, [(sent(two_kept[2]), grad_upper)])
+    sum_down_two = send_b(place, chip_terms(place, sum_down_two))
+    frames_out = from_clip(place, own_blocks(place, row_out, micro))
+    sum_up_two = other_terms(place, [(sent(two_kept[2]), grad_upper)])
     grad_normed = dot_f32(grad_upper, up_two, NT)
     grad_two_in, two_gain, two_shift = norm_back(
         grad_normed, two_kept[0], two_kept[1], vector_wide[second_base]
@@ -1124,15 +1160,15 @@
     (sum_down_two, sum_up_two, grad_three, conv_low, grad_depth, after, frames_out) = fence(
         sum_down_two, sum_up_two, grad_three, conv_low, grad_depth, after, frames_out
     )
-    sum_down_two = reduce_a(place, sum_down_two)
-    sum_up_two = reduce_b(place, sum_up_two)
+    sum_down_two = send_a(place, messages_a(place, sum_down_two))
+    sum_up_two = send_b(place, chip_terms(place, sum_up_two))
     grad_pair, tap_grads = convolve_back(
         meta, grad_depth, after, before, gated, taps, linear, logistic
     )
     (sum_down_two, sum_up_two, grad_pair) = fence(sum_down_two, sum_up_two, grad_pair)
-    sum_down_two = reduce_t(place, [(1, sum_down_two[0])])
-    sum_up_two = reduce_a(place, sum_up_two)
-    sum_point = reduce_core(
+    sum_down_two = reduce_t(tensor_blocks(place, [(1, sum_down_two[0])]))
+    sum_up_two = send_a(place, messages_a(place, sum_up_two))
+    sum_point = other_terms(
         place,
         [
             (sent(conv_normed), grad_pair),
@@ -1150,33 +1186,36 @@
     (sum_up_two, sum_point, grad_two, attend_low, grad_context) = fence(
         sum_up_two, sum_point, grad_two, attend_low, grad_context
     )
-    sum_up_two = reduce_t(place, [(1, sum_up_two[0])])
-    sum_point = reduce_b(place, sum_point)
+    sum_up_two = reduce_t(tensor_blocks(place, [(1, sum_up_two[0])]))
+    sum_point = send_b(place, chip_terms(place, sum_point))
     grad_queries, part_keys, part_values, grad_table = attend_back(
         meta, queries, key_rows, value_rows, table, grad_context, context, levels
     )
-    (sum_point, grad_queries, part_keys, part_values, grad_table) = fence(
-        sum_point, grad_queries, part_keys, part_values, grad_table
-    )
-    sum_point = reduce_a(place, sum_point)
+    (sum_point, grad_queries, part_keys, part_values, grad_table, sum_down_two) = fence(
+        sum_point, grad_queries, part_keys, part_values, grad_table, sum_down_two
+    )
+    sum_point = send_a(place, messages_a(place, sum_point))
     grad_keys = own_sum(place, part_keys).astype(jnp.bfloat16)
     grad_values = own_sum(place, part_values).astype(jnp.bfloat16)
     sum_distance = jnp.dot(
         pick_rows.astype(jnp.float32).T, table_grad(grad_table), precision=lax.Precision.HIGHEST
     )
-    sum_distance = sum(
-        (place.turn(sum_distance, "t", step) for step in place.steps("t")), sum_distance
-    )
-    sum_attend = reduce_core(
+    sent_attend, sent_out = sent(attend_normed), sent(attend_low)
+    (sum_point, sum_distance, grad_keys, grad_values, sum_up_two, sent_attend, sent_out) = fence(
+        sum_point, sum_distance, grad_keys, grad_values, sum_up_two, sent_attend, sent_out
+    )
+    sum_attend = other_terms(
         place,
         [
-            (
-                sent(attend_normed),
-                jnp.concatenate([grad_queries, grad_keys, grad_values], axis=1),
-            ),
-            (sent(attend_low), context),
+            (sent_attend, jnp.concatenate([grad_queries, grad_keys, grad_values], axis=1)),
+            (sent_out, context),
         ],
     )
+    sum_distance = sum(
+        [place.turn(sum_distance, "t", step) for step in place.steps("t")], sum_distance
+    )
+    sum_attend = chip_terms(place, sum_attend)
+    sum_point = tensor_blocks(place, [(2, sum_point[0]), (1, sum_point[1])])
     grad_attend_normed = (
         dot_f32(grad_queries, attend_mix[0], NT)
         + dot_f32(grad_keys, attend_mix[1], NT)
@@ -1187,24 +1226,42 @@
     )
     grad_one = grad_two + grad_attend_in
     (sum_point, sum_attend, sum_distance, grad_one) = fence(sum_point, sum_attend, sum_distance, grad_one)
-    sum_point = reduce_t(place, [(2, sum_point[0]), (1, sum_point[1])])
-    sum_attend = reduce_b(place, sum_attend)
+    sum_attend = send_b(place, sum_attend)
+    sum_point = reduce_t(sum_point)
+    grad_low, grad_upper, one_up_bias, one_down_bias = feed_back_down(0.5 * grad_one, one_kept, down_one)
+    sent_low, sent_one = sent(grad_low), sent(one_kept[2])
+    (sum_attend, grad_upper, sum_distance, sent_low, sent_one, one_up_bias) = fence(
+        sum_attend, grad_upper, sum_distance, sent_low, sent_one, one_up_bias
+    )
+    sum_attend = send_a(place, messages_a(place, sum_attend))
+    sum_down_one = other_terms(place, [(sent_low, one_hidden)])
+    sum_up_one = other_terms(place, [(sent_one, grad_upper)])
+    sum_down_one = chip_terms(place, sum_down_one)
     sum_distance = sum_distance + place.turn(sum_distance, "core", 1)
-    grad_low, grad_upper, one_up_bias, one_down_bias = feed_back_down(0.5 * grad_one, one_kept, down_one)
-    sum_down_one = reduce_core(place, [(sent(grad_low), one_hidden)])
-    sum_up_one = reduce_core(place, [(sent(one_kept[2]), grad_upper)])
-    (sum_attend, sum_down_one, sum_up_one, grad_upper) = fence(
-        sum_attend, sum_down_one, sum_up_one, grad_upper
-    )
-    sum_down_one = reduce_b(place, sum_down_one)
-    sum_attend = reduce_a(place, sum_attend)
-    sum_up_one = reduce_b(place, sum_up_one)
+    sum_attend = tensor_blocks(place, [(3, sum_attend[0]), (1, sum_attend[1])])
+    (sum_attend, sum_down_one, sum_up_one, grad_upper, sum_distance, sum_point) = fence(
+        sum_attend, sum_down_one, sum_up_one, grad_upper, sum_distance, sum_point
+    )
+    sum_down_one = send_b(place, sum_down_one)
+    sum_attend = reduce_t(sum_attend)
+    sum_up_one = chip_terms(place, sum_up_one)
     sum_distance = sum(
-        (place.turn(sum_distance, "b", step) for step in place.steps("b")), sum_distance
+        [place.turn(sum_distance, "b", step) for step in place.steps("b")], sum_distance
     )
     grad_normed = dot_f32(grad_upper, up_one, NT)
     grad_one_in, one_gain, one_shift = norm_back(grad_normed, one_kept[0], one_kept[1], vector_wide[0])
     grad_rows = grad_one + grad_one_in + (1.0 - valid_flag) * rows_cot
+
+    grad_blocks = own_blocks(place, grad_rows.astype(jnp.bfloat16), micro)
+    (sum_attend, sum_down_one, sum_up_one, grad_blocks, one_gain, one_shift, sum_distance) = fence(
+        sum_attend, sum_down_one, sum_up_one, grad_blocks, one_gain, one_shift, sum_distance
+    )
+    sum_down_one = send_a(place, messages_a(place, sum_down_one))
+    sum_up_one = send_b(place, sum_up_one)
+    frames_grad = from_clip(place, grad_blocks)
+    sum_distance = sum(
+        [place.turn(sum_distance, "a", step) for step in place.steps("a")], sum_distance
+    )
 
     def column_sum(rows):
         return jnp.sum(rows.astype(jnp.float32), axis=0)
@@ -1235,30 +1292,23 @@
         ],
         axis=0,
     )
-    grad_rows = grad_rows.astype(jnp.bfloat16)
     vector_part = jnp.dot(vector_part, order.astype(jnp.float32), precision=lax.Precision.HIGHEST)
-    (sum_attend, sum_down_one, sum_up_one, vector_part, grad_rows) = fence(
-        sum_attend, sum_down_one, sum_up_one, vector_part, grad_rows
-    )
-    sum_up_one = reduce_a(place, sum_up_one)
-    sum_down_one = reduce_a(place, sum_down_one)
     sum_vectors = reduce_vectors_core(place, vector_part)
-    sum_attend = reduce_t(place, [(3, sum_attend[0]), (1, sum_attend[1])])
-    sum_distance = sum(
-        (place.turn(sum_distance, "a", step) for step in place.steps("a")), sum_distance
-    )
-    frames_grad = from_clip(place, grad_rows, micro)
-    (sum_up_one, sum_down_one, sum_vectors) = fence(sum_up_one, sum_down_one, sum_vectors)
-    sum_up_one = reduce_t(place, [(1, sum_up_one[0])])
+    (sum_up_one, sum_down_one, sum_vectors, frames_grad) = fence(
+        sum_up_one, sum_down_one, sum_vectors, frames_grad
+    )
+    sum_up_one = send_a(place, messages_a(place, sum_up_one))
+    sum_down_one = reduce_t(tensor_blocks(place, [(1, sum_down_one[0])]))
     sum_vectors = reduce_vectors(place, sum_vectors, "b")
     sum_vectors = reduce_vectors(place, sum_vectors, "a")
-    sum_down_one, grad_vectors = reduce_t_vectors(place, sum_down_one[0], sum_vectors)
+    (sum_up_one, sum_vectors) = fence(sum_up_one, sum_vectors)
+    sum_up_one, grad_vectors = reduce_t_vectors(place, sum_up_one[0], sum_vectors)
     wide = jnp.float32
     return (
         own_clips(place, frames_out),
         own_clips(place, frames_grad),
-        sum_up_one[0].astype(wide),
-        sum_down_one.T.astype(wide),
+        sum_up_one.astype(wide),
+        sum_down_one[0].T.astype(wide),
         sum_attend[:3].astype(wide),
         sum_attend[3].T.astype(wide),
         sum_point[:2].astype(wide),

time: 834 us -> 824 us (0.988)
  local copies, waits for them, and re-layouts: 45.7 us -> 35.2 us
    ppermute x32, waiting for transfers between devices: 135 us -> 119 us  [turn(): return lax.ppermute(block, ('y', 'x', 'core'), pairs)]
    convert_element_type x18 -> x19, other arithmetic: 23.5 us -> 28 us  [the longest x8 11.9 us: messages_a(): messages.append(added([one[rows] for one in arrived]).astype(jnp.bfloat16))]
    unnamed x344 -> x320, local copies, waits for them, and re-layouts: 16.4 us -> 19.2 us
  transfers between devices with their start and end apart: 83 -> 83, of which waited for: 30 -> 30; matrix products, arithmetic and copies ran while one was open for 36% -> 34% of each run, Pallas kernels for 16% -> 16%
where the time goes in v4:
time: 824 us; the launch traced here: 815 us
  waiting for transfers between devices  239 us (29%)
  matrix products  203 us (25%)
  Pallas kernels  131 us (16%)
  other arithmetic  103 us (12%)
  starting transfers between devices  85.9 us (10%)
  local copies, waits for them, and re-layouts  35.2 us (4%)
  between operations  17.1 us (2%)
    dot_general x55, matrix products, dot_f32(): lax.dot_general(left_side, right_side, dims, preferred_element_type=jnp.f...  201 us
    ppermute x32, waiting for transfers between devices, turn(): return lax.ppermute(block, ('y', 'x', 'core'), pairs)  119 us
    all_gather x5, waiting for transfers between devices, gather_t(): return lax.all_gather(shard, TENSOR, axis=0)  56.3 us
    pallas_call x1, Pallas kernels, attend_back(): pl.pallas_call(functools.partial(attend_back_kernel, count), grid_spec=pl...  54.4 us
    ppermute x32, starting transfers between devices, turn(): return lax.ppermute(block, ('y', 'x', 'core'), pairs)  38.6 us
    reduce_scatter x1, waiting for transfers between devices, reduce_t_vectors(): result = lax.psum_scatter(jnp.stack(blocks), TENSOR, scatter_dimension=0)  27.8 us
    pallas_call x1, Pallas kernels, attend(): pl.pallas_call(functools.partial(attend_kernel, count), grid_spec=pltpu.P...  27 us
    pallas_call x6, Pallas kernels, assemble(): pl.pallas_call(kernel, grid_spec=pltpu.PrefetchScalarGridSpec(num_scalar_...  25.5 us
  transfers between devices with their start and end apart: 83, of which 30 were waited for; matrix products, arithmetic and copies ran while one was open for 34% of the time, Pallas kernels for 16%

profile of v4, /device:TPU:0, one launch (start us, length us, event | category | flops | bytes accessed | tf_op | source)
XLA Modules:
  0.0 815.1 jit_solution(16911725903350285601)
XLA Ops:
  11.0 32.4 %all-gather.11.cloned.1.call-done = bf16[576,1024]{1,0:T(8,128)(2,1)} async-done(((bf16[144,1024]{1,0:T(8,128)(2,1)}), bf16[576,1024]{1,0:T(8,128)(2,1)}) %all-gather.11.cloned.1.call-update) | async-done | bytes 1179664 | tf_op jit(solution)/shard_map/all_gather | solution.py:628
  48.6 11.2 %collective-permute-done = bf16[4,1,144,1024]{3,2,1,0:T(8,128)(2,1)} collective-permute-done((bf16[4,1,144,1024]{3,2,1,0:T(8,128)(2,1)}, bf16[4,1,144,1024]{3,2,1,0:T(8,128)(2,1)}, u32[]{:S(2)}, u32[]{:S(2)}) %collective-permute-start) | collective-permute-done | bytes 1179680 | tf_op jit(solution)/shard_map/ppermute | solution.py:598
  63.0 9.0 %all-gather.13.cloned.1.call-done = bf16[4096,128]{1,0:T(8,128)(2,1)} async-done(((bf16[1024,128]{1,0:T(8,128)(2,1)}), bf16[4096,128]{1,0:T(8,128)(2,1)}) %all-gather.13.cloned.1.call-update) | async-done | bytes 1048592 | tf_op jit(solution)/shard_map/all_gather | solution.py:628
  73.5 24.8 %collective-permute-done.2 = bf16[4,1024,128]{2,1,0:T(8,128)(2,1)S(1)} collective-permute-done((bf16[4,1024,128]{2,1,0:T(8,128)(2,1)}, bf16[4,1024,128]{2,1,0:T(8,128)(2,1)S(1)}, u32[]{:S(2)}, u32[]{:S(2)}) %collective-permute-start.2) | collective-permute-done | bytes 1048608 | tf_op jit(solution)/shard_map/ppermute | solution.py:598
  107.1 10.1 %all-gather.15.cloned.1.call-done = bf16[28,128,256]{2,1,0:T(8,128)(2,1)} async-done(((bf16[7,128,256]{2,1,0:T(8,128)(2,1)}), bf16[28,128,256]{2,1,0:T(8,128)(2,1)}) %all-gather.15.cloned.1.call-update) | async-done | bytes 1835024 | tf_op jit(solution)/shard_map/all_gather | solution.py:628
  141.5 8.4 %add_convert_fusion.1 = (bf16[512,4096]{1,0:T(8,128)(2,1)}, bf16[512,4096]{1,0:T(8,128)(2,1)}) fusion(f32[4096]{0:T(1024)S(1)} %bitcast.458, bf16[512,1024]{1,0:T(8,128)(2,1)S(1)} %get-tuple-element.351, bf16[1,1024,4096]{2,1,0:T(8,128)(2,1)S(1)} %get-tuple-element.214), kind=kOutput, calls=%fused_computation.13 | convolution fusion | flops 4315938816 | bytes 17842176 | tf_op jit(solution)/shard_map/dot_general | solution.py:29
  163.3 16.0 %collective-permute-done.10 = bf16[4,3,128,256]{3,2,1,0:T(8,128)(2,1)} collective-permute-done((bf16[4,3,128,256]{3,2,1,0:T(8,128)(2,1)}, bf16[4,3,128,256]{3,2,1,0:T(8,128)(2,1)}, u32[]{:S(2)}, u32[]{:S(2)}) %collective-permute-start.10) | collective-permute-done | bytes 786464 | tf_op jit(solution)/shard_map/ppermute | solution.py:598
  211.6 9.1 %collective-permute-done.14 = bf16[4,1,128,1024]{3,2,1,0:T(8,128)(2,1)S(1)} collective-permute-done((bf16[4,1,128,1024]{3,2,1,0:T(8,128)(2,1)}, bf16[4,1,128,1024]{3,2,1,0:T(8,128)(2,1)S(1)}, u32[]{:S(2)}, u32[]{:S(2)}) %collective-permute-start.14) | collective-permute-done | bytes 1048608 | tf_op jit(solution)/shard_map/ppermute | solution.py:598
  239.7 27.0 %attend.1 = (bf16[512,1024]{1,0:T(8,128)(2,1)S(1)}, f32[512,128]{1,0:T(8,128)S(1)}) custom-call(s32[3]{0:T(128)S(1)} %pad_add_fusion.2.meta_ref, bf16[512,1024]{1,0:T(8,128)(2,1)S(1)} %copy-done.15, bf16[256,128]{1,0:T(8,128)(2,1)S(1)} %pad_maximum_fusion.18.e_ref, bf16[512,1024]{1,0:T(8,128)(2,1)S(1)} %fusion.89.refs_0_, ...), custom_call_target="tpu_custom_call" | custom-call | tf_op jit(solution)/shard_map/attend/pallas_call | solution.py:309
  297.9 8.9 %convolve.1 = (f32[512,1024]{1,0:T(8,128)S(1)}, bf16[512,1024]{1,0:T(8,128)(2,1)S(1)}) custom-call(f32[32,1024]{1,0:T(8,128)S(1)} %collective-permute-done.29.before_ref, f32[512,1024]{1,0:T(8,128)S(1)} %get-tuple-element.566.gated_ref, f32[31,1024]{1,0:T(8,128)S(1)} %slice.760.taps_ref, f32[1,1024]{1,0:T(1,128)S(1)} %get-tuple-element.545.gain_ref, ...), custom_call_target="tpu_custom_call" | custom-call | tf_op jit(solution)/shard_map/convolve/pallas_call | solution.py:465
  329.6 7.8 add_convert_fusion
  369.8 9.9 %convert_reduce_fusion = (f32[4096]{0:T(1024)}, bf16[512,4096]{1,0:T(8,128)(2,1)S(1)}) fusion(bf16[512,4096]{1,0:T(8,128)(2,1)} %get-tuple-element.271, bf16[4096,1024]{1,0:T(8,128)(2,1)} %copy-done.9, f32[512,1024]{1,0:T(8,128)S(1)} %copy-done.69), kind=kOutput, calls=%fused_computation.5 | convolution fusion | flops 4306497536 | bytes 18890752 | tf_op jit(solution)/shard_map/dot_general | solution.py:29
  396.6 7.9 multiply_reduce_fusion
  432.3 15.5 %convolve_back.1 = (bf16[512,2048]{1,0:T(8,128)(2,1)S(1)}, f32[31,1024]{1,0:T(8,128)S(1)}) custom-call(s32[3]{0:T(128)S(1)} %pad_add_fusion.2.meta_ref, f32[512,1024]{1,0:T(8,128)S(1)} %subtract_multiply_fusion.grad_ref, f32[32,1024]{1,0:T(8,128)S(1)} %collective-permute-done.35.after_ref, f32[32,1024]{1,0:T(8,128)S(1)} %collective-permute-done.29.before_ref, ...), custom_call_target="tpu_custom_call" | custom-call | tf_op jit(solution)/shard_map/convolve_back/pallas_call | solution.py:537
  453.1 5.8 collective-permute-done.39
  491.0 54.4 %attend_back.1 = (bf16[512,1024]{1,0:T(8,128)(2,1)S(1)}, f32[128,256]{1,0:T(8,128)S(1)}, bf16[512,1024]{1,0:T(8,128)(2,1)S(1)}, bf16[512,1024]{1,0:T(8,128)(2,1)...) custom-call(s32[3]{0:T(128)S(1)} %pad_add_fusion.2.meta_ref, ...), custom_call_target="tpu_custom_call" | custom-call | tf_op jit(solution)/shard_map/attend_back/pallas_call | solution.py:339
  611.2 9.1 %convert_reduce_fusion.1 = (f32[4096]{0:T(1024)S(1)}, bf16[512,4096]{1,0:T(8,128)(2,1)S(1)}) fusion(bf16[512,4096]{1,0:T(8,128)(2,1)} %get-tuple-element.349, bf16[4096,1024]{1,0:T(8,128)(2,1)} %copy-done.7, f32[512,1024]{1,0:T(8,128)S(1)} %copy-done.61), kind=kOutput, calls=%fused_computation.6 | convolution fusion | flops 4306497536 | bytes 18890752 | tf_op jit(solution)/shard_map/dot_general | solution.py:29
  621.6 13.8 %collective-permute-done.55 = bf16[256,1024]{1,0:T(8,128)(2,1)S(1)} collective-permute-done((bf16[256,1024]{1,0:T(8,128)(2,1)}, bf16[256,1024]{1,0:T(8,128)(2,1)S(1)}, u32[]{:S(2)}, u32[]{:S(2)}) %collective-permute-start.55) | collective-permute-done | bytes 524320 | tf_op jit(solution)/shard_map/ppermute | solution.py:598
  653.9 9.0 %collective-permute-done.57 = bf16[128,1024]{1,0:T(8,128)(2,1)S(1)} collective-permute-done((bf16[128,1024]{1,0:T(8,128)(2,1)S(1)}, bf16[128,1024]{1,0:T(8,128)(2,1)S(1)}, u32[]{:S(2)}, u32[]{:S(2)}) %collective-permute-start.57) | collective-permute-done | bytes 262176 | tf_op jit(solution)/shard_map/ppermute | solution.py:598
  679.5 10.5 %multiply_reduce_fusion.4 = (f32[1024]{0:T(1024)S(1)}, f32[512]{0:T(512)S(1)}, f32[512]{0:T(512)S(1)}, f32[1024]{0:T(1024)S(1)}, f32[512,1024]{1,0:T(8,128)S(1)}) fusion(f32[512,1024]{1,0:T(8,128)} %get-tuple-element.369, f32[1024]{0:T(1024)S(1)} %bitcast.438, bf16[512,4096]{1,0:T(8,128)(2,1)} %copy-done.45, bf16[1,1024,4096]{2,1,0:T(8,128)(2,1)} %copy-done.29), kind=kOutput, calls=%fused_computation.117 | convolution fusion | flops 4298634240 | bytes 16793600 | tf_op jit(solution)/shard_map/dot_general | solution.py:29
  717.4 15.9 %collective-permute-done.67 = bf16[256,1024]{1,0:T(8,128)(2,1)S(1)} collective-permute-done((bf16[256,1024]{1,0:T(8,128)(2,1)}, bf16[256,1024]{1,0:T(8,128)(2,1)S(1)}, u32[]{:S(2)}, u32[]{:S(2)}) %collective-permute-start.67) | collective-permute-done | bytes 524320 | tf_op jit(solution)/shard_map/ppermute | solution.py:920
  734.7 6.7 collective-permute-done.63
  750.4 9.5 %collective-permute-done.70 = f32[56,128]{1,0:T(8,128)S(1)} collective-permute-done((f32[56,128]{1,0:T(8,128)S(1)}, f32[56,128]{1,0:T(8,128)S(1)}, u32[]{:S(2)}, u32[]{:S(2)}) %collective-permute-start.70) | collective-permute-done | bytes 28704 | tf_op jit(solution)/shard_map/ppermute | solution.py:598
  777.1 27.8 %reduce-scatter.15.cloned.1.call-done = bf16[1,144,1024]{2,1,0:T(8,128)(2,1)} async-done(((bf16[4,144,1024]{2,1,0:T(8,128)(2,1)}), bf16[1,144,1024]{2,1,0:T(8,128)(2,1)}) %reduce-scatter.15.cloned.1.call-update) | async-done | bytes 294928 | tf_op jit(solution)/shard_map/reduce_scatter | solution.py:853
  (723 shorter events, 437.5 us)
Async XLA Ops:
  7.2 36.2 %all-gather.11.cloned.1.call-start = ((), (), s32[]{:S(2)}) async-start(), calls=%async_computation.12 | async-start | bytes 1474560 | tf_op jit(solution)/shard_map/all_gather | solution.py:628
  9.7 62.3 %all-gather.13.cloned.1.call-start = ((), (), s32[]{:S(2)}) async-start(), calls=%async_computation.13 | async-start | bytes 1310720 | tf_op jit(solution)/shard_map/all_gather | solution.py:628
  44.8 72.3 %all-gather.15.cloned.1.call-start = ((), (), s32[]{:S(2)}) async-start(), calls=%async_computation.14 | async-start | bytes 2293760 | tf_op jit(solution)/shard_map/all_gather | solution.py:628
  61.4 40.2 %collective-permute-start.1 = (bf16[8,1,144,1024]{3,2,1,0:T(8,128)(2,1)S(1)}, bf16[8,1,144,1024]{3,2,1,0:T(8,128)(2,1)}, u32[]{:S(2)}, u32[]{:S(2)}) collective-permute-start(bf16[8,1,144,1024]{3,2,1,0:T(8,128)(2,1)S(1)} %pad_maximum_fusion.refs_0_), channel_id=1, source_target_pairs={{0,16},{4,12},{8,24},{12,4},{16,0},{20,28},{24,8},{28,20},{1,17},{... | collective-permute-start | bytes 7077896 | tf_op jit(solution)/shard_map/ppermute | solution.py:598
  62.9 132.1 %all-gather.17.cloned.1.call-start = ((), (), s32[]{:S(2)}) async-start(), calls=%async_computation.15 | async-start | bytes 1310720 | tf_op jit(solution)/shard_map/all_gather | solution.py:628
  161.3 68.0 %all-gather.19.cloned.1.call-start = ((), (), s32[]{:S(2)}) async-start(), calls=%async_computation.16 | async-start | bytes 1310720 | tf_op jit(solution)/shard_map/all_gather | solution.py:628
  195.6 358.6 %reduce-scatter.7.cloned.1.call-start = ((), (), s32[]{:S(2)}) async-start(), calls=%async_computation.6 | async-start | bytes 1310720 | tf_op jit(solution)/shard_map/reduce_scatter | solution.py:838
  229.3 40.6 %collective-permute-start.21 = (bf16[8,1,128,1024]{3,2,1,0:T(8,128)(2,1)}, bf16[8,1,128,1024]{3,2,1,0:T(8,128)(2,1)}, u32[]{:S(2)}, u32[]{:S(2)}) collective-permute-start(bf16[8,1,128,1024]{3,2,1,0:T(8,128)(2,1)} %pad_maximum_fusion.3.refs_0_), channel_id=1, source_target_pairs={{0,16},{4,12},{8,24},{12,4},{16,0},{20,28},{24,8},{28,20},{1,17},{... | collective-permute-start | bytes 6291464 | tf_op jit(solution)/shard_map/ppermute | solution.py:598
  230.8 39.0 %collective-permute-start.19 = (bf16[8,3,128,256]{3,2,1,0:T(8,128)(2,1)S(1)}, bf16[8,3,128,256]{3,2,1,0:T(8,128)(2,1)}, u32[]{:S(2)}, u32[]{:S(2)}) collective-permute-start(bf16[8,3,128,256]{3,2,1,0:T(8,128)(2,1)S(1)} %copy-done.13), channel_id=1, source_target_pairs={{0,4},{4,0},{1,5},{5,1},{2,6},{6,2},{3,7},{7,3},{8,12},{12,8},{9,1... | collective-permute-start | bytes 4718600 | tf_op jit(solution)/shard_map/ppermute | solution.py:599
  230.8 39.0 %collective-permute-start.20 = (bf16[8,3,128,256]{3,2,1,0:T(8,128)(2,1)}, bf16[8,3,128,256]{3,2,1,0:T(8,128)(2,1)}, u32[]{:S(2)}, u32[]{:S(2)}) collective-permute-start(bf16[8,3,128,256]{3,2,1,0:T(8,128)(2,1)} %collective-permute-done.13.refs_1_), channel_id=1, source_target_pairs={{0,4},{4,0},{1,5},{5,1},{2,6},{6,2},{3,7},{7,3},{8,12},{12,8},{9,1... | collective-permute-start | bytes 4718600 | tf_op jit(solution)/shard_map/ppermute | solution.py:599
  231.4 35.4 %collective-permute-start.22 = (bf16[4,1024,128]{2,1,0:T(8,128)(2,1)}, bf16[4,1024,128]{2,1,0:T(8,128)(2,1)}, u32[]{:S(2)}, u32[]{:S(2)}) collective-permute-start(bf16[4,1024,128]{2,1,0:T(8,128)(2,1)} %bitcast.410), channel_id=1, source_target_pairs={{0,8},{4,20},{8,0},{12,28},{16,24},{20,4},{24,16},{28,12},{1,9},{5... | collective-permute-start | bytes 3145736 | tf_op jit(solution)/shard_map/ppermute | solution.py:598
  271.8 43.9 %collective-permute-start.24 = (bf16[8,1,128,1024]{3,2,1,0:T(8,128)(2,1)}, bf16[8,1,128,1024]{3,2,1,0:T(8,128)(2,1)}, u32[]{:S(2)}, u32[]{:S(2)}) collective-permute-start(bf16[8,1,128,1024]{3,2,1,0:T(8,128)(2,1)} %pad_maximum_fusion.3.refs_0_), channel_id=1, source_target_pairs={{0,4},{4,0},{1,5},{5,1},{2,6},{6,2},{3,7},{7,3},{8,12},{12,8},{9,1... | collective-permute-start | bytes 6291464 | tf_op jit(solution)/shard_map/ppermute | solution.py:599
  272.0 43.6 %collective-permute-start.25 = (bf16[8,1,128,1024]{3,2,1,0:T(8,128)(2,1)}, bf16[8,1,128,1024]{3,2,1,0:T(8,128)(2,1)}, u32[]{:S(2)}, u32[]{:S(2)}) collective-permute-start(bf16[8,1,128,1024]{3,2,1,0:T(8,128)(2,1)} %collective-permute-done.21.refs_1_), channel_id=1, source_target_pairs={{0,4},{4,0},{1,5},{5,1},{2,6},{6,2},{3,7},{7,3},{8,12},{12,8},{9,1... | collective-permute-start | bytes 6291464 | tf_op jit(solution)/shard_map/ppermute | solution.py:599
  272.4 43.3 %collective-permute-start.26 = (bf16[8,1024,128]{2,1,0:T(8,128)(2,1)}, bf16[8,1024,128]{2,1,0:T(8,128)(2,1)}, u32[]{:S(2)}, u32[]{:S(2)}) collective-permute-start(bf16[8,1024,128]{2,1,0:T(8,128)(2,1)} %pad_maximum_fusion.4.refs_0_), channel_id=1, source_target_pairs={{0,16},{4,12},{8,24},{12,4},{16,0},{20,28},{24,8},{28,20},{1,17},{... | collective-permute-start | bytes 6291464 | tf_op jit(solution)/shard_map/ppermute | solution.py:598
  421.6 37.3 %collective-permute-start.39 = (bf16[256,4096]{1,0:T(8,128)(2,1)S(1)}, bf16[256,4096]{1,0:T(8,128)(2,1)S(1)}, u32[]{:S(2)}, u32[]{:S(2)}) collective-permute-start(bf16[256,4096]{1,0:T(8,128)(2,1)S(1)} %fusion.10), channel_id=1, source_target_pairs={{0,16},{4,12},{8,24},{12,4},{16,0},{20,28},{24,8},{28,20},{1,17},{... | collective-permute-start | bytes 6291464 | tf_op jit(solution)/shard_map/ppermute | solution.py:598
  430.6 49.5 %collective-permute-start.42 = (bf16[512,1024]{1,0:T(8,128)(2,1)}, bf16[512,1024]{1,0:T(8,128)(2,1)}, u32[]{:S(2)}, u32[]{:S(2)}) collective-permute-start(bf16[512,1024]{1,0:T(8,128)(2,1)} %convolution_convert_fusion.8), channel_id=1, source_target_pairs={{0,4},{4,0},{1,5},{5,1},{2,6},{6,2},{3,7},{7,3},{8,12},{12,8},{9,1... | collective-permute-start | bytes 3145736 | tf_op jit(solution)/shard_map/ppermute | solution.py:599
  468.9 100.5 %reduce-scatter.9.cloned.1.call-start = ((), (), s32[]{:S(2)}) async-start(), calls=%async_computation.7 | async-start | bytes 1310720 | tf_op jit(solution)/shard_map/reduce_scatter | solution.py:838
  482.5 71.7 %collective-permute-start.44 = (bf16[256,1024]{1,0:T(8,128)(2,1)}, bf16[256,1024]{1,0:T(8,128)(2,1)}, u32[]{:S(2)}, u32[]{:S(2)}) collective-permute-start(bf16[256,1024]{1,0:T(8,128)(2,1)} %fusion.108), channel_id=1, source_target_pairs={{0,16},{4,12},{8,24},{12,4},{16,0},{20,28},{24,8},{28,20},{1,17},{... | collective-permute-start | bytes 1572872 | tf_op jit(solution)/shard_map/ppermute | solution.py:598
  485.9 68.3 %collective-permute-start.43 = (bf16[256,2048]{1,0:T(8,128)(2,1)}, bf16[256,2048]{1,0:T(8,128)(2,1)}, u32[]{:S(2)}, u32[]{:S(2)}) collective-permute-start(bf16[256,2048]{1,0:T(8,128)(2,1)} %fusion.33), channel_id=1, source_target_pairs={{0,16},{4,12},{8,24},{12,4},{16,0},{20,28},{24,8},{28,20},{1,17},{... | collective-permute-start | bytes 3145736 | tf_op jit(solution)/shard_map/ppermute | solution.py:598
  490.5 186.5 %reduce-scatter.11.cloned.1.call-start = ((), (), s32[]{:S(2)}) async-start(), calls=%async_computation.8 | async-start | bytes 983040 | tf_op jit(solution)/shard_map/reduce_scatter | solution.py:838
  650.1 53.7 %reduce-scatter.13.cloned.1.call-start = ((), (), s32[]{:S(2)}) async-start(), calls=%async_computation.9 | async-start | bytes 1310720 | tf_op jit(solution)/shard_map/reduce_scatter | solution.py:838
  679.1 96.1 %reduce-scatter.17.cloned.1.call-start = ((), (), s32[]{:S(2)}) async-start(), calls=%async_computation.11 | async-start | bytes 1310720 | tf_op jit(solution)/shard_map/reduce_scatter | solution.py:838
  703.8 37.6 %collective-permute-start.63 = (bf16[256,4096]{1,0:T(8,128)(2,1)}, bf16[256,4096]{1,0:T(8,128)(2,1)}, u32[]{:S(2)}, u32[]{:S(2)}) collective-permute-start(bf16[256,4096]{1,0:T(8,128)(2,1)} %fusion.14), channel_id=1, source_target_pairs={{0,16},{4,12},{8,24},{12,4},{16,0},{20,28},{24,8},{28,20},{1,17},{... | collective-permute-start | bytes 6291464 | tf_op jit(solution)/shard_map/ppermute | solution.py:598
  750.2 54.8 %reduce-scatter.15.cloned.1.call-start = ((), (), s32[]{:S(2)}) async-start(), calls=%async_computation.10 | async-start | bytes 1474560 | tf_op jit(solution)/shard_map/reduce_scatter | solution.py:853
  (213 other events, 2696.8 us)
Sparse Core Ops, SparseCore 0:
  10.2 33.1 all-gather.10
  45.0 26.9 all-gather.12
  74.1 42.9 all-gather.14
  161.4 31.5 all-gather.16
  195.7 33.5 all-gather.18
  469.0 26.5 reduce-scatter.6
  498.0 25.7 reduce-scatter.8
  650.2 20.5 reduce-scatter.10
  679.1 24.1 reduce-scatter.12
  750.3 24.4 reduce-scatter.16
  777.1 27.8 reduce-scatter.14

commit v5 on v4

--- a/solution.py
+++ b/solution.py
@@ -624,6 +624,10 @@
     return blocks.transpose(1, 0, 2).reshape(columns, rows)
 
 
+def gather_t_turned(place, shard):
+    return jnp.stack([shard] + [place.turn(shard, "t", step) for step in place.steps("t")])
+
+
 def gather_t(place, shard):
     return lax.all_gather(shard, TENSOR, axis=0)
 
@@ -640,7 +644,7 @@
     return stacks + [place.turn(stack, "core", 1) for stack in stacks]
 
 
-def assemble(place, stacks, targets):
+def assemble(place, stacks, targets, turned=False):
     counts, dp_count, t_count = place.count, place.dp_count, place.count["t"]
     dtype = stacks[0].dtype
     shard_shape = stacks[0].shape[1:]
@@ -689,7 +693,7 @@
                     x_spot = jnp.where(core == 1, x_other, x_spot)
                 dp_spot = (y_spot * counts["x"] + x_spot) * 2 + core
                 for t_step in range(t_count):
-                    t_spot = t_step
+                    t_spot = lax.rem(meta_ref[3] - t_step + t_count, t_count) if turned else t_step
                     shard_ref = stack_ref.at[a_step * t_count + t_step]
                     for target, out_ref in zip(targets, out_refs):
                         t_columns = pl.ds(pl.multiple_of(t_spot * columns, columns), columns)
@@ -1016,7 +1020,7 @@
     )
 
     own_facts = jnp.stack([clip_valid, frame_counts])
-    up_one = gather_t(place, shard_up_one)
+    up_one = gather_t_turned(place, shard_up_one)
     up_one, first_down, own_facts = fence(up_one, first_down, own_facts)
     up_one = gather_a(place, up_one)
     down_one = gather_t(place, first_down)
@@ -1029,11 +1033,12 @@
     up_one, down_one, second_up = fence(up_one, down_one, second_up)
     up_one = gather_core(place, up_one)
     down_one = gather_b(place, down_one)
+    up_one, down_one, second_up = fence(up_one, down_one, second_up)
     attend_mix = gather_a(place, both_mix[:, : attend_in.shape[0] + 1])
     point_mix = both_mix[:, attend_in.shape[0] + 1 :]
     up_two = gather_t(place, second_up[None])
     up_one, vector_slabs = assemble(
-        place, up_one, [("rows", 0, 1, up_rows), ("slabs", up_rows, vector_rows)]
+        place, up_one, [("rows", 0, 1, up_rows), ("slabs", up_rows, vector_rows)], turned=True
     )
     up_one = up_one[0]
     vector_wide = vector_slabs.reshape(place.dp_count, vector_rows, vector_parts, -1)

time: 824 us -> 811 us (0.984)
  waiting for transfers between devices: 239 us -> 222 us
  starting transfers between devices: 85.9 us -> 95.3 us
    all_gather x5 -> x4, waiting for transfers between devices: 56.3 us -> 24.5 us  [gather_t(): return lax.all_gather(shard, TENSOR, axis=0)]
    ppermute x30 -> x33, waiting for transfers between devices: 11.2 us -> 29.1 us  [turn(): return lax.ppermute(block, self.names.get(axis, axis), pairs)]
    ppermute x30 -> x33, starting transfers between devices: 21.3 us -> 27.4 us  [turn(): return lax.ppermute(block, self.names.get(axis, axis), pairs)]
    unnamed x320 -> x323, local copies, waits for them, and re-layouts: 19.2 us -> 20.2 us
  transfers between devices with their start and end apart: 83 -> 85, of which waited for: 30 -> 31; matrix products, arithmetic and copies ran while one was open for 34% -> 33% of each run, Pallas kernels for 16% -> 15%
where the time goes in v5:
time: 811 us; the launch traced here: 802 us
  waiting for transfers between devices  222 us (27%)
  matrix products  204 us (25%)
  Pallas kernels  132 us (16%)
  other arithmetic  97.1 us (12%)
  starting transfers between devices  95.3 us (12%)
  local copies, waits for them, and re-layouts  34.4 us (4%)
  between operations  17.5 us (2%)
    dot_general x55, matrix products, dot_f32(): lax.dot_general(left_side, right_side, dims, preferred_element_type=jnp.f...  202 us
    ppermute x32, waiting for transfers between devices, turn(): return lax.ppermute(block, ('y', 'x', 'core'), pairs)  117 us
    pallas_call x1, Pallas kernels, attend_back(): pl.pallas_call(functools.partial(attend_back_kernel, count), grid_spec=pl...  54.4 us
    ppermute x32, starting transfers between devices, turn(): return lax.ppermute(block, ('y', 'x', 'core'), pairs)  39.4 us
    ppermute x33, waiting for transfers between devices, turn(): return lax.ppermute(block, self.names.get(axis, axis), pairs)  29.1 us
    reduce_scatter x1, waiting for transfers between devices, reduce_t_vectors(): result = lax.psum_scatter(jnp.stack(blocks), TENSOR, scatter_dimension=0)  28 us
    pallas_call x1, Pallas kernels, attend(): pl.pallas_call(functools.partial(attend_kernel, count), grid_spec=pltpu.P...  27.6 us
    ppermute x33, starting transfers between devices, turn(): return lax.ppermute(block, self.names.get(axis, axis), pairs)  27.4 us
  transfers between devices with their start and end apart: 85, of which 31 were waited for; matrix products, arithmetic and copies ran while one was open for 33% of the time, Pallas kernels for 15%

profile of v5, /device:TPU:0, one launch (start us, length us, event | category | flops | bytes accessed | tf_op | source)
XLA Modules:
  0.0 802.4 jit_solution(6687118983447740497)
XLA Ops:
  22.2 11.8 %collective-permute-done.1 = bf16[1,144,1024]{2,1,0:T(8,128)(2,1)S(1)} collective-permute-done((bf16[1,144,1024]{2,1,0:T(8,128)(2,1)S(1)}, bf16[1,144,1024]{2,1,0:T(8,128)(2,1)S(1)}, u32[]{:S(2)}, u32[]{:S(2)}) %collective-permute-start.1) | collective-permute-done | bytes 294944 | tf_op jit(solution)/shard_map/ppermute | solution.py:599
  36.9 13.6 %collective-permute-done.3 = bf16[4,1,144,1024]{3,2,1,0:T(8,128)(2,1)} collective-permute-done((bf16[4,1,144,1024]{3,2,1,0:T(8,128)(2,1)S(1)}, bf16[4,1,144,1024]{3,2,1,0:T(8,128)(2,1)}, u32[]{:S(2)}, u32[]{:S(2)}) %collective-permute-start.3) | collective-permute-done | bytes 1179680 | tf_op jit(solution)/shard_map/ppermute | solution.py:598
  53.7 14.7 %all-gather.9.cloned.1.call-done = bf16[4096,128]{1,0:T(8,128)(2,1)} async-done(((bf16[1024,128]{1,0:T(8,128)(2,1)}), bf16[4096,128]{1,0:T(8,128)(2,1)}) %all-gather.9.cloned.1.call-update) | async-done | bytes 1048592 | tf_op jit(solution)/shard_map/all_gather | solution.py:632
  69.8 20.4 %collective-permute-done.5 = bf16[4,1024,128]{2,1,0:T(8,128)(2,1)S(1)} collective-permute-done((bf16[4,1024,128]{2,1,0:T(8,128)(2,1)}, bf16[4,1024,128]{2,1,0:T(8,128)(2,1)S(1)}, u32[]{:S(2)}, u32[]{:S(2)}) %collective-permute-start.5) | collective-permute-done | bytes 1048608 | tf_op jit(solution)/shard_map/ppermute | solution.py:598
  105.0 8.6 %all-gather.11.cloned.1.call-done = bf16[28,128,256]{2,1,0:T(8,128)(2,1)} async-done(((bf16[7,128,256]{2,1,0:T(8,128)(2,1)}), bf16[28,128,256]{2,1,0:T(8,128)(2,1)}) %all-gather.11.cloned.1.call-update) | async-done | bytes 1835024 | tf_op jit(solution)/shard_map/all_gather | solution.py:632
  125.5 6.6 collective-permute-done.9
  140.5 8.5 %add_convert_fusion.1 = (bf16[512,4096]{1,0:T(8,128)(2,1)}, bf16[512,4096]{1,0:T(8,128)(2,1)}) fusion(f32[4096]{0:T(1024)S(1)} %bitcast.465, bf16[512,1024]{1,0:T(8,128)(2,1)S(1)} %get-tuple-element.365, bf16[1,1024,4096]{2,1,0:T(8,128)(2,1)S(1)} %get-tuple-element.228), kind=kOutput, calls=%fused_computation.13 | convolution fusion | flops 4315938816 | bytes 17842176 | tf_op jit(solution)/shard_map/dot_general | solution.py:29
  154.7 16.7 %collective-permute-done.13 = bf16[4,3,128,256]{3,2,1,0:T(8,128)(2,1)S(1)} collective-permute-done((bf16[4,3,128,256]{3,2,1,0:T(8,128)(2,1)}, bf16[4,3,128,256]{3,2,1,0:T(8,128)(2,1)S(1)}, u32[]{:S(2)}, u32[]{:S(2)}) %collective-permute-start.13) | collective-permute-done | bytes 786464 | tf_op jit(solution)/shard_map/ppermute | solution.py:598
  202.7 9.2 %collective-permute-done.17 = bf16[4,1,128,1024]{3,2,1,0:T(8,128)(2,1)S(1)} collective-permute-done((bf16[4,1,128,1024]{3,2,1,0:T(8,128)(2,1)}, bf16[4,1,128,1024]{3,2,1,0:T(8,128)(2,1)S(1)}, u32[]{:S(2)}, u32[]{:S(2)}) %collective-permute-start.17) | collective-permute-done | bytes 1048608 | tf_op jit(solution)/shard_map/ppermute | solution.py:598
  228.4 27.6 %attend.1 = (bf16[512,1024]{1,0:T(8,128)(2,1)S(1)}, f32[512,128]{1,0:T(8,128)S(1)}) custom-call(s32[3]{0:T(128)S(1)} %pad_add_fusion.2.meta_ref, bf16[512,1024]{1,0:T(8,128)(2,1)S(1)} %copy-done.13, bf16[256,128]{1,0:T(8,128)(2,1)S(1)} %pad_maximum_fusion.18.e_ref, bf16[512,1024]{1,0:T(8,128)(2,1)S(1)} %fusion.89.refs_0_, ...), custom_call_target="tpu_custom_call" | custom-call | tf_op jit(solution)/shard_map/attend/pallas_call | solution.py:309
  287.2 8.9 %convolve.1 = (f32[512,1024]{1,0:T(8,128)S(1)}, bf16[512,1024]{1,0:T(8,128)(2,1)S(1)}) custom-call(f32[32,1024]{1,0:T(8,128)S(1)} %collective-permute-done.32.before_ref, f32[512,1024]{1,0:T(8,128)S(1)} %get-tuple-element.580.gated_ref, f32[31,1024]{1,0:T(8,128)S(1)} %slice.760.taps_ref, f32[1,1024]{1,0:T(1,128)S(1)} %get-tuple-element.559.gain_ref, ...), custom_call_target="tpu_custom_call" | custom-call | tf_op jit(solution)/shard_map/convolve/pallas_call | solution.py:465
  317.7 7.9 add_convert_fusion
  357.9 10.0 %convert_reduce_fusion = (f32[4096]{0:T(1024)}, bf16[512,4096]{1,0:T(8,128)(2,1)S(1)}) fusion(bf16[512,4096]{1,0:T(8,128)(2,1)} %get-tuple-element.285, bf16[4096,1024]{1,0:T(8,128)(2,1)} %copy-done.9, f32[512,1024]{1,0:T(8,128)S(1)} %copy-done.67), kind=kOutput, calls=%fused_computation.5 | convolution fusion | flops 4306497536 | bytes 18890752 | tf_op jit(solution)/shard_map/dot_general | solution.py:29
  384.7 7.9 multiply_reduce_fusion
  420.4 15.5 %convolve_back.1 = (bf16[512,2048]{1,0:T(8,128)(2,1)S(1)}, f32[31,1024]{1,0:T(8,128)S(1)}) custom-call(s32[3]{0:T(128)S(1)} %pad_add_fusion.2.meta_ref, f32[512,1024]{1,0:T(8,128)S(1)} %subtract_multiply_fusion.grad_ref, f32[32,1024]{1,0:T(8,128)S(1)} %collective-permute-done.38.after_ref, f32[32,1024]{1,0:T(8,128)S(1)} %collective-permute-done.32.before_ref, ...), custom_call_target="tpu_custom_call" | custom-call | tf_op jit(solution)/shard_map/convolve_back/pallas_call | solution.py:537
  477.9 54.4 %attend_back.1 = (bf16[512,1024]{1,0:T(8,128)(2,1)S(1)}, f32[128,256]{1,0:T(8,128)S(1)}, bf16[512,1024]{1,0:T(8,128)(2,1)S(1)}, bf16[512,1024]{1,0:T(8,128)(2,1)...) custom-call(s32[3]{0:T(128)S(1)} %pad_add_fusion.2.meta_ref, ...), custom_call_target="tpu_custom_call" | custom-call | tf_op jit(solution)/shard_map/attend_back/pallas_call | solution.py:339
  598.3 9.1 %convert_reduce_fusion.1 = (f32[4096]{0:T(1024)S(1)}, bf16[512,4096]{1,0:T(8,128)(2,1)S(1)}) fusion(bf16[512,4096]{1,0:T(8,128)(2,1)} %get-tuple-element.363, bf16[4096,1024]{1,0:T(8,128)(2,1)} %copy-done.7, f32[512,1024]{1,0:T(8,128)S(1)} %copy-done.59), kind=kOutput, calls=%fused_computation.6 | convolution fusion | flops 4306497536 | bytes 18890752 | tf_op jit(solution)/shard_map/dot_general | solution.py:29
  608.7 13.8 %collective-permute-done.58 = bf16[256,1024]{1,0:T(8,128)(2,1)S(1)} collective-permute-done((bf16[256,1024]{1,0:T(8,128)(2,1)}, bf16[256,1024]{1,0:T(8,128)(2,1)S(1)}, u32[]{:S(2)}, u32[]{:S(2)}) %collective-permute-start.58) | collective-permute-done | bytes 524320 | tf_op jit(solution)/shard_map/ppermute | solution.py:598
  641.0 8.0 %collective-permute-done.60 = bf16[128,1024]{1,0:T(8,128)(2,1)S(1)} collective-permute-done((bf16[128,1024]{1,0:T(8,128)(2,1)S(1)}, bf16[128,1024]{1,0:T(8,128)(2,1)S(1)}, u32[]{:S(2)}, u32[]{:S(2)}) %collective-permute-start.60) | collective-permute-done | bytes 262176 | tf_op jit(solution)/shard_map/ppermute | solution.py:598
  665.8 10.5 %multiply_reduce_fusion.4 = (f32[1024]{0:T(1024)S(1)}, f32[512]{0:T(512)S(1)}, f32[512]{0:T(512)S(1)}, f32[1024]{0:T(1024)S(1)}, f32[512,1024]{1,0:T(8,128)S(1)}) fusion(f32[512,1024]{1,0:T(8,128)} %get-tuple-element.383, f32[1024]{0:T(1024)S(1)} %bitcast.445, bf16[512,4096]{1,0:T(8,128)(2,1)} %copy-done.43, bf16[1,1024,4096]{2,1,0:T(8,128)(2,1)} %copy-done.27), kind=kOutput, calls=%fused_computation.117 | convolution fusion | flops 4298634240 | bytes 16793600 | tf_op jit(solution)/shard_map/dot_general | solution.py:29
  704.7 15.7 %collective-permute-done.70 = bf16[256,1024]{1,0:T(8,128)(2,1)S(1)} collective-permute-done((bf16[256,1024]{1,0:T(8,128)(2,1)S(1)}, bf16[256,1024]{1,0:T(8,128)(2,1)S(1)}, u32[]{:S(2)}, u32[]{:S(2)}) %collective-permute-start.70) | collective-permute-done | bytes 524320 | tf_op jit(solution)/shard_map/ppermute | solution.py:924
  721.5 6.9 collective-permute-done.66
  737.2 9.5 %collective-permute-done.73 = f32[56,128]{1,0:T(8,128)S(1)} collective-permute-done((f32[56,128]{1,0:T(8,128)S(1)}, f32[56,128]{1,0:T(8,128)S(1)}, u32[]{:S(2)}, u32[]{:S(2)}) %collective-permute-start.73) | collective-permute-done | bytes 28704 | tf_op jit(solution)/shard_map/ppermute | solution.py:598
  764.0 28.0 %reduce-scatter.15.cloned.1.call-done = bf16[1,144,1024]{2,1,0:T(8,128)(2,1)} async-done(((bf16[4,144,1024]{2,1,0:T(8,128)(2,1)}), bf16[1,144,1024]{2,1,0:T(8,128)(2,1)}) %reduce-scatter.15.cloned.1.call-update) | async-done | bytes 294928 | tf_op jit(solution)/shard_map/reduce_scatter | solution.py:857
  (730 shorter events, 441.2 us)
Async XLA Ops:
  7.2 61.1 %all-gather.9.cloned.1.call-start = ((), (), s32[]{:S(2)}) async-start(), calls=%async_computation.12 | async-start | bytes 1310720 | tf_op jit(solution)/shard_map/all_gather | solution.py:632
  35.7 77.9 %all-gather.11.cloned.1.call-start = ((), (), s32[]{:S(2)}) async-start(), calls=%async_computation.13 | async-start | bytes 2293760 | tf_op jit(solution)/shard_map/all_gather | solution.py:632
  52.0 41.0 %collective-permute-start.4 = (bf16[8,1,144,1024]{3,2,1,0:T(8,128)(2,1)S(1)}, bf16[8,1,144,1024]{3,2,1,0:T(8,128)(2,1)}, u32[]{:S(2)}, u32[]{:S(2)}) collective-permute-start(bf16[8,1,144,1024]{3,2,1,0:T(8,128)(2,1)S(1)} %pad_maximum_fusion.refs_0_), channel_id=1, source_target_pairs={{0,16},{4,12},{8,24},{12,4},{16,0},{20,28},{24,8},{28,20},{1,17},{... | collective-permute-start | bytes 7077896 | tf_op jit(solution)/shard_map/ppermute | solution.py:598
  53.6 132.0 %all-gather.13.cloned.1.call-start = ((), (), s32[]{:S(2)}) async-start(), calls=%async_computation.14 | async-start | bytes 1310720 | tf_op jit(solution)/shard_map/all_gather | solution.py:632
  93.0 40.7 %collective-permute-start.6 = (bf16[8,1,144,1024]{3,2,1,0:T(8,128)(2,1)S(1)}, bf16[8,1,144,1024]{3,2,1,0:T(8,128)(2,1)}, u32[]{:S(2)}, u32[]{:S(2)}) collective-permute-start(bf16[8,1,144,1024]{3,2,1,0:T(8,128)(2,1)S(1)} %pad_maximum_fusion.refs_0_), channel_id=1, source_target_pairs={{0,4},{4,0},{1,5},{5,1},{2,6},{6,2},{3,7},{7,3},{8,12},{12,8},{9,1... | collective-permute-start | bytes 7077896 | tf_op jit(solution)/shard_map/ppermute | solution.py:599
  95.1 38.6 %collective-permute-start.7 = (bf16[8,1,144,1024]{3,2,1,0:T(8,128)(2,1)}, bf16[8,1,144,1024]{3,2,1,0:T(8,128)(2,1)}, u32[]{:S(2)}, u32[]{:S(2)}) collective-permute-start(bf16[8,1,144,1024]{3,2,1,0:T(8,128)(2,1)} %collective-permute-done.4.refs_1_), channel_id=1, source_target_pairs={{0,4},{4,0},{1,5},{5,1},{2,6},{6,2},{3,7},{7,3},{8,12},{12,8},{9,1... | collective-permute-start | bytes 7077896 | tf_op jit(solution)/shard_map/ppermute | solution.py:599
  95.2 38.5 %collective-permute-start.8 = (bf16[8,1024,128]{2,1,0:T(8,128)(2,1)}, bf16[8,1024,128]{2,1,0:T(8,128)(2,1)}, u32[]{:S(2)}, u32[]{:S(2)}) collective-permute-start(bf16[8,1024,128]{2,1,0:T(8,128)(2,1)} %pad_maximum_fusion.1.refs_0_), channel_id=1, source_target_pairs={{0,16},{4,12},{8,24},{12,4},{16,0},{20,28},{24,8},{28,20},{1,17},{... | collective-permute-start | bytes 6291464 | tf_op jit(solution)/shard_map/ppermute | solution.py:598
  154.4 62.6 %all-gather.15.cloned.1.call-start = ((), (), s32[]{:S(2)}) async-start(), calls=%async_computation.15 | async-start | bytes 1310720 | tf_op jit(solution)/shard_map/all_gather | solution.py:632
  186.3 354.9 %reduce-scatter.7.cloned.1.call-start = ((), (), s32[]{:S(2)}) async-start(), calls=%async_computation.6 | async-start | bytes 1310720 | tf_op jit(solution)/shard_map/reduce_scatter | solution.py:842
  217.8 41.3 %collective-permute-start.24 = (bf16[8,1,128,1024]{3,2,1,0:T(8,128)(2,1)}, bf16[8,1,128,1024]{3,2,1,0:T(8,128)(2,1)}, u32[]{:S(2)}, u32[]{:S(2)}) collective-permute-start(bf16[8,1,128,1024]{3,2,1,0:T(8,128)(2,1)} %pad_maximum_fusion.3.refs_0_), channel_id=1, source_target_pairs={{0,16},{4,12},{8,24},{12,4},{16,0},{20,28},{24,8},{28,20},{1,17},{... | collective-permute-start | bytes 6291464 | tf_op jit(solution)/shard_map/ppermute | solution.py:598
  219.6 39.6 %collective-permute-start.22 = (bf16[8,3,128,256]{3,2,1,0:T(8,128)(2,1)S(1)}, bf16[8,3,128,256]{3,2,1,0:T(8,128)(2,1)}, u32[]{:S(2)}, u32[]{:S(2)}) collective-permute-start(bf16[8,3,128,256]{3,2,1,0:T(8,128)(2,1)S(1)} %pad_maximum_fusion.5.refs_0_), channel_id=1, source_target_pairs={{0,4},{4,0},{1,5},{5,1},{2,6},{6,2},{3,7},{7,3},{8,12},{12,8},{9,1... | collective-permute-start | bytes 4718600 | tf_op jit(solution)/shard_map/ppermute | solution.py:599
  219.6 39.6 %collective-permute-start.23 = (bf16[8,3,128,256]{3,2,1,0:T(8,128)(2,1)}, bf16[8,3,128,256]{3,2,1,0:T(8,128)(2,1)}, u32[]{:S(2)}, u32[]{:S(2)}) collective-permute-start(bf16[8,3,128,256]{3,2,1,0:T(8,128)(2,1)} %collective-permute-done.16.refs_1_), channel_id=1, source_target_pairs={{0,4},{4,0},{1,5},{5,1},{2,6},{6,2},{3,7},{7,3},{8,12},{12,8},{9,1... | collective-permute-start | bytes 4718600 | tf_op jit(solution)/shard_map/ppermute | solution.py:599
  261.1 42.6 %collective-permute-start.27 = (bf16[8,1,128,1024]{3,2,1,0:T(8,128)(2,1)}, bf16[8,1,128,1024]{3,2,1,0:T(8,128)(2,1)}, u32[]{:S(2)}, u32[]{:S(2)}) collective-permute-start(bf16[8,1,128,1024]{3,2,1,0:T(8,128)(2,1)} %pad_maximum_fusion.3.refs_0_), channel_id=1, source_target_pairs={{0,4},{4,0},{1,5},{5,1},{2,6},{6,2},{3,7},{7,3},{8,12},{12,8},{9,1... | collective-permute-start | bytes 6291464 | tf_op jit(solution)/shard_map/ppermute | solution.py:599
  261.3 42.4 %collective-permute-start.28 = (bf16[8,1,128,1024]{3,2,1,0:T(8,128)(2,1)}, bf16[8,1,128,1024]{3,2,1,0:T(8,128)(2,1)}, u32[]{:S(2)}, u32[]{:S(2)}) collective-permute-start(bf16[8,1,128,1024]{3,2,1,0:T(8,128)(2,1)} %collective-permute-done.24.refs_1_), channel_id=1, source_target_pairs={{0,4},{4,0},{1,5},{5,1},{2,6},{6,2},{3,7},{7,3},{8,12},{12,8},{9,1... | collective-permute-start | bytes 6291464 | tf_op jit(solution)/shard_map/ppermute | solution.py:599
  261.7 42.1 %collective-permute-start.29 = (bf16[8,1024,128]{2,1,0:T(8,128)(2,1)}, bf16[8,1024,128]{2,1,0:T(8,128)(2,1)}, u32[]{:S(2)}, u32[]{:S(2)}) collective-permute-start(bf16[8,1024,128]{2,1,0:T(8,128)(2,1)} %pad_maximum_fusion.4.refs_0_), channel_id=1, source_target_pairs={{0,16},{4,12},{8,24},{12,4},{16,0},{20,28},{24,8},{28,20},{1,17},{... | collective-permute-start | bytes 6291464 | tf_op jit(solution)/shard_map/ppermute | solution.py:598
  418.4 49.8 %collective-permute-start.45 = (bf16[512,1024]{1,0:T(8,128)(2,1)}, bf16[512,1024]{1,0:T(8,128)(2,1)}, u32[]{:S(2)}, u32[]{:S(2)}) collective-permute-start(bf16[512,1024]{1,0:T(8,128)(2,1)} %convolution_convert_fusion.8), channel_id=1, source_target_pairs={{0,4},{4,0},{1,5},{5,1},{2,6},{6,2},{3,7},{7,3},{8,12},{12,8},{9,1... | collective-permute-start | bytes 3145736 | tf_op jit(solution)/shard_map/ppermute | solution.py:599
  457.1 99.3 %reduce-scatter.9.cloned.1.call-start = ((), (), s32[]{:S(2)}) async-start(), calls=%async_computation.7 | async-start | bytes 1310720 | tf_op jit(solution)/shard_map/reduce_scatter | solution.py:842
  470.6 70.5 %collective-permute-start.47 = (bf16[256,1024]{1,0:T(8,128)(2,1)}, bf16[256,1024]{1,0:T(8,128)(2,1)}, u32[]{:S(2)}, u32[]{:S(2)}) collective-permute-start(bf16[256,1024]{1,0:T(8,128)(2,1)} %fusion.108), channel_id=1, source_target_pairs={{0,16},{4,12},{8,24},{12,4},{16,0},{20,28},{24,8},{28,20},{1,17},{... | collective-permute-start | bytes 1572872 | tf_op jit(solution)/shard_map/ppermute | solution.py:598
  474.0 67.2 %collective-permute-start.46 = (bf16[256,2048]{1,0:T(8,128)(2,1)}, bf16[256,2048]{1,0:T(8,128)(2,1)}, u32[]{:S(2)}, u32[]{:S(2)}) collective-permute-start(bf16[256,2048]{1,0:T(8,128)(2,1)} %fusion.33), channel_id=1, source_target_pairs={{0,16},{4,12},{8,24},{12,4},{16,0},{20,28},{24,8},{28,20},{1,17},{... | collective-permute-start | bytes 3145736 | tf_op jit(solution)/shard_map/ppermute | solution.py:598
  477.4 185.8 %reduce-scatter.11.cloned.1.call-start = ((), (), s32[]{:S(2)}) async-start(), calls=%async_computation.8 | async-start | bytes 983040 | tf_op jit(solution)/shard_map/reduce_scatter | solution.py:842
  636.4 54.4 %reduce-scatter.13.cloned.1.call-start = ((), (), s32[]{:S(2)}) async-start(), calls=%async_computation.9 | async-start | bytes 1310720 | tf_op jit(solution)/shard_map/reduce_scatter | solution.py:842
  665.4 96.6 %reduce-scatter.17.cloned.1.call-start = ((), (), s32[]{:S(2)}) async-start(), calls=%async_computation.11 | async-start | bytes 1310720 | tf_op jit(solution)/shard_map/reduce_scatter | solution.py:842
  690.8 37.6 %collective-permute-start.66 = (bf16[256,4096]{1,0:T(8,128)(2,1)}, bf16[256,4096]{1,0:T(8,128)(2,1)}, u32[]{:S(2)}, u32[]{:S(2)}) collective-permute-start(bf16[256,4096]{1,0:T(8,128)(2,1)} %fusion.14), channel_id=1, source_target_pairs={{0,16},{4,12},{8,24},{12,4},{16,0},{20,28},{24,8},{28,20},{1,17},{... | collective-permute-start | bytes 6291464 | tf_op jit(solution)/shard_map/ppermute | solution.py:598
  737.0 55.0 %reduce-scatter.15.cloned.1.call-start = ((), (), s32[]{:S(2)}) async-start(), calls=%async_computation.10 | async-start | bytes 1474560 | tf_op jit(solution)/shard_map/reduce_scatter | solution.py:857
  (216 other events, 2785.6 us)
Sparse Core Ops, SparseCore 0:
  35.9 32.4 all-gather.8
  70.5 43.0 all-gather.10
  154.5 28.3 all-gather.12
  186.4 30.5 all-gather.14
  457.2 28.1 reduce-scatter.6
  487.6 25.7 reduce-scatter.8
  636.5 21.4 reduce-scatter.10
  665.4 25.1 reduce-scatter.12
  737.1 24.8 reduce-scatter.16
  764.1 27.8 reduce-scatter.14

commit v6 on v5

--- a/solution.py
+++ b/solution.py
@@ -761,12 +761,20 @@
     return (jnp.arange(width)[:, None] == sources).astype(jnp.bfloat16)
 
 
-def other_terms(place, pairs):
+def other_products(pairs):
     result = []
     for inputs, grads in pairs:
         product = dot_f32(inputs[:, : inputs.shape[1] // 2], grads, TN).astype(jnp.bfloat16)
-        result.append((inputs, grads, place.turn(product, "core", 1)))
+        result.append((inputs, grads, product))
     return result
+
+
+def send_core(place, group):
+    return [(inputs, grads, place.turn(product, "core", 1)) for inputs, grads, product in group]
+
+
+def other_terms(place, pairs):
+    return send_core(place, other_products(pairs))
 
 
 def chip_terms(place, group):
@@ -1025,7 +1033,7 @@
     up_one = gather_a(place, up_one)
     down_one = gather_t(place, first_down)
     other_facts = place.turn(own_facts, "core", 1)
-    up_one, frames, shard_mix = fence(up_one, frames, shard_mix)
+    up_one, frames, shard_mix, other_facts = fence(up_one, frames, shard_mix, other_facts)
     up_one = gather_b(place, up_one)
     rows_low = to_clip(place, clip_blocks(place, frames))
     down_one = gather_a(place, down_one)
@@ -1234,13 +1242,14 @@
     sum_attend = send_b(place, sum_attend)
     sum_point = reduce_t(sum_point)
     grad_low, grad_upper, one_up_bias, one_down_bias = feed_back_down(0.5 * grad_one, one_kept, down_one)
-    sent_low, sent_one = sent(grad_low), sent(one_kept[2])
-    (sum_attend, grad_upper, sum_distance, sent_low, sent_one, one_up_bias) = fence(
-        sum_attend, grad_upper, sum_distance, sent_low, sent_one, one_up_bias
+    sum_down_one = other_products([(sent(grad_low), one_hidden)])
+    sum_up_one = other_products([(sent(one_kept[2]), grad_upper)])
+    (sum_attend, grad_upper, sum_distance, sum_down_one, sum_up_one, one_up_bias) = fence(
+        sum_attend, grad_upper, sum_distance, sum_down_one, sum_up_one, one_up_bias
     )
     sum_attend = send_a(place, messages_a(place, sum_attend))
-    sum_down_one = other_terms(place, [(sent_low, one_hidden)])
-    sum_up_one = other_terms(place, [(sent_one, grad_upper)])
+    sum_down_one = send_core(place, sum_down_one)
+    sum_up_one = send_core(place, sum_up_one)
     sum_down_one = chip_terms(place, sum_down_one)
     sum_distance = sum_distance + place.turn(sum_distance, "core", 1)
     sum_attend = tensor_blocks(place, [(3, sum_attend[0]), (1, sum_attend[1])])

time: 811 us -> 807 us (level)
  waiting for transfers between devices: 222 us -> 212 us
    ppermute x32, waiting for transfers between devices: 117 us -> 108 us  [turn(): return lax.ppermute(block, ('y', 'x', 'core'), pairs)]
    unnamed x323 -> x319, local copies, waits for them, and re-layouts: 20.2 us -> 20.7 us
  transfers between devices with their start and end apart: 85 -> 85, of which waited for: 31 -> 28; matrix products, arithmetic and copies ran while one was open for 33% -> 34% of each run, Pallas kernels for 15% -> 16%
where the time goes in v6:
time: 807 us; the launch traced here: 798 us
  waiting for transfers between devices  212 us (26%)
  matrix products  206 us (26%)
  Pallas kernels  132 us (16%)
  other arithmetic  99.6 us (12%)
  starting transfers between devices  95.4 us (12%)
  local copies, waits for them, and re-layouts  35 us (4%)
  between operations  17.4 us (2%)
    dot_general x55, matrix products, dot_f32(): lax.dot_general(left_side, right_side, dims, preferred_element_type=jnp.f...  204 us
    ppermute x32, waiting for transfers between devices, turn(): return lax.ppermute(block, ('y', 'x', 'core'), pairs)  108 us
    pallas_call x1, Pallas kernels, attend_back(): pl.pallas_call(functools.partial(attend_back_kernel, count), grid_spec=pl...  54.4 us
    ppermute x32, starting transfers between devices, turn(): return lax.ppermute(block, ('y', 'x', 'core'), pairs)  40.1 us
    ppermute x33, waiting for transfers between devices, turn(): return lax.ppermute(block, self.names.get(axis, axis), pairs)  28 us
    reduce_scatter x1, waiting for transfers between devices, reduce_t_vectors(): result = lax.psum_scatter(jnp.stack(blocks), TENSOR, scatter_dimension=0)  28 us
    ppermute x33, starting transfers between devices, turn(): return lax.ppermute(block, self.names.get(axis, axis), pairs)  27.5 us
    pallas_call x1, Pallas kernels, attend(): pl.pallas_call(functools.partial(attend_kernel, count), grid_spec=pltpu.P...  27.5 us
  transfers between devices with their start and end apart: 85, of which 28 were waited for; matrix products, arithmetic and copies ran while one was open for 34% of the time, Pallas kernels for 16%

profile of v6, /device:TPU:0, one launch (start us, length us, event | category | flops | bytes accessed | tf_op | source)
XLA Modules:
  0.0 798.1 jit_solution(17722326039415464390)
XLA Ops:
  22.2 11.8 %collective-permute-done.1 = bf16[1,144,1024]{2,1,0:T(8,128)(2,1)S(1)} collective-permute-done((bf16[1,144,1024]{2,1,0:T(8,128)(2,1)S(1)}, bf16[1,144,1024]{2,1,0:T(8,128)(2,1)S(1)}, u32[]{:S(2)}, u32[]{:S(2)}) %collective-permute-start.1) | collective-permute-done | bytes 294944 | tf_op jit(solution)/shard_map/ppermute | solution.py:599
  36.9 13.6 %collective-permute-done.3 = bf16[4,1,144,1024]{3,2,1,0:T(8,128)(2,1)} collective-permute-done((bf16[4,1,144,1024]{3,2,1,0:T(8,128)(2,1)S(1)}, bf16[4,1,144,1024]{3,2,1,0:T(8,128)(2,1)}, u32[]{:S(2)}, u32[]{:S(2)}) %collective-permute-start.3) | collective-permute-done | bytes 1179680 | tf_op jit(solution)/shard_map/ppermute | solution.py:598
  53.7 14.7 %all-gather.9.cloned.1.call-done = bf16[4096,128]{1,0:T(8,128)(2,1)} async-done(((bf16[1024,128]{1,0:T(8,128)(2,1)}), bf16[4096,128]{1,0:T(8,128)(2,1)}) %all-gather.9.cloned.1.call-update) | async-done | bytes 1048592 | tf_op jit(solution)/shard_map/all_gather | solution.py:632
  69.8 20.4 %collective-permute-done.6 = bf16[4,1024,128]{2,1,0:T(8,128)(2,1)S(1)} collective-permute-done((bf16[4,1024,128]{2,1,0:T(8,128)(2,1)}, bf16[4,1024,128]{2,1,0:T(8,128)(2,1)S(1)}, u32[]{:S(2)}, u32[]{:S(2)}) %collective-permute-start.6) | collective-permute-done | bytes 1048608 | tf_op jit(solution)/shard_map/ppermute | solution.py:598
  105.1 8.6 %all-gather.11.cloned.1.call-done = bf16[28,128,256]{2,1,0:T(8,128)(2,1)} async-done(((bf16[7,128,256]{2,1,0:T(8,128)(2,1)}), bf16[28,128,256]{2,1,0:T(8,128)(2,1)}) %all-gather.11.cloned.1.call-update) | async-done | bytes 1835024 | tf_op jit(solution)/shard_map/all_gather | solution.py:632
  140.4 8.5 %add_convert_fusion.1 = (bf16[512,4096]{1,0:T(8,128)(2,1)}, bf16[512,4096]{1,0:T(8,128)(2,1)}) fusion(f32[4096]{0:T(1024)S(1)} %bitcast.467, bf16[512,1024]{1,0:T(8,128)(2,1)S(1)} %get-tuple-element.371, bf16[1,1024,4096]{2,1,0:T(8,128)(2,1)S(1)} %get-tuple-element.234), kind=kOutput, calls=%fused_computation.13 | convolution fusion | flops 4315938816 | bytes 17842176 | tf_op jit(solution)/shard_map/dot_general | solution.py:29
  154.6 16.8 %collective-permute-done.14 = bf16[4,3,128,256]{3,2,1,0:T(8,128)(2,1)S(1)} collective-permute-done((bf16[4,3,128,256]{3,2,1,0:T(8,128)(2,1)}, bf16[4,3,128,256]{3,2,1,0:T(8,128)(2,1)S(1)}, u32[]{:S(2)}, u32[]{:S(2)}) %collective-permute-start.14) | collective-permute-done | bytes 786464 | tf_op jit(solution)/shard_map/ppermute | solution.py:598
  202.7 9.2 %collective-permute-done.18 = bf16[4,1,128,1024]{3,2,1,0:T(8,128)(2,1)S(1)} collective-permute-done((bf16[4,1,128,1024]{3,2,1,0:T(8,128)(2,1)}, bf16[4,1,128,1024]{3,2,1,0:T(8,128)(2,1)S(1)}, u32[]{:S(2)}, u32[]{:S(2)}) %collective-permute-start.18) | collective-permute-done | bytes 1048608 | tf_op jit(solution)/shard_map/ppermute | solution.py:598
  225.4 27.5 %attend.1 = (bf16[512,1024]{1,0:T(8,128)(2,1)S(1)}, f32[512,128]{1,0:T(8,128)S(1)}) custom-call(s32[3]{0:T(128)S(1)} %pad_add_fusion.2.meta_ref, bf16[512,1024]{1,0:T(8,128)(2,1)S(1)} %copy-done.13, bf16[256,128]{1,0:T(8,128)(2,1)S(1)} %pad_maximum_fusion.18.e_ref, bf16[512,1024]{1,0:T(8,128)(2,1)S(1)} %fusion.89.refs_0_, ...), custom_call_target="tpu_custom_call" | custom-call | tf_op jit(solution)/shard_map/attend/pallas_call | solution.py:309
  282.9 8.9 %convolve.1 = (f32[512,1024]{1,0:T(8,128)S(1)}, bf16[512,1024]{1,0:T(8,128)(2,1)S(1)}) custom-call(f32[32,1024]{1,0:T(8,128)S(1)} %collective-permute-done.32.before_ref, f32[512,1024]{1,0:T(8,128)S(1)} %get-tuple-element.590.gated_ref, f32[31,1024]{1,0:T(8,128)S(1)} %slice.760.taps_ref, f32[1,1024]{1,0:T(1,128)S(1)} %get-tuple-element.569.gain_ref, ...), custom_call_target="tpu_custom_call" | custom-call | tf_op jit(solution)/shard_map/convolve/pallas_call | solution.py:465
  313.3 7.9 add_convert_fusion
  353.8 10.0 %convert_reduce_fusion = (f32[4096]{0:T(1024)}, bf16[512,4096]{1,0:T(8,128)(2,1)S(1)}) fusion(bf16[512,4096]{1,0:T(8,128)(2,1)} %get-tuple-element.291, bf16[4096,1024]{1,0:T(8,128)(2,1)} %copy-done.9, f32[512,1024]{1,0:T(8,128)S(1)} %copy-done.66), kind=kOutput, calls=%fused_computation.5 | convolution fusion | flops 4306497536 | bytes 18890752 | tf_op jit(solution)/shard_map/dot_general | solution.py:29
  382.3 7.9 multiply_reduce_fusion
  417.7 15.5 %convolve_back.1 = (bf16[512,2048]{1,0:T(8,128)(2,1)S(1)}, f32[31,1024]{1,0:T(8,128)S(1)}) custom-call(s32[3]{0:T(128)S(1)} %pad_add_fusion.2.meta_ref, f32[512,1024]{1,0:T(8,128)S(1)} %subtract_multiply_fusion.grad_ref, f32[32,1024]{1,0:T(8,128)S(1)} %collective-permute-done.38.after_ref, f32[32,1024]{1,0:T(8,128)S(1)} %collective-permute-done.32.before_ref, ...), custom_call_target="tpu_custom_call" | custom-call | tf_op jit(solution)/shard_map/convolve_back/pallas_call | solution.py:537
  475.2 54.4 %attend_back.1 = (bf16[512,1024]{1,0:T(8,128)(2,1)S(1)}, f32[128,256]{1,0:T(8,128)S(1)}, bf16[512,1024]{1,0:T(8,128)(2,1)S(1)}, bf16[512,1024]{1,0:T(8,128)(2,1)...) custom-call(s32[3]{0:T(128)S(1)} %pad_add_fusion.2.meta_ref, ...), custom_call_target="tpu_custom_call" | custom-call | tf_op jit(solution)/shard_map/attend_back/pallas_call | solution.py:339
  603.1 8.6 %convert_reduce_fusion.1 = (f32[4096]{0:T(1024)S(1)}, bf16[512,4096]{1,0:T(8,128)(2,1)}) fusion(bf16[512,4096]{1,0:T(8,128)(2,1)} %get-tuple-element.369, bf16[4096,1024]{1,0:T(8,128)(2,1)S(1)} %bitcast.396, f32[512,1024]{1,0:T(8,128)} %multiply_add_fusion.2), kind=kOutput, calls=%fused_computation.6 | convolution fusion | flops 4306497536 | bytes 18890752 | tf_op jit(solution)/shard_map/dot_general | solution.py:29
  611.7 6.9 convolution_convert_fusion
  618.6 8.8 %collective-permute-done.58 = bf16[256,1024]{1,0:T(8,128)(2,1)S(1)} collective-permute-done((bf16[256,1024]{1,0:T(8,128)(2,1)}, bf16[256,1024]{1,0:T(8,128)(2,1)S(1)}, u32[]{:S(2)}, u32[]{:S(2)}) %collective-permute-start.58) | collective-permute-done | bytes 524320 | tf_op jit(solution)/shard_map/ppermute | solution.py:598
  633.5 7.0 collective-permute-done.63
  661.9 10.4 %multiply_reduce_fusion.4 = (f32[1024]{0:T(1024)S(1)}, f32[512]{0:T(512)S(1)}, f32[512]{0:T(512)S(1)}, f32[1024]{0:T(1024)S(1)}, f32[512,1024]{1,0:T(8,128)S(1)}) fusion(f32[512,1024]{1,0:T(8,128)} %get-tuple-element.393, f32[1024]{0:T(1024)S(1)} %bitcast.447, bf16[512,4096]{1,0:T(8,128)(2,1)} %get-tuple-element.392, bf16[1,1024,4096]{2,1,0:T(8,128)(2,1)} %copy-done.27), kind=kOutput, calls=%fused_computation.117 | convolution fusion | flops 4298634240 | bytes 16793600 | tf_op jit(solution)/shard_map/dot_general | solution.py:29
  700.3 15.8 %collective-permute-done.70 = bf16[256,1024]{1,0:T(8,128)(2,1)S(1)} collective-permute-done((bf16[256,1024]{1,0:T(8,128)(2,1)}, bf16[256,1024]{1,0:T(8,128)(2,1)S(1)}, u32[]{:S(2)}, u32[]{:S(2)}) %collective-permute-start.70) | collective-permute-done | bytes 524320 | tf_op jit(solution)/shard_map/ppermute | solution.py:932
  717.2 7.1 collective-permute-done.66
  733.2 9.2 %collective-permute-done.73 = f32[56,128]{1,0:T(8,128)S(1)} collective-permute-done((f32[56,128]{1,0:T(8,128)S(1)}, f32[56,128]{1,0:T(8,128)S(1)}, u32[]{:S(2)}, u32[]{:S(2)}) %collective-permute-start.73) | collective-permute-done | bytes 28704 | tf_op jit(solution)/shard_map/ppermute | solution.py:598
  759.6 28.0 %reduce-scatter.15.cloned.1.call-done = bf16[1,144,1024]{2,1,0:T(8,128)(2,1)} async-done(((bf16[4,144,1024]{2,1,0:T(8,128)(2,1)}), bf16[1,144,1024]{2,1,0:T(8,128)(2,1)}) %reduce-scatter.15.cloned.1.call-update) | async-done | bytes 294928 | tf_op jit(solution)/shard_map/reduce_scatter | solution.py:865
  (727 shorter events, 443.2 us)
Async XLA Ops:
  7.2 61.1 %all-gather.9.cloned.1.call-start = ((), (), s32[]{:S(2)}) async-start(), calls=%async_computation.12 | async-start | bytes 1310720 | tf_op jit(solution)/shard_map/all_gather | solution.py:632
  35.7 77.9 %all-gather.11.cloned.1.call-start = ((), (), s32[]{:S(2)}) async-start(), calls=%async_computation.13 | async-start | bytes 2293760 | tf_op jit(solution)/shard_map/all_gather | solution.py:632
  52.0 41.0 %collective-permute-start.5 = (bf16[8,1,144,1024]{3,2,1,0:T(8,128)(2,1)S(1)}, bf16[8,1,144,1024]{3,2,1,0:T(8,128)(2,1)}, u32[]{:S(2)}, u32[]{:S(2)}) collective-permute-start(bf16[8,1,144,1024]{3,2,1,0:T(8,128)(2,1)S(1)} %pad_maximum_fusion.refs_0_), channel_id=1, source_target_pairs={{0,16},{4,12},{8,24},{12,4},{16,0},{20,28},{24,8},{28,20},{1,17},{... | collective-permute-start | bytes 7077896 | tf_op jit(solution)/shard_map/ppermute | solution.py:598
  53.6 132.0 %all-gather.13.cloned.1.call-start = ((), (), s32[]{:S(2)}) async-start(), calls=%async_computation.14 | async-start | bytes 1310720 | tf_op jit(solution)/shard_map/all_gather | solution.py:632
  93.0 40.6 %collective-permute-start.7 = (bf16[8,1,144,1024]{3,2,1,0:T(8,128)(2,1)S(1)}, bf16[8,1,144,1024]{3,2,1,0:T(8,128)(2,1)}, u32[]{:S(2)}, u32[]{:S(2)}) collective-permute-start(bf16[8,1,144,1024]{3,2,1,0:T(8,128)(2,1)S(1)} %pad_maximum_fusion.refs_0_), channel_id=1, source_target_pairs={{0,4},{4,0},{1,5},{5,1},{2,6},{6,2},{3,7},{7,3},{8,12},{12,8},{9,1... | collective-permute-start | bytes 7077896 | tf_op jit(solution)/shard_map/ppermute | solution.py:599
  95.1 38.5 %collective-permute-start.8 = (bf16[8,1,144,1024]{3,2,1,0:T(8,128)(2,1)}, bf16[8,1,144,1024]{3,2,1,0:T(8,128)(2,1)}, u32[]{:S(2)}, u32[]{:S(2)}) collective-permute-start(bf16[8,1,144,1024]{3,2,1,0:T(8,128)(2,1)} %collective-permute-done.5.refs_1_), channel_id=1, source_target_pairs={{0,4},{4,0},{1,5},{5,1},{2,6},{6,2},{3,7},{7,3},{8,12},{12,8},{9,1... | collective-permute-start | bytes 7077896 | tf_op jit(solution)/shard_map/ppermute | solution.py:599
  95.2 38.4 %collective-permute-start.9 = (bf16[8,1024,128]{2,1,0:T(8,128)(2,1)}, bf16[8,1024,128]{2,1,0:T(8,128)(2,1)}, u32[]{:S(2)}, u32[]{:S(2)}) collective-permute-start(bf16[8,1024,128]{2,1,0:T(8,128)(2,1)} %pad_maximum_fusion.1.refs_0_), channel_id=1, source_target_pairs={{0,16},{4,12},{8,24},{12,4},{16,0},{20,28},{24,8},{28,20},{1,17},{... | collective-permute-start | bytes 6291464 | tf_op jit(solution)/shard_map/ppermute | solution.py:598
  154.3 62.6 %all-gather.15.cloned.1.call-start = ((), (), s32[]{:S(2)}) async-start(), calls=%async_computation.15 | async-start | bytes 1310720 | tf_op jit(solution)/shard_map/all_gather | solution.py:632
  186.3 352.2 %reduce-scatter.7.cloned.1.call-start = ((), (), s32[]{:S(2)}) async-start(), calls=%async_computation.6 | async-start | bytes 1310720 | tf_op jit(solution)/shard_map/reduce_scatter | solution.py:850
  217.8 38.3 %collective-permute-start.25 = (bf16[8,1,128,1024]{3,2,1,0:T(8,128)(2,1)}, bf16[8,1,128,1024]{3,2,1,0:T(8,128)(2,1)}, u32[]{:S(2)}, u32[]{:S(2)}) collective-permute-start(bf16[8,1,128,1024]{3,2,1,0:T(8,128)(2,1)} %pad_maximum_fusion.3.refs_0_), channel_id=1, source_target_pairs={{0,16},{4,12},{8,24},{12,4},{16,0},{20,28},{24,8},{28,20},{1,17},{... | collective-permute-start | bytes 6291464 | tf_op jit(solution)/shard_map/ppermute | solution.py:598
  219.6 36.5 %collective-permute-start.23 = (bf16[8,3,128,256]{3,2,1,0:T(8,128)(2,1)S(1)}, bf16[8,3,128,256]{3,2,1,0:T(8,128)(2,1)}, u32[]{:S(2)}, u32[]{:S(2)}) collective-permute-start(bf16[8,3,128,256]{3,2,1,0:T(8,128)(2,1)S(1)} %pad_maximum_fusion.5.refs_0_), channel_id=1, source_target_pairs={{0,4},{4,0},{1,5},{5,1},{2,6},{6,2},{3,7},{7,3},{8,12},{12,8},{9,1... | collective-permute-start | bytes 4718600 | tf_op jit(solution)/shard_map/ppermute | solution.py:599
  258.1 41.3 %collective-permute-start.27 = (bf16[8,1,128,1024]{3,2,1,0:T(8,128)(2,1)}, bf16[8,1,128,1024]{3,2,1,0:T(8,128)(2,1)}, u32[]{:S(2)}, u32[]{:S(2)}) collective-permute-start(bf16[8,1,128,1024]{3,2,1,0:T(8,128)(2,1)} %pad_maximum_fusion.3.refs_0_), channel_id=1, source_target_pairs={{0,4},{4,0},{1,5},{5,1},{2,6},{6,2},{3,7},{7,3},{8,12},{12,8},{9,1... | collective-permute-start | bytes 6291464 | tf_op jit(solution)/shard_map/ppermute | solution.py:599
  258.1 41.3 %collective-permute-start.28 = (bf16[8,1,128,1024]{3,2,1,0:T(8,128)(2,1)}, bf16[8,1,128,1024]{3,2,1,0:T(8,128)(2,1)}, u32[]{:S(2)}, u32[]{:S(2)}) collective-permute-start(bf16[8,1,128,1024]{3,2,1,0:T(8,128)(2,1)} %collective-permute-done.25.refs_1_), channel_id=1, source_target_pairs={{0,4},{4,0},{1,5},{5,1},{2,6},{6,2},{3,7},{7,3},{8,12},{12,8},{9,1... | collective-permute-start | bytes 6291464 | tf_op jit(solution)/shard_map/ppermute | solution.py:599
  258.6 40.8 %collective-permute-start.29 = (bf16[8,1024,128]{2,1,0:T(8,128)(2,1)}, bf16[8,1024,128]{2,1,0:T(8,128)(2,1)}, u32[]{:S(2)}, u32[]{:S(2)}) collective-permute-start(bf16[8,1024,128]{2,1,0:T(8,128)(2,1)} %pad_maximum_fusion.4.refs_0_), channel_id=1, source_target_pairs={{0,16},{4,12},{8,24},{12,4},{16,0},{20,28},{24,8},{28,20},{1,17},{... | collective-permute-start | bytes 6291464 | tf_op jit(solution)/shard_map/ppermute | solution.py:598
  406.7 37.3 %collective-permute-start.42 = (bf16[256,4096]{1,0:T(8,128)(2,1)S(1)}, bf16[256,4096]{1,0:T(8,128)(2,1)S(1)}, u32[]{:S(2)}, u32[]{:S(2)}) collective-permute-start(bf16[256,4096]{1,0:T(8,128)(2,1)S(1)} %fusion.10), channel_id=1, source_target_pairs={{0,16},{4,12},{8,24},{12,4},{16,0},{20,28},{24,8},{28,20},{1,17},{... | collective-permute-start | bytes 6291464 | tf_op jit(solution)/shard_map/ppermute | solution.py:598
  415.8 48.3 %collective-permute-start.45 = (bf16[512,1024]{1,0:T(8,128)(2,1)}, bf16[512,1024]{1,0:T(8,128)(2,1)}, u32[]{:S(2)}, u32[]{:S(2)}) collective-permute-start(bf16[512,1024]{1,0:T(8,128)(2,1)} %convolution_convert_fusion.8), channel_id=1, source_target_pairs={{0,4},{4,0},{1,5},{5,1},{2,6},{6,2},{3,7},{7,3},{8,12},{12,8},{9,1... | collective-permute-start | bytes 3145736 | tf_op jit(solution)/shard_map/ppermute | solution.py:599
  453.0 100.7 %reduce-scatter.9.cloned.1.call-start = ((), (), s32[]{:S(2)}) async-start(), calls=%async_computation.7 | async-start | bytes 1310720 | tf_op jit(solution)/shard_map/reduce_scatter | solution.py:850
  466.6 71.9 %collective-permute-start.47 = (bf16[256,1024]{1,0:T(8,128)(2,1)}, bf16[256,1024]{1,0:T(8,128)(2,1)}, u32[]{:S(2)}, u32[]{:S(2)}) collective-permute-start(bf16[256,1024]{1,0:T(8,128)(2,1)} %fusion.108), channel_id=1, source_target_pairs={{0,16},{4,12},{8,24},{12,4},{16,0},{20,28},{24,8},{28,20},{1,17},{... | collective-permute-start | bytes 1572872 | tf_op jit(solution)/shard_map/ppermute | solution.py:598
  471.3 67.1 %collective-permute-start.46 = (bf16[256,2048]{1,0:T(8,128)(2,1)}, bf16[256,2048]{1,0:T(8,128)(2,1)}, u32[]{:S(2)}, u32[]{:S(2)}) collective-permute-start(bf16[256,2048]{1,0:T(8,128)(2,1)} %fusion.33), channel_id=1, source_target_pairs={{0,16},{4,12},{8,24},{12,4},{16,0},{20,28},{24,8},{28,20},{1,17},{... | collective-permute-start | bytes 3145736 | tf_op jit(solution)/shard_map/ppermute | solution.py:598
  474.7 184.7 %reduce-scatter.11.cloned.1.call-start = ((), (), s32[]{:S(2)}) async-start(), calls=%async_computation.8 | async-start | bytes 983040 | tf_op jit(solution)/shard_map/reduce_scatter | solution.py:850
  633.5 53.2 %reduce-scatter.13.cloned.1.call-start = ((), (), s32[]{:S(2)}) async-start(), calls=%async_computation.9 | async-start | bytes 1310720 | tf_op jit(solution)/shard_map/reduce_scatter | solution.py:850
  661.6 96.1 %reduce-scatter.17.cloned.1.call-start = ((), (), s32[]{:S(2)}) async-start(), calls=%async_computation.11 | async-start | bytes 1310720 | tf_op jit(solution)/shard_map/reduce_scatter | solution.py:850
  686.7 37.6 %collective-permute-start.66 = (bf16[256,4096]{1,0:T(8,128)(2,1)}, bf16[256,4096]{1,0:T(8,128)(2,1)}, u32[]{:S(2)}, u32[]{:S(2)}) collective-permute-start(bf16[256,4096]{1,0:T(8,128)(2,1)} %fusion.14), channel_id=1, source_target_pairs={{0,16},{4,12},{8,24},{12,4},{16,0},{20,28},{24,8},{28,20},{1,17},{... | collective-permute-start | bytes 6291464 | tf_op jit(solution)/shard_map/ppermute | solution.py:598
  732.7 55.0 %reduce-scatter.15.cloned.1.call-start = ((), (), s32[]{:S(2)}) async-start(), calls=%async_computation.10 | async-start | bytes 1474560 | tf_op jit(solution)/shard_map/reduce_scatter | solution.py:865
  (214 other events, 2731.6 us)
Sparse Core Ops, SparseCore 0:
  35.9 32.4 all-gather.8
  70.5 43.0 all-gather.10
  154.5 28.2 all-gather.12
  186.4 30.5 all-gather.14
  453.1 28.3 reduce-scatter.6
  483.8 25.7 reduce-scatter.8
  633.6 20.8 reduce-scatter.10
  661.7 24.5 reduce-scatter.12
  732.8 24.7 reduce-scatter.16
  759.8 27.8 reduce-scatter.14
